TPU v7x, 32 devices: a whole 2x2x4 slice. The times are simulated.
32 devices in a mesh: seq: 8 (over z, y), fsdp: 4 (over x, core).
Axes of the slice: x: 2, y: 2, z: 4, core: 2. Of those that a mesh axis runs over, the one named last changes fastest.
Arguments:
- tokens: bfloat16 [4, 3072, 1024], P('fsdp', 'seq'), may hold values from -6 to 6
- cotangent: bfloat16 [4, 3072, 1024], P('fsdp', 'seq'), may hold values from -6 to 6
- lengths: int32 [4, 4], replicated, may hold values from 1 to 1152, as said below
- deal: int32 [4], replicated, may hold values from 0 to 3, each once
- ln1_gain: bfloat16 [1024], P('fsdp'), may hold values from 0.5 to 1.5
- ln1_shift: bfloat16 [1024], P('fsdp'), may hold values from -1.75 to 1.75
- w_qkv: bfloat16 [1024, 3072], P('fsdp'), may hold values from -0.1875 to 0.1875
- bias_qv: bfloat16 [2048], P('fsdp'), may hold values from -1.75 to 1.75
- w_out: bfloat16 [1024, 1024], P('fsdp'), may hold values from -3 to 3
- bias_out: bfloat16 [1024], P('fsdp'), may hold values from -1.75 to 1.75
- ln2_gain: bfloat16 [1024], P('fsdp'), may hold values from 0.5 to 1.5
- ln2_shift: bfloat16 [1024], P('fsdp'), may hold values from -1.75 to 1.75
- w_fc: bfloat16 [1024, 4096], P('fsdp'), may hold values from -0.1875 to 0.1875
- bias_fc: bfloat16 [4096], P('fsdp'), may hold values from -1.75 to 1.75
- w_proj: bfloat16 [4096, 1024], P('fsdp'), may hold values from -0.09375 to 0.09375
- bias_proj: bfloat16 [1024], P('fsdp'), may hold values from -1.75 to 1.75
Outputs:
- output: bfloat16 [4, 3072, 1024], P('fsdp', 'seq')
- input_grad: float32 [4, 3072, 1024], P('fsdp', 'seq')
- grad_ln1_gain: float32 [1024], P('fsdp')
- grad_ln1_shift: float32 [1024], P('fsdp')
- grad_w_qkv: float32 [1024, 3072], P('fsdp')
- grad_bias_qv: float32 [2048], P('fsdp')
- grad_w_out: float32 [1024, 1024], P('fsdp')
- grad_bias_out: float32 [1024], P('fsdp')
- grad_ln2_gain: float32 [1024], P('fsdp')
- grad_ln2_shift: float32 [1024], P('fsdp')
- grad_w_fc: float32 [1024, 4096], P('fsdp')
- grad_bias_fc: float32 [4096], P('fsdp')
- grad_w_proj: float32 [4096, 1024], P('fsdp')
- grad_bias_proj: float32 [1024], P('fsdp')
- stats: float32 [3], replicated
Inputs may be any that keep to these rules, and one draw needn't show every extreme that they name: Each row lists 4 - 1 sequence lengths and then the padding count, which is 1 or more; every sequence has 384 tokens or more, one in each row exactly 1152; a row sums to 3072. `deal`: every group is named by exactly one home pack.
All inputs are finite; a program needn't handle non-finite values.
Results may differ from a plain program's by a relative error of at most 0.017.
Values may be sent and summed in bfloat16 or wider, within the bound.
No kernel may reach another device: no remote copies, remote signals or barrier semaphores. Data moves between devices by JAX's collectives and lax.ppermute only.
A program may use at most 192 MiB of HBM per device.

v0:
```python
from functools import partial

import jax
import jax.numpy as jnp
from jax import lax
from jax.sharding import PartitionSpec as P

H = 16
HEAD = 64


def layer_norm(value, gain, shift):
    mean = jnp.mean(value, axis=-1, keepdims=True)
    centred = value - mean
    spread = jnp.mean(centred * centred, axis=-1, keepdims=True)
    return centred * lax.rsqrt(spread + 1e-05) * gain + shift


def segment_ids(row, count):
    ends = jnp.cumsum(row)
    places = jnp.arange(count, dtype=jnp.int32)
    return jnp.sum((places[:, None] >= ends[None, :]).astype(jnp.int32), axis=1)


def contract_rows(left, right):
    return lax.dot_general(
        left, right, (((0,), (0,)), ((), ())), preferred_element_type=jnp.float32
    )


def times_rows(left, right):
    return lax.dot_general(
        left, right, (((1,), (1,)), ((), ())), preferred_element_type=jnp.float32
    )


def allowed_block(segments, first, block):
    count = segments.shape[0]
    seg_rows = lax.dynamic_slice_in_dim(segments, first, block, 0)
    query_pos = first + jnp.arange(block, dtype=jnp.int32)
    key_pos = jnp.arange(count, dtype=jnp.int32)
    return (seg_rows[:, None] == segments[None, :]) & (key_pos[None, :] <= query_pos[:, None])


def score_block(query_rows, keys, allowed, scale):
    raw = jnp.einsum("qhe,khe->hqk", query_rows, keys, preferred_element_type=jnp.float32) * scale
    return jnp.where(allowed[None], raw, -1e30)


def select_rows(mask, piece):
    return jnp.sum(
        jnp.where(mask[:, None, None], piece, jnp.zeros((), piece.dtype)), axis=0
    ).astype(piece.dtype)


def shards(
    tokens,
    cotangent,
    lengths,
    deal,
    ln1_gain,
    ln1_shift,
    w_qkv,
    bias_qv,
    w_out,
    bias_out,
    ln2_gain,
    ln2_shift,
    w_fc,
    bias_fc,
    w_proj,
    bias_proj,
):
    rows = tokens.shape[1]
    width = tokens.shape[2]
    group_me = lax.axis_index("fsdp")
    pieces = (
        lax.all_gather(tokens, "fsdp", axis=0, tiled=True),
        lax.all_gather(cotangent, "fsdp", axis=0, tiled=True),
    )
    count = pieces[0].shape[0]
    mask = deal == group_me
    here_x = select_rows(mask, pieces[0])
    here_dy = select_rows(mask, pieces[1])
    row = lengths[group_me]
    gathered = (
        lax.all_gather(ln1_gain, "fsdp", axis=0, tiled=True),
        lax.all_gather(ln1_shift, "fsdp", axis=0, tiled=True),
        lax.all_gather(w_qkv, "fsdp", axis=0, tiled=True),
        lax.all_gather(bias_qv, "fsdp", axis=0, tiled=True),
        lax.all_gather(w_out, "fsdp", axis=0, tiled=True),
        lax.all_gather(bias_out, "fsdp", axis=0, tiled=True),
        lax.all_gather(ln2_gain, "fsdp", axis=0, tiled=True),
        lax.all_gather(ln2_shift, "fsdp", axis=0, tiled=True),
        lax.all_gather(w_fc, "fsdp", axis=0, tiled=True),
        lax.all_gather(bias_fc, "fsdp", axis=0, tiled=True),
        lax.all_gather(w_proj, "fsdp", axis=0, tiled=True),
        lax.all_gather(bias_proj, "fsdp", axis=0, tiled=True),
    )
    gain_one, shift_one, wqkv, bqv, wout, bout, gain_two, shift_two, wfc, bfc, wproj, bproj = (
        gathered
    )
    seq_count = lax.axis_size("seq")
    group_rows = rows * seq_count
    local_heads = H // seq_count
    block = min(512, group_rows)
    blocks = group_rows // block
    scale = HEAD ** (-0.5)
    segments = segment_ids(row, group_rows)
    last = lengths.shape[1] - 1
    own = lax.dynamic_slice_in_dim(segments, lax.axis_index("seq") * rows, rows, 0)
    valid = (own < last)[:, None]
    xf = here_x.astype(jnp.float32)
    normed_one, norm_one_back = jax.vjp(
        layer_norm, xf, gain_one.astype(jnp.float32), shift_one.astype(jnp.float32)
    )
    low_one = normed_one.astype(jnp.bfloat16)
    mixed = jnp.dot(low_one, wqkv, preferred_element_type=jnp.float32).reshape(rows, H, 3, HEAD)
    biases = bqv.astype(jnp.float32).reshape(H, 2, HEAD)
    roles = jnp.stack([biases[:, 0], jnp.zeros((H, HEAD), jnp.float32), biases[:, 1]], axis=1)
    packed = (mixed + roles).astype(jnp.bfloat16).reshape(rows, H * 3 * HEAD)
    grouped = lax.all_to_all(packed, "seq", split_axis=1, concat_axis=0, tiled=True).reshape(
        group_rows, local_heads, 3, HEAD
    )
    queries = grouped[:, :, 0]
    keys = grouped[:, :, 1]
    values = grouped[:, :, 2]

    def forward_block(index):
        first = index * block
        allowed = allowed_block(segments, first, block)
        query_rows = lax.dynamic_slice_in_dim(queries, first, block, 0)
        scores = score_block(query_rows, keys, allowed, scale)
        top = jnp.max(scores, axis=-1, keepdims=True)
        expd = jnp.exp(scores - top)
        total = jnp.sum(expd, axis=-1, keepdims=True)
        probs = (expd / total).astype(jnp.bfloat16)
        result_rows = jnp.einsum(
            "hqk,khe->qhe", probs, values, preferred_element_type=jnp.float32
        ).astype(jnp.bfloat16)
        return (result_rows, (top + jnp.log(total))[..., 0])

    attended_blocks, lse_blocks = lax.map(forward_block, jnp.arange(blocks, dtype=jnp.int32))
    attended = attended_blocks.reshape(group_rows, local_heads * HEAD)
    merged = lax.all_to_all(attended, "seq", split_axis=0, concat_axis=1, tiled=True)
    attn_branch = jnp.dot(merged, wout, preferred_element_type=jnp.float32) + bout.astype(
        jnp.float32
    )
    middle = xf + attn_branch
    normed_two, norm_two_back = jax.vjp(
        layer_norm, middle, gain_two.astype(jnp.float32), shift_two.astype(jnp.float32)
    )
    low_two = normed_two.astype(jnp.bfloat16)
    inner = jnp.dot(low_two, wfc, preferred_element_type=jnp.float32) + bfc.astype(jnp.float32)
    activated, gelu_back = jax.vjp(partial(jax.nn.gelu, approximate=True), inner)
    hidden = activated.astype(jnp.bfloat16)
    mlp_branch = jnp.dot(hidden, wproj, preferred_element_type=jnp.float32) + bproj.astype(
        jnp.float32
    )
    result = middle + mlp_branch
    output = jnp.where(valid, result, 0.0).astype(jnp.bfloat16)
    squares = jnp.stack(
        [jnp.sum(jnp.where(valid, part * part, 0.0)) for part in (result, attn_branch, mlp_branch)]
    )
    counted = jnp.sum(valid.astype(jnp.float32))
    totals, count_all = lax.psum((squares, counted), ("seq", "fsdp"))
    stats = jnp.sqrt(totals / (count_all * width))
    d_result = jnp.where(valid, here_dy.astype(jnp.float32), 0.0)
    d_mlp = d_result.astype(jnp.bfloat16)
    grad_wproj = contract_rows(hidden, d_mlp)
    grad_bproj = jnp.sum(d_mlp.astype(jnp.float32), axis=0)
    d_hidden = times_rows(d_mlp, wproj)
    d_inner = gelu_back(d_hidden)[0].astype(jnp.bfloat16)
    grad_wfc = contract_rows(low_two, d_inner)
    grad_bfc = jnp.sum(d_inner.astype(jnp.float32), axis=0)
    d_two = times_rows(d_inner, wfc)
    d_mid_norm, grad_gain_two, grad_shift_two = norm_two_back(d_two)
    d_middle = d_result + d_mid_norm
    d_attn = d_middle.astype(jnp.bfloat16)
    grad_wout = contract_rows(merged, d_attn)
    grad_bout = jnp.sum(d_attn.astype(jnp.float32), axis=0)
    d_merged = times_rows(d_attn, wout).astype(jnp.bfloat16)
    d_heads = lax.all_to_all(d_merged, "seq", split_axis=1, concat_axis=0, tiled=True).reshape(
        group_rows, local_heads, HEAD
    )

    def back_block(carry, index):
        d_keys, d_values = carry
        first = index * block
        allowed = allowed_block(segments, first, block)
        query_rows = lax.dynamic_slice_in_dim(queries, first, block, 0)
        grad_rows = lax.dynamic_slice_in_dim(d_heads, first, block, 0)
        scores = score_block(query_rows, keys, allowed, scale)
        probs = jnp.exp(scores - lse_blocks[index][..., None])
        d_values = d_values + jnp.einsum(
            "hqk,qhe->khe",
            probs.astype(jnp.bfloat16),
            grad_rows,
            preferred_element_type=jnp.float32,
        )
        d_probs = jnp.einsum("qhe,khe->hqk", grad_rows, values, preferred_element_type=jnp.float32)
        delta = jnp.sum(probs * d_probs, axis=-1, keepdims=True)
        d_scores = (probs * (d_probs - delta)).astype(jnp.bfloat16)
        d_query_rows = (
            jnp.einsum("hqk,khe->qhe", d_scores, keys, preferred_element_type=jnp.float32) * scale
        )
        d_keys = (
            d_keys
            + jnp.einsum("hqk,qhe->khe", d_scores, query_rows, preferred_element_type=jnp.float32)
            * scale
        )
        return ((d_keys, d_values), d_query_rows.astype(jnp.bfloat16))

    zero_rows = jnp.zeros((group_rows, local_heads, HEAD), jnp.float32)
    (d_keys, d_values), d_query_blocks = lax.scan(
        back_block, (zero_rows, zero_rows), jnp.arange(blocks, dtype=jnp.int32)
    )
    d_queries = d_query_blocks.reshape(group_rows, local_heads, HEAD)
    d_grouped = jnp.stack(
        [d_queries, d_keys.astype(jnp.bfloat16), d_values.astype(jnp.bfloat16)], axis=2
    ).reshape(group_rows, local_heads * 3 * HEAD)
    d_packed = lax.all_to_all(d_grouped, "seq", split_axis=0, concat_axis=1, tiled=True)
    d_roles = d_packed.astype(jnp.float32).reshape(rows, H, 3, HEAD)
    grad_bqv = jnp.stack(
        [jnp.sum(d_roles[:, :, 0], axis=0), jnp.sum(d_roles[:, :, 2], axis=0)], axis=1
    ).reshape(2 * H * HEAD)
    grad_wqkv = contract_rows(low_one, d_packed)
    d_one = times_rows(d_packed, wqkv)
    d_in_norm, grad_gain_one, grad_shift_one = norm_one_back(d_one)
    input_grad = d_middle + d_in_norm
    shares = (
        lax.psum_scatter(
            grad_gain_one.astype(jnp.bfloat16), "fsdp", scatter_dimension=0, tiled=True
        ).astype(jnp.float32),
        lax.psum_scatter(
            grad_shift_one.astype(jnp.bfloat16), "fsdp", scatter_dimension=0, tiled=True
        ).astype(jnp.float32),
        lax.psum_scatter(
            grad_wqkv.astype(jnp.bfloat16), "fsdp", scatter_dimension=0, tiled=True
        ).astype(jnp.float32),
        lax.psum_scatter(
            grad_bqv.astype(jnp.bfloat16), "fsdp", scatter_dimension=0, tiled=True
        ).astype(jnp.float32),
        lax.psum_scatter(
            grad_wout.astype(jnp.bfloat16), "fsdp", scatter_dimension=0, tiled=True
        ).astype(jnp.float32),
        lax.psum_scatter(
            grad_bout.astype(jnp.bfloat16), "fsdp", scatter_dimension=0, tiled=True
        ).astype(jnp.float32),
        lax.psum_scatter(
            grad_gain_two.astype(jnp.bfloat16), "fsdp", scatter_dimension=0, tiled=True
        ).astype(jnp.float32),
        lax.psum_scatter(
            grad_shift_two.astype(jnp.bfloat16), "fsdp", scatter_dimension=0, tiled=True
        ).astype(jnp.float32),
        lax.psum_scatter(
            grad_wfc.astype(jnp.bfloat16), "fsdp", scatter_dimension=0, tiled=True
        ).astype(jnp.float32),
        lax.psum_scatter(
            grad_bfc.astype(jnp.bfloat16), "fsdp", scatter_dimension=0, tiled=True
        ).astype(jnp.float32),
        lax.psum_scatter(
            grad_wproj.astype(jnp.bfloat16), "fsdp", scatter_dimension=0, tiled=True
        ).astype(jnp.float32),
        lax.psum_scatter(
            grad_bproj.astype(jnp.bfloat16), "fsdp", scatter_dimension=0, tiled=True
        ).astype(jnp.float32),
    )
    (
        share_g1,
        share_s1,
        share_qkv,
        share_bqv,
        share_out,
        share_bout,
        share_g2,
        share_s2,
        share_fc,
        share_bfc,
        share_proj,
        share_bproj,
    ) = shares
    summed = (
        lax.psum(share_g1.astype(jnp.bfloat16), "seq").astype(jnp.float32),
        lax.psum(share_s1.astype(jnp.bfloat16), "seq").astype(jnp.float32),
        lax.psum(share_qkv.astype(jnp.bfloat16), "seq").astype(jnp.float32),
        lax.psum(share_bqv.astype(jnp.bfloat16), "seq").astype(jnp.float32),
        lax.psum(share_out.astype(jnp.bfloat16), "seq").astype(jnp.float32),
        lax.psum(share_bout.astype(jnp.bfloat16), "seq").astype(jnp.float32),
        lax.psum(share_g2.astype(jnp.bfloat16), "seq").astype(jnp.float32),
        lax.psum(share_s2.astype(jnp.bfloat16), "seq").astype(jnp.float32),
        lax.psum(share_fc.astype(jnp.bfloat16), "seq").astype(jnp.float32),
        lax.psum(share_bfc.astype(jnp.bfloat16), "seq").astype(jnp.float32),
        lax.psum(share_proj.astype(jnp.bfloat16), "seq").astype(jnp.float32),
        lax.psum(share_bproj.astype(jnp.bfloat16), "seq").astype(jnp.float32),
    )
    source = deal[group_me]

    def fetch(carry, piece):
        count = piece.shape[0]
        mask = jnp.arange(count, dtype=jnp.int32) == source
        return carry + select_rows(mask, piece)

    output_home = fetch(
        jnp.zeros((rows, width), jnp.bfloat16),
        lax.all_gather(output[None], "fsdp", axis=0, tiled=True),
    )
    grad_home = fetch(
        jnp.zeros((rows, width), jnp.float32),
        lax.all_gather(input_grad[None].astype(jnp.bfloat16), "fsdp", axis=0, tiled=True).astype(
            jnp.float32
        ),
    )
    return (
        output_home[None],
        grad_home[None],
        summed[0],
        summed[1],
        summed[2],
        summed[3],
        summed[4],
        summed[5],
        summed[6],
        summed[7],
        summed[8],
        summed[9],
        summed[10],
        summed[11],
        stats,
    )


def solution(mesh):
    in_specs = (
        P("fsdp", "seq", None),
        P("fsdp", "seq", None),
        P(),
        P(),
        P("fsdp"),
        P("fsdp"),
        P("fsdp", None),
        P("fsdp"),
        P("fsdp", None),
        P("fsdp"),
        P("fsdp"),
        P("fsdp"),
        P("fsdp", None),
        P("fsdp"),
        P("fsdp", None),
        P("fsdp"),
    )
    out_specs = (
        P("fsdp", "seq", None),
        P("fsdp", "seq", None),
        P("fsdp"),
        P("fsdp"),
        P("fsdp", None),
        P("fsdp"),
        P("fsdp", None),
        P("fsdp"),
        P("fsdp"),
        P("fsdp"),
        P("fsdp", None),
        P("fsdp"),
        P("fsdp", None),
        P("fsdp"),
        P(),
    )
    return jax.shard_map(shards, mesh=mesh, in_specs=in_specs, out_specs=out_specs, check_vma=False)
```

profile of v0, /device:TPU:0, one launch (start us, length us, event | category | flops | bytes accessed | tf_op | source)
XLA Modules:
  0.0 1137.1 jit_solution(11222870705564991038)
XLA Ops:
  27.6 13.3 %all-gather.18.cloned.1.call-done = bf16[4,384,1024]{2,1,0:T(8,128)(2,1)} async-done(((bf16[1,384,1024]{2,1,0:T(8,128)(2,1)}), bf16[4,384,1024]{2,1,0:T(8,128)(2,1)}) %all-gather.18.cloned.1.call-update) | async-done | bytes 3145744 | tf_op jit(solution)/shard_map/all_gather | solution.py:78
  40.9 30.1 %all-gather.28.cloned.1.call-done = bf16[4,384,1024]{2,1,0:T(8,128)(2,1)} async-done(((bf16[1,384,1024]{2,1,0:T(8,128)(2,1)}), bf16[4,384,1024]{2,1,0:T(8,128)(2,1)}) %all-gather.28.cloned.1.call-update) | async-done | bytes 3145744 | tf_op jit(solution)/shard_map/all_gather | solution.py:79
  77.4 41.6 %all-gather.20.cloned.1.call-done = bf16[1024,3072]{1,0:T(8,128)(2,1)} async-done(((bf16[256,3072]{1,0:T(8,128)(2,1)}), bf16[1024,3072]{1,0:T(8,128)(2,1)}) %all-gather.20.cloned.1.call-update) | async-done | bytes 6291472 | tf_op jit(solution)/shard_map/all_gather | solution.py:89
  136.6 53.5 %all-to-all-done = bf16[384,8,384]{0,2,1:T(8,128)(2,1)} async-done(((bf16[384,8,384]{0,2,1:T(8,128)(2,1)}), bf16[384,8,384]{0,2,1:T(8,128)(2,1)}, u32[]{:S(2)}, u32[]{:S(2)}) %all-to-all-start) | async-done | bytes 2359328 | tf_op jit(solution)/shard_map/all_to_all | solution.py:122
  202.3 85.4 %while.27 = (s32[]{:T(128)}, bf16[6,512,2,64]{1,3,2,0:T(8,128)(2,1)}, f32[6,2,512]{2,1,0:T(2,128)S(1)}, s32[6]{0:T(128)S(1)}, s32[3072]{0:T(1024)S(1)}, /*index=...) while((s32[]{:T(128)}, ...), condition=%wide.region_8.9_spmd, body=%wide.region_5.8_spmd.sunk | while | flops 847838720 | bytes 45931196 | solution.py:143
  331.0 10.0 convolution_add_fusion
  341.0 15.3 %fusion.80 = (bf16[4096]{0:T(1024)(128)(2,1)}, bf16[384,4096]{1,0:T(8,128)(2,1)}) fusion(f32[384,4096]{1,0:T(8,128)} %convolution_add_fusion, bf16[4096,1024]{1,0:T(8,128)(2,1)} %all-gather.26.cloned.1.call-done, bf16[384,1024]{1,0:T(8,128)(2,1)S(1)} %copy-done.15, pred[384]{0:T(512)(128)(4,1)S(1)} %get-tuple-element.246), kind=kOutput, calls=%fused_computation.145 | convolution fusion | flops 3255431168 | bytes 18620800 | tf_op jit(solution)/shard_map/dot_general | solution.py:32
  361.8 9.2 select_reduce_fusion.5
  378.6 10.4 convolution_convert_fusion.1
  398.9 11.1 convolution_convert_fusion
  410.0 9.5 all-to-all-done.2
  423.4 287.9 %while.28 = (s32[]{:T(128)}, f32[3072,2,64]{0,2,1:T(8,128)}, f32[3072,2,64]{0,2,1:T(8,128)}, bf16[6,512,2,64]{1,3,2,0:T(8,128)(2,1)}, s32[6]{0:T(128)S(1)}, /*in...) while((s32[]{:T(128)}, f32[3072,2,64]{0,2,1:T(8,128)}, ...), condition=%wide.region_17.18_spmd.clone, body=%wide.region_15.17_spmd.clone.sunk | while | flops 2067267072 | bytes 198102096 | solution.py:215
  461.2 9.9 fusion.143
  509.6 10.7 fusion.143
  558.2 10.1 fusion.143
  605.9 10.0 fusion.143
  653.5 10.0 fusion.143
  701.2 10.0 fusion.143
  717.1 58.7 %all_to_all.70 = bf16[8,384,384]{1,2,0:T(8,128)(2,1)S(1)} all-to-all(bf16[8,384,384]{1,2,0:T(8,128)(2,1)S(1)} %copy.77), channel_id=1, replica_groups=mesh['seq'=8,'fsdp'=4] {'seq'}, dimensions={0} | all-to-all | bytes 4718592 | tf_op jit(solution)/shard_map/all_to_all | solution.py:222
  791.8 47.1 %reduce-scatter.5.cloned.1.call-done = bf16[256,3072]{1,0:T(8,128)(2,1)} async-done(((bf16[1024,3072]{1,0:T(8,128)(2,1)}), bf16[256,3072]{1,0:T(8,128)(2,1)}) %reduce-scatter.5.cloned.1.call-update) | async-done | bytes 1572880 | tf_op jit(solution)/shard_map/reduce_scatter | solution.py:238
  845.3 39.8 %all-reduce.8 = (f32[3]{0:T(128)S(1)}, f32[]{:T(128)}) all-reduce(f32[3]{0:T(128)S(1)} %pad_maximum_fusion.3, f32[]{:T(128)} %get-tuple-element.245), channel_id=1, replica_groups=mesh['seq'=8,'fsdp'=4] {'seq','fsdp'}, use_global_device_ids=true, to_apply=%region_57.58 | all-reduce | flops 4 | bytes 32 | tf_op jit(solution)/shard_map/psum | solution.py:166
  891.4 11.9 %all-reduce.11 = (bf16[1024]{0:T(1024)(128)(2,1)S(1)}, bf16[1024]{0:T(1024)(128)(2,1)S(1)}, bf16[2048]{0:T(1024)(128)(2,1)S(1)}, bf16[1024]{0:T(1024)(128)(2,1)S...) all-reduce(bf16[1024]{0:T(1024)(128)(2,1)S(1)} %get-tuple-element.1, ...), channel_id=4, replica_groups=mesh['seq'=8,'fsdp'=4] {'fsdp'}, use_global_device_ids=true, to_apply=%region_22.23.clone | all-reduce | flops 12288 | bytes 49152
  903.8 21.3 %all-reduce.9 = (bf16[256]{0:T(256)(128)(2,1)S(1)}, bf16[256]{0:T(256)(128)(2,1)S(1)}, bf16[512]{0:T(512)(128)(2,1)S(1)}, bf16[256]{0:T(256)(128)(2,1)S(1)}, bf1...) all-reduce(bf16[256]{0:T(256)(128)(2,1)S(1)} %dynamic-slice.1, ...), channel_id=1, replica_groups=mesh['seq'=8,'fsdp'=4] {'seq'}, use_global_device_ids=true, to_apply=%region_23.24 | all-reduce | flops 3072 | bytes 12288 | tf_op jit(solution)/shard_map/psum | solution.py:284
  933.7 186.8 %all-reduce.14.cloned.1.call-done = (bf16[256,3072]{1,0:T(8,128)(2,1)}, bf16[256,1024]{1,0:T(8,128)(2,1)}, bf16[256,4096]{1,0:T(8,128)(2,1)}, bf16[1024,1024]{1,0:T(8,128)(2,1)}) async-done(((bf16[256,3072]{1,0:T(8,128)(2,1)}, bf16[256,1024]{1,0:T(8,128)(2,1)}, bf16[256,4096]{1,0:T(8,128)(2,1)}, bf16[1024,1024]{1,0:T(8,128)(2,1)}), (bf16[256,3072]{1,0:T(8,128)(2,1)}, bf16[256,1024]{1,0:T(8,128)(2,1)}, ...) | async-done | bytes 6291472 | tf_op jit(solution)/shard_map/psum | solution.py:286
  (492 shorter events, 468.3 us)
Async XLA Ops:
  7.2 129.2 %copy-start = (s32[4,4]{1,0:T(4,128)S(1)}, s32[4,4]{1,0:T(4,128)}, u32[]{:S(2)}) copy-start(s32[4,4]{1,0:T(4,128)} %param.22) | copy-start | bytes 196
  7.2 33.7 %all-gather.18.cloned.1.call-start = ((), (), s32[]{:S(2)}) async-start(), calls=%async_computation.8 | async-start | bytes 3932160 | tf_op jit(solution)/shard_map/all_gather | solution.py:78
  8.0 63.1 %all-gather.28.cloned.1.call-start = ((), (), s32[]{:S(2)}) async-start(), calls=%async_computation.13 | async-start | bytes 3932160 | tf_op jit(solution)/shard_map/all_gather | solution.py:79
  8.7 110.3 %all-gather.20.cloned.1.call-start = ((), (), s32[]{:S(2)}) async-start(), calls=%async_computation.9 | async-start | bytes 7864320 | tf_op jit(solution)/shard_map/all_gather | solution.py:89
  9.5 316.0 %all-gather.22.cloned.1.call-start = ((), (), s32[]{:S(2)}) async-start(), calls=%async_computation.10 | async-start | bytes 2621440 | tf_op jit(solution)/shard_map/all_gather | solution.py:91
  10.0 320.9 %all-gather.24.cloned.1.call-start = ((), (), s32[]{:S(2)}) async-start(), calls=%async_computation.11 | async-start | bytes 10485760 | tf_op jit(solution)/shard_map/all_gather | solution.py:95
  16.6 102.4 %copy-start.24 = (f32[4,1,256]{2,1,0:T(1,128)}, f32[4,1,256]{2,1,0:T(1,128)S(1)}, u32[]{:S(2)}) copy-start(f32[4,1,256]{2,1,0:T(1,128)S(1)} %convert_element_type.256) | copy-start | bytes 12292
  27.6 91.4 %copy-start.39 = (f32[4,1,256]{2,1,0:T(1,128)}, f32[4,1,256]{2,1,0:T(1,128)S(1)}, u32[]{:S(2)}) copy-start(f32[4,1,256]{2,1,0:T(1,128)S(1)} %convert_element_type.257) | copy-start | bytes 12292
  76.8 248.7 %copy-start.7 = (bf16[384,1024]{1,0:T(8,128)(2,1)}, bf16[384,1024]{1,0:T(8,128)(2,1)S(1)}, u32[]{:S(2)}) copy-start(bf16[384,1024]{1,0:T(8,128)(2,1)S(1)} %get-tuple-element.184) | copy-start | bytes 2359300
  130.2 59.9 %all-to-all-start = ((bf16[384,8,384]{0,2,1:T(8,128)(2,1)}), bf16[384,8,384]{0,2,1:T(8,128)(2,1)}, u32[]{:S(2)}, u32[]{:S(2)}) async-start(bf16[384,8,384]{0,2,1:T(8,128)(2,1)} %bitcast.151), calls=%async_computation | async-start | bytes 4718592 | tf_op jit(solution)/shard_map/all_to_all | solution.py:122
  135.7 205.3 %all-gather.26.cloned.1.call-start = ((), (), s32[]{:S(2)}) async-start(), calls=%async_computation.12 | async-start | bytes 10485760 | tf_op jit(solution)/shard_map/all_gather | solution.py:97
  294.8 30.7 %all-to-all-start.1 = ((bf16[8,384,128]{1,2,0:T(8,128)(2,1)}), bf16[8,384,128]{1,2,0:T(8,128)(2,1)}, u32[]{:S(2)}, u32[]{:S(2)}) async-start(bf16[8,384,128]{1,2,0:T(8,128)(2,1)} %copy.72), calls=%async_computation.1 | async-start | bytes 1572864 | tf_op jit(solution)/shard_map/all_to_all | solution.py:145
  299.0 492.7 %reduce-scatter.7.cloned.1.call-start = ((), (), s32[]{:S(2)}) async-start(), calls=%async_computation.15 | async-start | bytes 2621440 | tf_op jit(solution)/shard_map/reduce_scatter | solution.py:244
  325.5 73.4 %copy-start.37 = (pred[384]{0:T(512)(128)(4,1)}, pred[384]{0:T(512)(128)(4,1)S(1)}, u32[]{:S(2)}) copy-start(pred[384]{0:T(512)(128)(4,1)S(1)} %get-tuple-element.246) | copy-start | bytes 1156
  378.4 413.3 %reduce-scatter.9.cloned.1.call-start = ((), (), s32[]{:S(2)}) async-start(), calls=%async_computation.16 | async-start | bytes 10485760 | tf_op jit(solution)/shard_map/reduce_scatter | solution.py:256
  393.0 26.6 %all-to-all-start.2 = ((bf16[384,8,128]{2,0,1:T(8,128)(2,1)}), bf16[384,8,128]{2,0,1:T(8,128)(2,1)}, u32[]{:S(2)}, u32[]{:S(2)}) async-start(bf16[384,8,128]{2,0,1:T(8,128)(2,1)} %bitcast.155), calls=%async_computation.2 | async-start | bytes 1572864 | tf_op jit(solution)/shard_map/all_to_all | solution.py:183
  398.8 393.0 %reduce-scatter.11.cloned.1.call-start = ((), (), s32[]{:S(2)}) async-start(), calls=%async_computation.17 | async-start | bytes 10485760 | tf_op jit(solution)/shard_map/reduce_scatter | solution.py:262
  410.0 428.8 %reduce-scatter.5.cloned.1.call-start = ((), (), s32[]{:S(2)}) async-start(), calls=%async_computation.14 | async-start | bytes 7864320 | tf_op jit(solution)/shard_map/reduce_scatter | solution.py:238
  717.1 58.7 %copy-start.8 = (bf16[384,1024]{1,0:T(8,128)(2,1)S(1)}, bf16[384,1024]{1,0:T(8,128)(2,1)}, u32[]{:S(2)}) copy-start(bf16[384,1024]{1,0:T(8,128)(2,1)} %copy-done.7) | copy-start | bytes 2359300
  717.1 58.7 %copy-start.25 = (f32[4,1,256]{2,1,0:T(1,128)S(1)}, f32[4,1,256]{2,1,0:T(1,128)}, u32[]{:S(2)}) copy-start(f32[4,1,256]{2,1,0:T(1,128)} %copy-done.24) | copy-start | bytes 12292
  717.1 58.7 %copy-start.27 = (f32[384]{0:T(512)S(1)}, f32[384]{0:T(512)}, u32[]{:S(2)}) copy-start(f32[384]{0:T(512)} %copy-done.26) | copy-start | bytes 4612
  781.8 104.4 %all-gather.30.cloned.1.call-start = ((), (), s32[]{:S(2)}) async-start(), calls=%async_computation.18 | async-start | bytes 3932160 | tf_op jit(solution)/shard_map/all_gather | solution.py:306
  782.6 147.1 %all-gather.32.cloned.1.call-start = ((), (), s32[]{:S(2)}) async-start(), calls=%async_computation.19 | async-start | bytes 3932160 | tf_op jit(solution)/shard_map/all_gather | solution.py:310
  791.7 328.9 %all-reduce.14.cloned.1.call-start = ((), (), s32[]{:S(2)}) async-start(), calls=%async_computation.20 | async-start | bytes 12582912 | tf_op jit(solution)/shard_map/psum | solution.py:286
  (106 other events, 1045.2 us)
Sparse Core Ops, SparseCore 0:
  9.6 31.2 all-gather.17
  42.4 28.5 all-gather.27
  72.6 46.3 all-gather.19
  120.4 22.5 all-gather.21
  144.4 58.2 all-gather.23
  204.2 58.2 all-gather.25
  378.5 31.7 reduce-scatter.6
  413.1 71.7 reduce-scatter.8
  487.4 71.7 reduce-scatter.10
  782.0 56.8 reduce-scatter.4
  841.0 29.2 all-gather.29
  872.3 29.1 all-gather.31
  905.9 214.6 all-reduce.13
where the time goes:
time: 1140 us
  waiting for transfers between devices  386 us (34%)
  matrix products  335 us (29%)
  blocking collectives  174 us (15%)
  other arithmetic  136 us (12%)
  local copies, waits for them, and re-layouts  52 us (5%)
  loops' own time  21 us (2%)
  between operations  17.4 us (2%)
  starting transfers between devices  16.4 us (1%)
    psum x1, waiting for transfers between devices, shards(): lax.psum(share_qkv.astype(jnp.bfloat16), 'seq').astype(jnp.float32)  187 us
    dot_general x6, matrix products, back_block(): jnp.einsum('hqk,qhe->khe', probs.astype(jnp.bfloat16), grad_rows, preferr...  60.9 us
    all_to_all x1, blocking collectives, shards(): lax.all_to_all(d_grouped, 'seq', split_axis=0, concat_axis=1, tiled=True)  58.7 us
    dot_general x12, matrix products, score_block(): jnp.einsum('qhe,khe->hqk', query_rows, keys, preferred_element_type=jnp.f...  55.4 us
    all_to_all x1, waiting for transfers between devices, shards(): lax.all_to_all(packed, 'seq', split_axis=1, concat_axis=0, tiled=True)  53.5 us
    dot_general x6, matrix products, back_block(): jnp.einsum('qhe,khe->hqk', grad_rows, values, preferred_element_type=jnp....  50.7 us
    reduce_scatter x1, waiting for transfers between devices, shards(): lax.psum_scatter(grad_wqkv.astype(jnp.bfloat16), 'fsdp', scatter_dimensio...  47.1 us
    convert_element_type x6, other arithmetic, back_block(): d_scores = (probs * (d_probs - delta)).astype(jnp.bfloat16)  44.3 us
  transfers between devices with their start and end apart: 16, of which 7 were waited for; matrix products, arithmetic and copies ran while one was open for 41% of the time, Pallas kernels for 0%

commit v1 on v0

v1 whole, which is shorter than its diff:
```python
import functools

import jax
import jax.numpy as jnp
from jax import lax
from jax.experimental import pallas as pl
from jax.experimental.pallas import tpu as pltpu
from jax.sharding import PartitionSpec as P

H = 16
HEAD = 64
NT = (((1,), (1,)), ((), ()))
TN = (((0,), (0,)), ((), ()))
F32 = jnp.float32
BF16 = jnp.bfloat16


def seg_starts(len_ref, segs, place):
    start = jnp.zeros_like(place)
    end = jnp.int32(0)
    for k in range(segs - 1):
        end = end + len_ref[k]
        start = jnp.where(place >= end, end, start)
    return start


def head_part(block, h, heads):
    if heads == 1:
        return block
    lane = lax.broadcasted_iota(jnp.int32, block.shape, 1)
    return jnp.where((lane >= h * HEAD) & (lane < (h + 1) * HEAD), block, jnp.zeros_like(block))


def forward_kernel(heads, block, segs, len_ref, qkv_ref, o_ref, lse_ref, vt_ref):
    hd = heads * HEAD
    steps = qkv_ref.shape[0] // block

    def flip(i, _):
        at = pl.multiple_of(i * block, block)
        vt_ref[:, pl.ds(at, block)] = qkv_ref[pl.ds(at, block), 2 * hd : 3 * hd].T
        return 0

    lax.fori_loop(0, steps, flip, 0)
    key_rows = lax.broadcasted_iota(jnp.int32, (block, block), 0)

    def query_step(i, _):
        r0 = pl.multiple_of(i * block, block)
        q = qkv_ref[pl.ds(r0, block), 0:hd] * jnp.asarray(HEAD**-0.5, BF16)
        qs = [head_part(q, h, heads) for h in range(heads)]
        place = r0 + lax.broadcasted_iota(jnp.int32, (1, block), 1)
        start = seg_starts(len_ref, segs, place)
        first = seg_starts(len_ref, segs, r0) // block

        def key_step(j, carry):
            c0 = pl.multiple_of(j * block, block)
            kb = qkv_ref[pl.ds(c0, block), hd : 2 * hd]
            key_pos = key_rows + c0
            ok = (key_pos >= start) & (key_pos <= place)
            out = []
            for h in range(heads):
                top, total, acc = carry[3 * h : 3 * h + 3]
                s = lax.dot_general(kb, qs[h], NT, preferred_element_type=F32)
                s = jnp.where(ok, s, -1e30)
                new = jnp.maximum(top, jnp.max(s, axis=0, keepdims=True))
                p = jnp.exp(s - new)
                shrink = jnp.exp(top - new)
                total = total * shrink + jnp.sum(p, axis=0, keepdims=True)
                vt = vt_ref[h * HEAD : (h + 1) * HEAD, pl.ds(c0, block)]
                acc = acc * shrink + jnp.dot(vt, p.astype(BF16), preferred_element_type=F32)
                out += [new, total, acc]
            return tuple(out)

        init = (
            jnp.full((1, block), -1e30, F32),
            jnp.zeros((1, block), F32),
            jnp.zeros((HEAD, block), F32),
        ) * heads
        res = lax.fori_loop(first, i + 1, key_step, init)
        flat = jnp.concatenate([res[3 * h + 2] / res[3 * h + 1] for h in range(heads)], axis=0)
        o_ref[pl.ds(r0, block), :] = flat.T.astype(BF16)
        for h in range(heads):
            lse_ref[h : h + 1, pl.ds(r0, block)] = res[3 * h] + jnp.log(res[3 * h + 1])
        return 0

    lax.fori_loop(0, steps, query_step, 0)


def backward_kernel(
    heads, block, segs, len_ref, qkv_ref, o_ref, lse_ref, do_ref, d_ref, kt_ref, dk_ref, dv_ref
):
    hd = heads * HEAD
    steps = qkv_ref.shape[0] // block

    def flip(i, _):
        at = pl.multiple_of(i * block, block)
        kt_ref[:, pl.ds(at, block)] = qkv_ref[pl.ds(at, block), hd : 2 * hd].T
        dk_ref[pl.ds(at, block), :] = jnp.zeros((block, hd), F32)
        dv_ref[pl.ds(at, block), :] = jnp.zeros((block, hd), F32)
        return 0

    lax.fori_loop(0, steps, flip, 0)
    key_rows = lax.broadcasted_iota(jnp.int32, (block, block), 0)

    def query_step(i, _):
        r0 = pl.multiple_of(i * block, block)
        q = qkv_ref[pl.ds(r0, block), 0:hd] * jnp.asarray(HEAD**-0.5, BF16)
        do = do_ref[pl.ds(r0, block), :]
        both = (do.astype(F32) * o_ref[pl.ds(r0, block), :].astype(F32)).T
        qs = [head_part(q, h, heads) for h in range(heads)]
        dos = [head_part(do, h, heads) for h in range(heads)]
        q_all = jnp.concatenate(qs, axis=0)
        do_all = jnp.concatenate(dos, axis=0)
        delta = [
            jnp.sum(both[h * HEAD : (h + 1) * HEAD], axis=0, keepdims=True) for h in range(heads)
        ]
        lse = [lse_ref[h : h + 1, pl.ds(r0, block)] for h in range(heads)]
        place = r0 + lax.broadcasted_iota(jnp.int32, (1, block), 1)
        start = seg_starts(len_ref, segs, place)
        first = seg_starts(len_ref, segs, r0) // block

        def key_step(j, dqs):
            c0 = pl.multiple_of(j * block, block)
            kb = qkv_ref[pl.ds(c0, block), hd : 2 * hd]
            vb = qkv_ref[pl.ds(c0, block), 2 * hd : 3 * hd]
            key_pos = key_rows + c0
            ok = (key_pos >= start) & (key_pos <= place)
            ps = []
            dss = []
            out = []
            for h in range(heads):
                s = lax.dot_general(kb, qs[h], NT, preferred_element_type=F32)
                p = jnp.where(ok, jnp.exp(s - lse[h]), 0.0)
                dp = lax.dot_general(vb, dos[h], NT, preferred_element_type=F32)
                ds = (p * (dp - delta[h])).astype(BF16)
                ps.append(p.astype(BF16))
                dss.append(ds)
                kt = kt_ref[h * HEAD : (h + 1) * HEAD, pl.ds(c0, block)]
                out.append(dqs[h] + jnp.dot(kt, ds, preferred_element_type=F32))
            dv_ref[pl.ds(c0, block), :] += jnp.dot(
                jnp.concatenate(ps, axis=1), do_all, preferred_element_type=F32
            )
            dk_ref[pl.ds(c0, block), :] += jnp.dot(
                jnp.concatenate(dss, axis=1), q_all, preferred_element_type=F32
            )
            return tuple(out)

        res = lax.fori_loop(first, i + 1, key_step, (jnp.zeros((HEAD, block), F32),) * heads)
        dq = jnp.concatenate(res, axis=0) * HEAD**-0.5
        d_ref[pl.ds(r0, block), 0:hd] = dq.T.astype(BF16)
        return 0

    lax.fori_loop(0, steps, query_step, 0)

    def finish(i, _):
        at = pl.multiple_of(i * block, block)
        d_ref[pl.ds(at, block), hd : 2 * hd] = dk_ref[pl.ds(at, block), :].astype(BF16)
        d_ref[pl.ds(at, block), 2 * hd : 3 * hd] = dv_ref[pl.ds(at, block), :].astype(BF16)
        return 0

    lax.fori_loop(0, steps, finish, 0)


VM = pl.BlockSpec(memory_space=pltpu.VMEM)
SM = pl.BlockSpec(memory_space=pltpu.SMEM)
LIMIT = 40 << 20


def attention_forward(row, qkv, block):
    rows, wide = qkv.shape
    hd = wide // 3
    heads = hd // HEAD
    pairs = rows * rows // 3 * heads
    return pl.pallas_call(
        functools.partial(forward_kernel, heads, block, row.shape[0]),
        out_shape=(
            jax.ShapeDtypeStruct((rows, hd), BF16),
            jax.ShapeDtypeStruct((heads, rows), F32),
        ),
        in_specs=[SM, VM],
        out_specs=(VM, VM),
        scratch_shapes=[pltpu.VMEM((hd, rows), BF16)],
        compiler_params=pltpu.CompilerParams(vmem_limit_bytes=LIMIT),
        cost_estimate=pl.CostEstimate(
            flops=pairs * 4 * HEAD, bytes_accessed=rows * wide * 4, transcendentals=pairs
        ),
        name="attention_forward",
    )(row, qkv)


def attention_backward(row, qkv, o, lse, do, block):
    rows, wide = qkv.shape
    hd = wide // 3
    heads = hd // HEAD
    pairs = rows * rows // 3 * heads
    return pl.pallas_call(
        functools.partial(backward_kernel, heads, block, row.shape[0]),
        out_shape=jax.ShapeDtypeStruct((rows, wide), BF16),
        in_specs=[SM] + [VM] * 4,
        out_specs=VM,
        scratch_shapes=[
            pltpu.VMEM((hd, rows), BF16),
            pltpu.VMEM((rows, hd), F32),
            pltpu.VMEM((rows, hd), F32),
        ],
        compiler_params=pltpu.CompilerParams(vmem_limit_bytes=LIMIT),
        cost_estimate=pl.CostEstimate(
            flops=pairs * 10 * HEAD, bytes_accessed=rows * wide * 6, transcendentals=pairs
        ),
        name="attention_backward",
    )(row, qkv, o, lse, do)


class Ring:
    def __init__(self, axis):
        self.axis = axis
        self.n = n = lax.axis_size(axis)
        me = lax.axis_index(axis)
        self.pos = jnp.where(me % 2 == 0, me // 2, n - 1 - me // 2)
        order = list(range(0, n, 2)) + list(range(1, n, 2))[::-1]
        self.up = [(order[i], order[(i + 1) % n]) for i in range(n)]
        self.down = [(b, a) for a, b in self.up]

    def shard(self, distance):
        p = (self.pos + distance + self.n) % self.n
        return jnp.where(p < self.n // 2, 2 * p, 2 * (self.n - 1 - p) + 1)

    def send_up(self, value):
        return lax.ppermute(value, self.axis, self.up)

    def send_down(self, value):
        return lax.ppermute(value, self.axis, self.down)

    def gather(self, value):
        half = value.shape[0] // 2
        above = below = value
        out = [(0, value)]
        for step in range(1, self.n // 2):
            below = self.send_up(below)
            above = self.send_down(above)
            out += [(-step, below), (step, above)]
        far = jnp.concatenate([self.send_up(below[:half]), self.send_down(above[half:])], axis=0)
        out.append((self.n // 2, far))
        return out

    def reduce(self, term):
        mid = self.n // 2
        far = term(mid).astype(BF16)
        half = far.shape[0] // 2
        up = self.send_up(far[:half])
        down = self.send_down(far[half:])
        for step in range(mid - 1, 0, -1):
            mine = term(step)
            other = term(-step)
            if step == mid - 1:
                low_mine = jnp.concatenate([mine[:half] + up.astype(F32), mine[half:]], axis=0)
                low_other = jnp.concatenate([other[:half], other[half:] + down.astype(F32)], axis=0)
            else:
                low_mine = mine + up.astype(F32)
                low_other = other + down.astype(F32)
            up = self.send_up(low_mine.astype(BF16))
            down = self.send_down(low_other.astype(BF16))
        return term(0) + up.astype(F32) + down.astype(F32)


def bits(n):
    return [1 << b for b in range(n.bit_length() - 1)]


def swap(value, axis, bit):
    n = lax.axis_size(axis)
    return lax.ppermute(value, axis, [(i, i ^ bit) for i in range(n)])


def cube_gather(value, axis):
    me = lax.axis_index(axis)
    held = [(0, value)]
    for bit in reversed(bits(lax.axis_size(axis))):
        held = held + [(mask ^ bit, swap(block, axis, bit)) for mask, block in held]
    return [(me ^ mask, block) for mask, block in held]


def gather_rows(value, axis):
    count = value.shape[0]
    whole = jnp.zeros((count * lax.axis_size(axis),) + value.shape[1:], value.dtype)
    for index, block in cube_gather(value, axis):
        whole = lax.dynamic_update_slice_in_dim(whole, block, index * count, 0)
    return whole


def scatter_sum(left, right, axis):
    n = lax.axis_size(axis)
    me = lax.axis_index(axis)
    tokens, wide = left.shape
    if n == 1:
        return lax.dot_general(left, right, TN, preferred_element_type=F32)
    split = left.reshape(tokens, n // 2, 2, wide // n)

    def half(which):
        part = lax.dynamic_index_in_dim(split, which, 2, keepdims=False)
        part = part.reshape(tokens, wide // 2)
        return lax.dot_general(part, right, TN, preferred_element_type=F32)

    away = half(1 - me % 2).astype(BF16)
    held = half(me % 2) + swap(away, axis, 1).astype(F32)
    count = n // 2
    for bit in bits(n)[1:]:
        held = held.reshape(count // 2, 2, wide // n, -1)
        side = (me // bit) % 2
        away = lax.dynamic_index_in_dim(held, 1 - side, 1, keepdims=False).astype(BF16)
        mine = lax.dynamic_index_in_dim(held, side, 1, keepdims=False)
        held = mine + swap(away, axis, bit).astype(F32)
        count = count // 2
    return held.reshape(wide // n, right.shape[1])


def ring_total(ring, value):
    rows, columns = value.shape
    wide = columns // ring.n

    def term(distance):
        return lax.dynamic_slice_in_dim(value, ring.shard(distance) * wide, wide, 1)

    mine = ring.reduce(term).astype(BF16)
    whole = jnp.zeros((rows, columns), F32)
    for distance, block in ring.gather(mine):
        whole = lax.dynamic_update_slice_in_dim(
            whole, block.astype(F32), ring.shard(distance) * wide, 1
        )
    return whole


def cube_sum(value):
    for axis in ("fsdp", "seq"):
        for bit in bits(lax.axis_size(axis)):
            value = value + swap(value, axis, bit)
    return value


def layer_norm(value, gain, shift):
    mean = jnp.mean(value, axis=-1, keepdims=True)
    centred = value - mean
    spread = jnp.mean(centred * centred, axis=-1, keepdims=True)
    return centred * lax.rsqrt(spread + 1e-05) * gain + shift


def shards(
    tokens,
    cotangent,
    lengths,
    deal,
    ln1_gain,
    ln1_shift,
    w_qkv,
    bias_qv,
    w_out,
    bias_out,
    ln2_gain,
    ln2_shift,
    w_fc,
    bias_fc,
    w_proj,
    bias_proj,
):
    x = tokens[0]
    dy = cotangent[0]
    rows, width = x.shape
    ring = Ring("seq")
    n_seq = ring.n
    n_fsdp = lax.axis_size("fsdp")
    me_seq = lax.axis_index("seq")
    me_fsdp = lax.axis_index("fsdp")
    group_rows = rows * n_seq
    heads = H // n_seq
    hd = heads * HEAD
    block = rows
    row = lengths[deal[me_fsdp]]
    last = lengths.shape[1] - 1

    small = (ln1_gain, ln1_shift, bias_qv, bias_out, ln2_gain, ln2_shift, bias_fc, bias_proj)
    packed_small = gather_rows(jnp.concatenate(small)[None], "fsdp")
    vectors = []
    at = 0
    for vector in small:
        count = vector.shape[0]
        vectors.append(packed_small[:, at : at + count].reshape(-1).astype(F32))
        at += count
    gain_one, shift_one, bqv, bout, gain_two, shift_two, bfc, bproj = vectors

    own_cols = lax.dynamic_index_in_dim(
        w_qkv.reshape(-1, n_seq, heads, 3, HEAD), me_seq, 1, keepdims=False
    )
    own_cols = own_cols.transpose(0, 2, 1, 3).reshape(-1, 3 * hd)
    w_own = gather_rows(own_cols, "fsdp")
    b_own = lax.dynamic_index_in_dim(bqv.reshape(n_seq, heads, 2, HEAD), me_seq, 0, keepdims=False)
    b_own = jnp.concatenate(
        [b_own[:, 0].reshape(hd), jnp.zeros((hd,), F32), b_own[:, 1].reshape(hd)]
    )

    wout = gather_rows(w_out, "fsdp")
    wfc = gather_rows(w_fc, "fsdp")
    wproj = gather_rows(w_proj, "fsdp")

    low_all = jnp.zeros((group_rows, width), BF16)
    qkv = jnp.zeros((group_rows, 3 * hd), BF16)
    for distance, piece in ring.gather(x):
        low = layer_norm(piece.astype(F32), gain_one, shift_one).astype(BF16)
        part = (jnp.dot(low, w_own, preferred_element_type=F32) + b_own).astype(BF16)
        place = ring.shard(distance) * rows
        low_all = lax.dynamic_update_slice_in_dim(low_all, low, place, 0)
        qkv = lax.dynamic_update_slice_in_dim(qkv, part, place, 0)

    attended, lse = attention_forward(row, qkv, block)
    merged = lax.all_to_all(
        attended.reshape(n_seq, rows, hd), "seq", split_axis=0, concat_axis=0, tiled=True
    )
    merged = merged.transpose(1, 0, 2).reshape(rows, n_seq * hd)

    xf = x.astype(F32)
    ends = jnp.cumsum(row)
    places = me_seq * rows + jnp.arange(rows, dtype=jnp.int32)
    own = jnp.sum((places[:, None] >= ends[None, :]).astype(jnp.int32), axis=1)
    valid = (own < last)[:, None]

    attn_branch = jnp.dot(merged, wout, preferred_element_type=F32) + bout
    middle = xf + attn_branch
    normed_two, norm_two_back = jax.vjp(layer_norm, middle, gain_two, shift_two)
    low_two = normed_two.astype(BF16)
    inner = jnp.dot(low_two, wfc, preferred_element_type=F32) + bfc
    activated, gelu_back = jax.vjp(functools.partial(jax.nn.gelu, approximate=True), inner)
    hidden = activated.astype(BF16)
    mlp_branch = jnp.dot(hidden, wproj, preferred_element_type=F32) + bproj
    result = middle + mlp_branch
    output = jnp.where(valid, result, 0.0).astype(BF16)
    squares = jnp.stack(
        [jnp.sum(jnp.where(valid, part * part, 0.0)) for part in (result, attn_branch, mlp_branch)]
        + [jnp.sum(valid.astype(F32))]
    )

    d_result = jnp.where(valid, dy.astype(F32), 0.0)
    d_mlp = d_result.astype(BF16)
    grad_bproj = jnp.sum(d_result, axis=0)
    d_hidden = lax.dot_general(d_mlp, wproj, NT, preferred_element_type=F32)
    d_inner = gelu_back(d_hidden)[0].astype(BF16)
    grad_bfc = jnp.sum(d_inner.astype(F32), axis=0)
    d_two = lax.dot_general(d_inner, wfc, NT, preferred_element_type=F32)
    d_mid_norm, grad_gain_two, grad_shift_two = norm_two_back(d_two)
    d_middle = d_result + d_mid_norm
    d_attn = d_middle.astype(BF16)
    grad_bout = jnp.sum(d_attn.astype(F32), axis=0)
    d_merged = lax.dot_general(d_attn, wout, NT, preferred_element_type=F32).astype(BF16)
    d_heads = lax.all_to_all(
        d_merged.reshape(rows, n_seq, hd).transpose(1, 0, 2),
        "seq",
        split_axis=0,
        concat_axis=0,
        tiled=True,
    ).reshape(group_rows, hd)

    grad_wproj = ring_total(ring, scatter_sum(hidden, d_mlp, "fsdp"))
    share_wfc = scatter_sum(low_two, d_inner, "fsdp")
    share_wout = scatter_sum(merged, d_attn, "fsdp")
    total = ring_total(ring, jnp.concatenate([share_wfc, share_wout], axis=1))
    grad_wfc = total[:, : wfc.shape[1]]
    grad_wout = total[:, wfc.shape[1] :]

    d_own = attention_backward(row, qkv, attended, lse, d_heads, block)

    share_qkv = scatter_sum(low_all, d_own, "fsdp").astype(BF16)
    parts = jnp.zeros((n_seq,) + share_qkv.shape, BF16)
    for distance, piece in ring.gather(share_qkv):
        parts = lax.dynamic_update_slice_in_dim(parts, piece[None], ring.shard(distance), 0)
    grad_wqkv = (
        parts.reshape(n_seq, -1, 3, heads, HEAD)
        .transpose(1, 0, 3, 2, 4)
        .reshape(-1, 3 * H * HEAD)
        .astype(F32)
    )
    d_sums = jnp.sum(d_own.astype(F32), axis=0).reshape(3, heads, HEAD)
    d_sums = jnp.stack([d_sums[0], d_sums[2]], axis=1).reshape(1, 2 * hd)
    grad_bqv = lax.dynamic_update_slice_in_dim(
        jnp.zeros((n_seq, 2 * hd), F32), d_sums, me_seq, 0
    ).reshape(-1)

    def share_one(distance):
        part = lax.dynamic_slice_in_dim(d_own, ring.shard(distance) * rows, rows, 0)
        return lax.dot_general(part, w_own, NT, preferred_element_type=F32)

    d_one = ring.reduce(share_one)
    _, norm_one_back = jax.vjp(layer_norm, xf, gain_one, shift_one)
    d_in_norm, grad_gain_one, grad_shift_one = norm_one_back(d_one)
    input_grad = d_middle + d_in_norm

    def own_share(vector):
        count = vector.shape[0] // n_fsdp
        return lax.dynamic_slice_in_dim(vector, me_fsdp * count, count, 0)

    early = [grad_bout, grad_gain_two, grad_shift_two, grad_bfc, grad_bproj, squares]
    late = [grad_gain_one, grad_shift_one, grad_bqv]

    def summed(vectors):
        flat = cube_sum(jnp.concatenate(vectors))
        out = []
        at = 0
        for vector in vectors:
            out.append(flat[at : at + vector.shape[0]])
            at += vector.shape[0]
        return out

    sum_bout, sum_g2, sum_s2, sum_bfc, sum_bproj, sum_squares = summed(early)
    sum_g1, sum_s1, sum_bqv = summed(late)
    stats = jnp.sqrt(sum_squares[:3] / (sum_squares[3] * width))
    return (
        output[None],
        input_grad[None],
        own_share(sum_g1),
        own_share(sum_s1),
        grad_wqkv,
        own_share(sum_bqv),
        grad_wout,
        own_share(sum_bout),
        own_share(sum_g2),
        own_share(sum_s2),
        grad_wfc,
        own_share(sum_bfc),
        grad_wproj,
        own_share(sum_bproj),
        stats,
    )


def solution(mesh):
    rows_split = P("fsdp", "seq", None)
    matrix = P("fsdp", None)
    vector = P("fsdp")
    params = (
        vector,
        vector,
        matrix,
        vector,
        matrix,
        vector,
        vector,
        vector,
        matrix,
        vector,
        matrix,
        vector,
    )
    return jax.shard_map(
        shards,
        mesh=mesh,
        in_specs=(rows_split, rows_split, P(), P()) + params,
        out_specs=(rows_split, rows_split) + params + (P(),),
        check_vma=False,
    )
```

time: 1140 us -> 724 us (0.64)
  matrix products: 335 us -> 85.6 us
  blocking collectives: 174 us -> 0 us
  waiting for transfers between devices: 386 us -> 253 us
  local copies, waits for them, and re-layouts: 52 us -> 179 us
  other arithmetic: 136 us -> 42.1 us
  starting transfers between devices: 16.4 us -> 98.6 us
  Pallas kernels: 0 us -> 50.1 us
  loops' own time: 21 us -> 0 us
    dot_general x54 -> x30, matrix products: 335 us -> 85.6 us  [the longest x8 32.7 us: half(): return lax.dot_general(part, right, TN, preferred_element_type=F32)]
    ppermute x0 -> x89, waiting for transfers between devices: none -> 249 us  [the longest x33 122 us: swap(): return lax.ppermute(value, axis, [(i, i ^ bit) for i in range(n)])]
    psum x1 -> x0, waiting for transfers between devices: 187 us -> none  [shards(): lax.psum(share_qkv.astype(jnp.bfloat16), 'seq').astype(jnp.float32)]
    ppermute x0 -> x89, starting transfers between devices: none -> 89.2 us  [the longest x28 34.3 us: send_up(): return lax.ppermute(value, self.axis, self.up)]
    all_gather x8 -> x0, waiting for transfers between devices: 85.1 us -> none  [the longest x1 41.6 us: shards(): lax.all_gather(w_qkv, 'fsdp', axis=0, tiled=True)]
    psum x2 -> x0, blocking collectives: 61 us -> none  [the longest x1 39.8 us: shards(): totals, count_all = lax.psum((squares, counted), ('seq', 'fsdp'))]
    all_to_all x3 -> x2, waiting for transfers between devices: 63 us -> 3.91 us  [the longest x1 3.9 us: shards(): lax.all_to_all(attended.reshape(n_seq, rows, hd), 'seq', split_axis=0, co...]
    all_to_all x1 -> x0, blocking collectives: 58.7 us -> none  [shards(): lax.all_to_all(d_grouped, 'seq', split_axis=0, concat_axis=1, tiled=True)]
  transfers between devices with their start and end apart: 16 -> 91, of which waited for: 7 -> 37; matrix products, arithmetic and copies ran while one was open for 41% -> 35% of each run, Pallas kernels for 0% -> 7%
where the time goes in v1:
time: 724 us; the launch traced here: 714 us
  waiting for transfers between devices  253 us (35%)
  local copies, waits for them, and re-layouts  179 us (25%)
  starting transfers between devices  98.6 us (14%)
  matrix products  85.6 us (12%)
  Pallas kernels  50.1 us (7%)
  other arithmetic  42.1 us (6%)
    ppermute x33, waiting for transfers between devices, swap(): return lax.ppermute(value, axis, [(i, i ^ bit) for i in range(n)])  122 us
    ppermute x28, waiting for transfers between devices, send_down(): return lax.ppermute(value, self.axis, self.down)  78.9 us
    ppermute x28, waiting for transfers between devices, send_up(): return lax.ppermute(value, self.axis, self.up)  48.4 us
    unnamed x226, local copies, waits for them, and re-layouts  47.6 us
    ppermute x28, starting transfers between devices, send_up(): return lax.ppermute(value, self.axis, self.up)  34.3 us
    dot_general x8, matrix products, half(): return lax.dot_general(part, right, TN, preferred_element_type=F32)  32.7 us
    ppermute x28, starting transfers between devices, send_down(): return lax.ppermute(value, self.axis, self.down)  29.2 us
    dynamic_update_slice x20, local copies, waits for them, and re-layouts, gather_rows(): whole = lax.dynamic_update_slice_in_dim(whole, block, index * count, 0)  29.1 us
  transfers between devices with their start and end apart: 91, of which 37 were waited for; matrix products, arithmetic and copies ran while one was open for 35% of the time, Pallas kernels for 7%

profile of v1, /device:TPU:0, one launch (start us, length us, event | category | flops | bytes accessed | tf_op | source)
XLA Modules:
  0.0 714.1 jit_solution(1818989794738339211)
XLA Ops:
  51.3 8.0 %collective-permute-done.6 = bf16[384,1024]{1,0:T(8,128)(2,1)S(1)} collective-permute-done((bf16[384,1024]{1,0:T(8,128)(2,1)S(1)}, bf16[384,1024]{1,0:T(8,128)(2,1)S(1)}, u32[]{:S(2)}, u32[]{:S(2)}) %collective-permute-start.6) | collective-permute-done | bytes 786464 | tf_op jit(solution)/shard_map/ppermute | solution.py:228
  59.5 5.3 collective-permute-done.7
  70.3 14.0 %collective-permute-done.9 = bf16[384,1024]{1,0:T(8,128)(2,1)S(1)} collective-permute-done((bf16[384,1024]{1,0:T(8,128)(2,1)S(1)}, bf16[384,1024]{1,0:T(8,128)(2,1)S(1)}, u32[]{:S(2)}, u32[]{:S(2)}) %collective-permute-start.9) | collective-permute-done | bytes 786464 | tf_op jit(solution)/shard_map/ppermute | solution.py:231
  88.3 6.7 collective-permute-done.17
  99.7 39.4 %collective-permute-done.20 = bf16[1024,1024]{1,0:T(8,128)(2,1)} collective-permute-done((bf16[1024,1024]{1,0:T(8,128)(2,1)S(1)}, bf16[1024,1024]{1,0:T(8,128)(2,1)}, u32[]{:S(2)}, u32[]{:S(2)}) %collective-permute-start.20) | collective-permute-done | bytes 2097184 | tf_op jit(solution)/shard_map/ppermute | solution.py:271
  187.3 21.6 %attention_forward.1 = (bf16[3072,128]{1,0:T(8,128)(2,1)S(1)}, f32[2,3072]{1,0:T(2,128)S(1)}) custom-call(s32[4]{0:T(128)S(1)} %get-tuple-element.139.len_ref, bf16[3072,384]{1,0:T(8,128)(2,1)S(1)} %fusion.77.qkv_ref), custom_call_target="tpu_custom_call" | custom-call | flops 1610612736 | bytes 4718592 | tf_op jit(solution)/shard_map/attention_forward/pallas_call | solution.py:173
  210.0 5.5 all-to-all-start
  224.2 6.2 constant_dynamic-slice_fusion.8
  256.2 7.2 %multiply_convert_fusion = (bf16[384,4096]{1,0:T(8,128)(2,1)S(1)}, f32[384,4096]{1,0:T(8,128)S(1)}) fusion(f32[4096]{0:T(1024)S(1)} %bitcast.303, bf16[384,1024]{1,0:T(8,128)(2,1)S(1)} %copy-done.48, bf16[1024,4096]{1,0:T(8,128)(2,1)} %constant_dynamic-update-slice_fusion.13), kind=kOutput, calls=%fused_computation.28 | convolution fusion | flops 3236954112 | bytes 18628608 | tf_op jit(solution)/shard_map/dot_general | solution.py:428
  267.8 9.5 %convert_reduce_fusion = (f32[4096]{0:T(1024)S(1)}, bf16[384,4096]{1,0:T(8,128)(2,1)S(1)}) fusion(f32[384,4096]{1,0:T(8,128)S(1)} %get-tuple-element.143, bf16[4096,1024]{1,0:T(8,128)(2,1)} %constant_dynamic-update-slice_fusion.9, bf16[1,384,1024]{2,1,0:T(8,128)(2,1)S(1)} %copy-done.19, pred[384]{0:T(512)(128)(4,1)S(1)} %copy-done.90), kind=kOutput, calls=%fused_computation.27 | convolution fusion | flops 3257004032 | bytes 18628992 | tf_op jit(solution)/shard_map/dot_general | solution.py:442
  277.3 7.0 fusion.179
  284.4 9.1 %select_reduce_fusion = (f32[]{:T(128)}, f32[]{:T(128)}, f32[384]{0:T(512)S(1)}, f32[1024]{0:T(1024)S(1)}, f32[1024]{0:T(1024)S(1)}, /*index=5*/f32[]{:T(128)}, f32[1024]{0:T(1024)S(1)}, bf16[1,384,1024]{2,1,0:T(8,128)(2,1)}) fusion(f32[1024]{0:T(1024)S(1)} %bitcast.304, pred[384]{0:T(512)(128)(4,1)S(1)} %copy-done.90, ...), kind=kOutput, calls=%fused_computation.121 | convolution fusion | flops 3230659072 | bytes 17851276 | tf_op jit(solution)/shard_map/dot_general | solution.py:431
  300.8 6.1 reshape.494
  312.7 6.4 convolution_convert_fusion
  325.6 9.2 %constant_dynamic-slice_fusion.1 = (bf16[384,2,1,1024]{3,2,1,0:T(2,128)(2,1)}, bf16[384,2,1,1024]{3,2,1,0:T(2,128)(2,1)}) fusion(bf16[384,2,2,1024]{3,2,1,0:T(2,128)(2,1)S(1)} %copy-done.13, s32[]{:T(128)S(6)} %select_n.537, s32[]{:T(128)S(6)} %select_n.538), kind=kLoop, calls=%fused_computation.282 | loop fusion | bytes 6291464 | tf_op jit(solution)/shard_map/jit(dynamic_index_in_dim)/dynamic_slice | solution.py:299
  334.8 8.3 %copy.90 = bf16[384,2,1,1024]{0,3,1,2:T(8,128)(2,1)} copy(bf16[384,2,1,1024]{3,2,1,0:T(2,128)(2,1)} %get-tuple-element.106) | data formatting | bytes 3145728
  347.8 5.8 convolution_convert_fusion.1
  353.6 8.4 %copy.89 = bf16[384,2,1,1024]{0,3,1,2:T(8,128)(2,1)} copy(bf16[384,2,1,1024]{3,2,1,0:T(2,128)(2,1)} %get-tuple-element.105) | data formatting | bytes 3145728
  374.8 28.5 %attention_backward.1 = bf16[3072,384]{1,0:T(8,128)(2,1)S(1)} custom-call(s32[4]{0:T(128)S(1)} %get-tuple-element.139.len_ref, bf16[3072,384]{1,0:T(8,128)(2,1)S(1)} %copy-done.1, bf16[3072,128]{1,0:T(8,128)(2,1)S(1)} %get-tuple-element.17.o_ref, f32[2,3072]{1,0:T(2,128)S(1)} %get-tuple-element.18.lse_ref, bf16[3072,128]{1,0:T(8,128)(2,1)S(1)} %bitcast.262), custom_call_target="tpu_custom_call" | custom-call | flops 4026531840 | bytes 7077888 | tf_op jit(solution)/shard_map/attention_backward/pallas_call | solution.py:195
  434.9 18.4 %collective-permute-done.38 = bf16[256,384]{0,1:T(8,128)(2,1)S(1)} collective-permute-done((bf16[256,384]{0,1:T(8,128)(2,1)S(1)}, bf16[256,384]{0,1:T(8,128)(2,1)S(1)}, u32[]{:S(2)}, u32[]{:S(2)}) %collective-permute-start.38) | collective-permute-done | bytes 196640 | tf_op jit(solution)/shard_map/ppermute | solution.py:228
  483.2 11.0 %collective-permute-done.29 = bf16[384,1024]{1,0:T(8,128)(2,1)S(1)} collective-permute-done((bf16[384,1024]{1,0:T(8,128)(2,1)S(1)}, bf16[384,1024]{1,0:T(8,128)(2,1)S(1)}, u32[]{:S(2)}, u32[]{:S(2)}) %collective-permute-start.29) | collective-permute-done | bytes 786464 | tf_op jit(solution)/shard_map/ppermute | solution.py:231
  500.0 7.9 %convert_add_fusion.1 = f32[512,4096]{1,0:T(8,128)} fusion(bf16[512,4096]{1,0:T(8,128)(2,1)} %collective-permute-done.46, bf16[384,512]{0,1:T(8,128)(2,1)S(1)} %bitcast.280, bf16[384,4096]{1,0:T(8,128)(2,1)S(1)} %copy-done.57), kind=kOutput, calls=%fused_computation.11 | convolution fusion | flops 1614807040 | bytes 16121856 | tf_op jit(solution)/shard_map/dot_general | solution.py:301
  524.3 72.9 %collective-permute-done.32 = f32[4096]{0:T(1024)S(1)} collective-permute-done((f32[4096]{0:T(1024)S(1)}, f32[4096]{0:T(1024)S(1)}, u32[]{:S(2)}, u32[]{:S(2)}) %collective-permute-start.32) | collective-permute-done | bytes 16416 | tf_op jit(solution)/shard_map/ppermute | solution.py:271
  644.8 9.8 %collective-permute-done.79 = bf16[1024,128]{1,0:T(8,128)(2,1)S(1)} collective-permute-done((bf16[1024,128]{1,0:T(8,128)(2,1)S(1)}, bf16[1024,128]{1,0:T(8,128)(2,1)S(1)}, u32[]{:S(2)}, u32[]{:S(2)}) %collective-permute-start.79) | collective-permute-done | bytes 262176 | tf_op jit(solution)/shard_map/ppermute | solution.py:231
  (645 shorter events, 375.9 us)
Async XLA Ops:
  8.0 28.3 %collective-permute-start = (bf16[1,3072]{1,0:T(2,128)(2,1)}, bf16[1,3072]{1,0:T(2,128)(2,1)}, u32[]{:S(2)}, u32[]{:S(2)}) collective-permute-start(bf16[1,3072]{1,0:T(2,128)(2,1)} %broadcast_in_dim.87), channel_id=1, source_target_pairs={{0,2},{1,3},{2,0},{3,1},{4,6},{5,7},{6,4},{7,5},{8,10},{9,11},{10,... | collective-permute-start | bytes 18440 | tf_op jit(solution)/shard_map/ppermute | solution.py:271
  12.8 32.0 %collective-permute-start.3 = (bf16[256,384]{0,1:T(8,128)(2,1)S(1)}, bf16[256,384]{0,1:T(8,128)(2,1)S(1)}, u32[]{:S(2)}, u32[]{:S(2)}) collective-permute-start(bf16[256,384]{0,1:T(8,128)(2,1)S(1)} %bitcast.281), channel_id=1, source_target_pairs={{0,2},{1,3},{2,0},{3,1},{4,6},{5,7},{6,4},{7,5},{8,10},{9,11},{10,... | collective-permute-start | bytes 589832 | tf_op jit(solution)/shard_map/ppermute | solution.py:271
  12.9 31.9 %collective-permute-start.4 = (bf16[256,384]{0,1:T(8,128)(2,1)S(1)}, bf16[256,384]{0,1:T(8,128)(2,1)S(1)}, u32[]{:S(2)}, u32[]{:S(2)}) collective-permute-start(bf16[256,384]{0,1:T(8,128)(2,1)S(1)} %bitcast.282), channel_id=1, source_target_pairs={{0,1},{1,0},{2,3},{3,2},{4,5},{5,4},{6,7},{7,6},{8,9},{9,8},{10,11... | collective-permute-start | bytes 589832 | tf_op jit(solution)/shard_map/ppermute | solution.py:271
  13.4 33.3 %collective-permute-start.14 = (bf16[256,1024]{1,0:T(8,128)(2,1)}, bf16[256,1024]{1,0:T(8,128)(2,1)}, u32[]{:S(2)}, u32[]{:S(2)}) collective-permute-start(bf16[256,1024]{1,0:T(8,128)(2,1)} %param.24), channel_id=1, source_target_pairs={{0,2},{1,3},{2,0},{3,1},{4,6},{5,7},{6,4},{7,5},{8,10},{9,11},{10,... | collective-permute-start | bytes 1572872 | tf_op jit(solution)/shard_map/ppermute | solution.py:271
  46.2 48.8 %collective-permute-start.17 = (bf16[256,4096]{1,0:T(8,128)(2,1)}, bf16[256,4096]{1,0:T(8,128)(2,1)}, u32[]{:S(2)}, u32[]{:S(2)}) collective-permute-start(bf16[256,4096]{1,0:T(8,128)(2,1)} %param.28), channel_id=1, source_target_pairs={{0,2},{1,3},{2,0},{3,1},{4,6},{5,7},{6,4},{7,5},{8,10},{9,11},{10,... | collective-permute-start | bytes 6291464 | tf_op jit(solution)/shard_map/ppermute | solution.py:271
  46.8 95.4 %collective-permute-start.18 = (bf16[256,4096]{1,0:T(8,128)(2,1)}, bf16[256,4096]{1,0:T(8,128)(2,1)S(1)}, u32[]{:S(2)}, u32[]{:S(2)}) collective-permute-start(bf16[256,4096]{1,0:T(8,128)(2,1)} %param.28), channel_id=1, source_target_pairs={{0,1},{1,0},{2,3},{3,2},{4,5},{5,4},{6,7},{7,6},{8,9},{9,8},{10,11... | collective-permute-start | bytes 6291464 | tf_op jit(solution)/shard_map/ppermute | solution.py:271
  68.9 70.2 %collective-permute-start.20 = (bf16[1024,1024]{1,0:T(8,128)(2,1)S(1)}, bf16[1024,1024]{1,0:T(8,128)(2,1)}, u32[]{:S(2)}, u32[]{:S(2)}) collective-permute-start(bf16[1024,1024]{1,0:T(8,128)(2,1)S(1)} %copy-done.60), channel_id=1, source_target_pairs={{0,2},{1,3},{2,0},{3,1},{4,6},{5,7},{6,4},{7,5},{8,10},{9,11},{10,... | collective-permute-start | bytes 6291464 | tf_op jit(solution)/shard_map/ppermute | solution.py:271
  84.3 59.9 %collective-permute-start.21 = (bf16[1024,1024]{1,0:T(8,128)(2,1)S(1)}, bf16[1024,1024]{1,0:T(8,128)(2,1)S(1)}, u32[]{:S(2)}, u32[]{:S(2)}) collective-permute-start(bf16[1024,1024]{1,0:T(8,128)(2,1)S(1)} %copy-done.60), channel_id=1, source_target_pairs={{0,1},{1,0},{2,3},{3,2},{4,5},{5,4},{6,7},{7,6},{8,9},{9,8},{10,11... | collective-permute-start | bytes 6291464 | tf_op jit(solution)/shard_map/ppermute | solution.py:271
  84.5 61.3 %collective-permute-start.11 = (bf16[384,1024]{1,0:T(8,128)(2,1)S(1)}, bf16[384,1024]{1,0:T(8,128)(2,1)S(1)}, u32[]{:S(2)}, u32[]{:S(2)}) collective-permute-start(bf16[384,1024]{1,0:T(8,128)(2,1)S(1)} %collective-permute-done.9), channel_id=1, source_target_pairs={{8,0},{16,8},{24,16},{28,24},{20,28},{12,20},{4,12},{0,4},{9,1},{1... | collective-permute-start | bytes 2359304 | tf_op jit(solution)/shard_map/ppermute | solution.py:231
  95.0 51.4 %collective-permute-start.10 = (bf16[384,1024]{1,0:T(8,128)(2,1)S(1)}, bf16[384,1024]{1,0:T(8,128)(2,1)S(1)}, u32[]{:S(2)}, u32[]{:S(2)}) collective-permute-start(bf16[384,1024]{1,0:T(8,128)(2,1)S(1)} %collective-permute-done.8), channel_id=1, source_target_pairs={{0,8},{8,16},{16,24},{24,28},{28,20},{20,12},{12,4},{4,0},{1,9},{9... | collective-permute-start | bytes 2359304 | tf_op jit(solution)/shard_map/ppermute | solution.py:228
  139.1 113.8 %collective-permute-start.19 = (bf16[256,4096]{1,0:T(8,128)(2,1)}, bf16[256,4096]{1,0:T(8,128)(2,1)}, u32[]{:S(2)}, u32[]{:S(2)}) collective-permute-start(bf16[256,4096]{1,0:T(8,128)(2,1)} %collective-permute-done.17), channel_id=1, source_target_pairs={{0,1},{1,0},{2,3},{3,2},{4,5},{5,4},{6,7},{7,6},{8,9},{9,8},{10,11... | collective-permute-start | bytes 6291464 | tf_op jit(solution)/shard_map/ppermute | solution.py:271
  142.2 121.3 %collective-permute-start.22 = (bf16[1024,1024]{1,0:T(8,128)(2,1)}, bf16[1024,1024]{1,0:T(8,128)(2,1)}, u32[]{:S(2)}, u32[]{:S(2)}) collective-permute-start(bf16[1024,1024]{1,0:T(8,128)(2,1)} %collective-permute-done.20), channel_id=1, source_target_pairs={{0,1},{1,0},{2,3},{3,2},{4,5},{5,4},{6,7},{7,6},{8,9},{9,8},{10,11... | collective-permute-start | bytes 6291464 | tf_op jit(solution)/shard_map/ppermute | solution.py:271
  308.0 63.1 %all-to-all-start.1 = ((bf16[8,384,128]{2,1,0:T(8,128)(2,1)}), bf16[8,384,128]{2,1,0:T(8,128)(2,1)S(1)}, u32[]{:S(2)}, u32[]{:S(2)}) async-start(bf16[8,384,128]{2,1,0:T(8,128)(2,1)} %bitcast.259), calls=%async_computation.1 | async-start | bytes 1572864 | tf_op jit(solution)/shard_map/all_to_all | solution.py:451
  319.1 179.0 %collective-permute-start.46 = (bf16[512,4096]{1,0:T(8,128)(2,1)}, bf16[512,4096]{1,0:T(8,128)(2,1)}, u32[]{:S(2)}, u32[]{:S(2)}) collective-permute-start(bf16[512,4096]{1,0:T(8,128)(2,1)} %convolution_convert_fusion), channel_id=1, source_target_pairs={{0,1},{1,0},{2,3},{3,2},{4,5},{5,4},{6,7},{7,6},{8,9},{9,8},{10,11... | collective-permute-start | bytes 12582920 | tf_op jit(solution)/shard_map/ppermute | solution.py:271
  322.9 44.1 %collective-permute-start.48 = (bf16[512,1024]{1,0:T(8,128)(2,1)}, bf16[512,1024]{1,0:T(8,128)(2,1)}, u32[]{:S(2)}, u32[]{:S(2)}) collective-permute-start(bf16[512,1024]{1,0:T(8,128)(2,1)} %convolution_convert_fusion.2), channel_id=1, source_target_pairs={{0,1},{1,0},{2,3},{3,2},{4,5},{5,4},{6,7},{7,6},{8,9},{9,8},{10,11... | collective-permute-start | bytes 3145736 | tf_op jit(solution)/shard_map/ppermute | solution.py:271
  353.6 161.4 %collective-permute-start.71 = (bf16[2048,1024]{1,0:T(8,128)(2,1)}, bf16[2048,1024]{1,0:T(8,128)(2,1)}, u32[]{:S(2)}, u32[]{:S(2)}) collective-permute-start(bf16[2048,1024]{1,0:T(8,128)(2,1)} %convolution_convert_fusion.1), channel_id=1, source_target_pairs={{0,1},{1,0},{2,3},{3,2},{4,5},{5,4},{6,7},{7,6},{8,9},{9,8},{10,11... | collective-permute-start | bytes 12582920 | tf_op jit(solution)/shard_map/ppermute | solution.py:271
  370.4 47.4 %collective-permute-start.49 = (bf16[1,256,1024]{2,1,0:T(8,128)(2,1)}, bf16[1,256,1024]{2,1,0:T(8,128)(2,1)}, u32[]{:S(2)}, u32[]{:S(2)}) collective-permute-start(bf16[1,256,1024]{2,1,0:T(8,128)(2,1)} %fusion.117), channel_id=1, source_target_pairs={{0,2},{1,3},{2,0},{3,1},{4,6},{5,7},{6,4},{7,5},{8,10},{9,11},{10,... | collective-permute-start | bytes 1572872 | tf_op jit(solution)/shard_map/ppermute | solution.py:271
  422.5 50.6 %collective-permute-start.28 = (bf16[384,1024]{1,0:T(8,128)(2,1)}, bf16[384,1024]{1,0:T(8,128)(2,1)}, u32[]{:S(2)}, u32[]{:S(2)}) collective-permute-start(bf16[384,1024]{1,0:T(8,128)(2,1)} %pad_maximum_fusion.2), channel_id=1, source_target_pairs={{8,0},{16,8},{24,16},{28,24},{20,28},{12,20},{4,12},{0,4},{9,1},{1... | collective-permute-start | bytes 2359304 | tf_op jit(solution)/shard_map/ppermute | solution.py:231
  429.2 45.7 %collective-permute-start.24 = (bf16[384,1024]{1,0:T(8,128)(2,1)}, bf16[384,1024]{1,0:T(8,128)(2,1)}, u32[]{:S(2)}, u32[]{:S(2)}) collective-permute-start(bf16[384,1024]{1,0:T(8,128)(2,1)} %pad_maximum_fusion.1), channel_id=1, source_target_pairs={{0,8},{8,16},{16,24},{24,28},{28,20},{20,12},{12,4},{4,0},{1,9},{9... | collective-permute-start | bytes 2359304 | tf_op jit(solution)/shard_map/ppermute | solution.py:228
  481.3 43.0 %collective-permute-start.45 = (bf16[128,384]{0,1:T(8,128)(2,1)S(1)}, bf16[128,384]{0,1:T(8,128)(2,1)S(1)}, u32[]{:S(2)}, u32[]{:S(2)}) collective-permute-start(bf16[128,384]{0,1:T(8,128)(2,1)S(1)} %slice.272), channel_id=1, source_target_pairs={{8,0},{16,8},{24,16},{28,24},{20,28},{12,20},{4,12},{0,4},{9,1},{1... | collective-permute-start | bytes 294920 | tf_op jit(solution)/shard_map/ppermute | solution.py:231
  494.2 30.1 %collective-permute-start.44 = (bf16[128,384]{0,1:T(8,128)(2,1)S(1)}, bf16[128,384]{0,1:T(8,128)(2,1)S(1)}, u32[]{:S(2)}, u32[]{:S(2)}) collective-permute-start(bf16[128,384]{0,1:T(8,128)(2,1)S(1)} %slice.271), channel_id=1, source_target_pairs={{0,8},{8,16},{16,24},{24,28},{28,20},{20,12},{12,4},{4,0},{1,9},{9... | collective-permute-start | bytes 294920 | tf_op jit(solution)/shard_map/ppermute | solution.py:228
  511.8 93.0 %collective-permute-start.47 = (bf16[1,256,4096]{2,1,0:T(8,128)(2,1)}, bf16[1,256,4096]{2,1,0:T(8,128)(2,1)}, u32[]{:S(2)}, u32[]{:S(2)}) collective-permute-start(bf16[1,256,4096]{2,1,0:T(8,128)(2,1)} %fusion.12), channel_id=1, source_target_pairs={{0,2},{1,3},{2,0},{3,1},{4,6},{5,7},{6,4},{7,5},{8,10},{9,11},{10,... | collective-permute-start | bytes 6291464 | tf_op jit(solution)/shard_map/ppermute | solution.py:271
  522.2 86.3 %collective-permute-start.72 = (bf16[1,1024,1024]{2,1,0:T(8,128)(2,1)}, bf16[1,1024,1024]{2,1,0:T(8,128)(2,1)}, u32[]{:S(2)}, u32[]{:S(2)}) collective-permute-start(bf16[1,1024,1024]{2,1,0:T(8,128)(2,1)} %fusion.13), channel_id=1, source_target_pairs={{0,2},{1,3},{2,0},{3,1},{4,6},{5,7},{6,4},{7,5},{8,10},{9,11},{10,... | collective-permute-start | bytes 6291464 | tf_op jit(solution)/shard_map/ppermute | solution.py:271
  523.5 73.7 %collective-permute-start.32 = (f32[4096]{0:T(1024)S(1)}, f32[4096]{0:T(1024)S(1)}, u32[]{:S(2)}, u32[]{:S(2)}) collective-permute-start(f32[4096]{0:T(1024)S(1)} %fusion.166), channel_id=1, source_target_pairs={{0,2},{1,3},{2,0},{3,1},{4,6},{5,7},{6,4},{7,5},{8,10},{9,11},{10,... | collective-permute-start | bytes 49160 | tf_op jit(solution)/shard_map/ppermute | solution.py:271
  (169 other events, 1829.8 us)

commit v2 on v1

v2 whole, which is shorter than its diff:
```python
import functools

import jax
import jax.numpy as jnp
from jax import lax
from jax.experimental import pallas as pl
from jax.experimental.pallas import tpu as pltpu
from jax.sharding import PartitionSpec as P

H = 16
HEAD = 64
NT = (((1,), (1,)), ((), ()))
TN = (((0,), (0,)), ((), ()))
F32 = jnp.float32
BF16 = jnp.bfloat16


def seg_starts(len_ref, segs, place):
    start = jnp.zeros_like(place)
    end = jnp.int32(0)
    for k in range(segs - 1):
        end = end + len_ref[k]
        start = jnp.where(place >= end, end, start)
    return start


def head_part(block, h, heads):
    if heads == 1:
        return block
    lane = lax.broadcasted_iota(jnp.int32, block.shape, 1)
    return jnp.where((lane >= h * HEAD) & (lane < (h + 1) * HEAD), block, jnp.zeros_like(block))


def forward_kernel(heads, block, segs, len_ref, qkv_ref, o_ref, lse_ref, vt_ref):
    hd = heads * HEAD
    steps = qkv_ref.shape[0] // block

    def flip(i, _):
        at = pl.multiple_of(i * block, block)
        vt_ref[:, pl.ds(at, block)] = qkv_ref[pl.ds(at, block), 2 * hd : 3 * hd].T
        return 0

    lax.fori_loop(0, steps, flip, 0)
    key_rows = lax.broadcasted_iota(jnp.int32, (block, block), 0)

    def query_step(i, _):
        r0 = pl.multiple_of(i * block, block)
        q = qkv_ref[pl.ds(r0, block), 0:hd] * jnp.asarray(HEAD**-0.5, BF16)
        qs = [head_part(q, h, heads) for h in range(heads)]
        place = r0 + lax.broadcasted_iota(jnp.int32, (1, block), 1)
        start = seg_starts(len_ref, segs, place)
        first = seg_starts(len_ref, segs, r0) // block

        def key_step(j, carry):
            c0 = pl.multiple_of(j * block, block)
            kb = qkv_ref[pl.ds(c0, block), hd : 2 * hd]
            key_pos = key_rows + c0
            ok = (key_pos >= start) & (key_pos <= place)
            out = []
            for h in range(heads):
                top, total, acc = carry[3 * h : 3 * h + 3]
                s = lax.dot_general(kb, qs[h], NT, preferred_element_type=F32)
                s = jnp.where(ok, s, -1e30)
                new = jnp.maximum(top, jnp.max(s, axis=0, keepdims=True))
                p = jnp.exp(s - new)
                shrink = jnp.exp(top - new)
                total = total * shrink + jnp.sum(p, axis=0, keepdims=True)
                vt = vt_ref[h * HEAD : (h + 1) * HEAD, pl.ds(c0, block)]
                acc = acc * shrink + jnp.dot(vt, p.astype(BF16), preferred_element_type=F32)
                out += [new, total, acc]
            return tuple(out)

        init = (
            jnp.full((1, block), -1e30, F32),
            jnp.zeros((1, block), F32),
            jnp.zeros((HEAD, block), F32),
        ) * heads
        res = lax.fori_loop(first, i + 1, key_step, init)
        flat = jnp.concatenate([res[3 * h + 2] / res[3 * h + 1] for h in range(heads)], axis=0)
        o_ref[pl.ds(r0, block), :] = flat.T.astype(BF16)
        for h in range(heads):
            lse_ref[h : h + 1, pl.ds(r0, block)] = res[3 * h] + jnp.log(res[3 * h + 1])
        return 0

    lax.fori_loop(0, steps, query_step, 0)


def backward_kernel(heads, h, block, segs, len_ref, qkv_ref, o_ref, lse_ref, do_ref, *rest):
    before_ref = rest[0] if h else None
    d_ref, kt_ref, dq_ref, dk_ref, dv_ref = rest[-5:]
    hd = heads * HEAD
    steps = qkv_ref.shape[0] // block
    mine = slice(h * HEAD, (h + 1) * HEAD)

    def flip(i, _):
        at = pl.multiple_of(i * block, block)
        kt_ref[:, pl.ds(at, block)] = qkv_ref[pl.ds(at, block), hd : 2 * hd].T[mine]
        dk_ref[pl.ds(at, block), :] = jnp.zeros((block, hd), F32)
        dv_ref[pl.ds(at, block), :] = jnp.zeros((block, hd), F32)
        return 0

    lax.fori_loop(0, steps, flip, 0)
    key_rows = lax.broadcasted_iota(jnp.int32, (block, block), 0)

    def query_step(i, _):
        r0 = pl.multiple_of(i * block, block)
        q = qkv_ref[pl.ds(r0, block), 0:hd] * jnp.asarray(HEAD**-0.5, BF16)
        q = head_part(q, h, heads)
        do = head_part(do_ref[pl.ds(r0, block), :], h, heads)
        both = (do.astype(F32) * o_ref[pl.ds(r0, block), :].astype(F32)).T
        delta = jnp.sum(both[mine], axis=0, keepdims=True)
        lse = lse_ref[h : h + 1, pl.ds(r0, block)]
        place = r0 + lax.broadcasted_iota(jnp.int32, (1, block), 1)
        start = seg_starts(len_ref, segs, place)
        first = seg_starts(len_ref, segs, r0) // block

        def key_step(j, dq):
            c0 = pl.multiple_of(j * block, block)
            kb = qkv_ref[pl.ds(c0, block), hd : 2 * hd]
            vb = qkv_ref[pl.ds(c0, block), 2 * hd : 3 * hd]
            key_pos = key_rows + c0
            ok = (key_pos >= start) & (key_pos <= place)
            s = lax.dot_general(kb, q, NT, preferred_element_type=F32)
            p = jnp.where(ok, jnp.exp(s - lse), 0.0)
            dp = lax.dot_general(vb, do, NT, preferred_element_type=F32)
            ds = (p * (dp - delta)).astype(BF16)
            dv_ref[pl.ds(c0, block), :] += jnp.dot(p.astype(BF16), do, preferred_element_type=F32)
            dk_ref[pl.ds(c0, block), :] += jnp.dot(ds, q, preferred_element_type=F32)
            return dq + jnp.dot(kt_ref[:, pl.ds(c0, block)], ds, preferred_element_type=F32)

        dq = lax.fori_loop(first, i + 1, key_step, jnp.zeros((HEAD, block), F32))
        dq_ref[pl.ds(r0, block), :] = (dq * HEAD**-0.5).T
        return 0

    lax.fori_loop(0, steps, query_step, 0)

    def finish(i, _):
        at = pl.multiple_of(i * block, block)
        rows = pl.ds(at, block)
        d = [dq_ref[rows, :], dk_ref[rows, mine], dv_ref[rows, mine]]
        d = jnp.concatenate(d, axis=1).astype(BF16)
        if before_ref is not None:
            d = jnp.concatenate([before_ref[rows, :], d], axis=1)
        d_ref[rows, :] = d
        return 0

    lax.fori_loop(0, steps, finish, 0)


def takes(us):
    return pl.CostEstimate(flops=int(us * 1.1e9), bytes_accessed=1 << 20, transcendentals=0)


VM = pl.BlockSpec(memory_space=pltpu.VMEM)
SM = pl.BlockSpec(memory_space=pltpu.SMEM)
LIMIT = 40 << 20


def attention_forward(row, qkv, block):
    rows, wide = qkv.shape
    hd = wide // 3
    heads = hd // HEAD
    return pl.pallas_call(
        functools.partial(forward_kernel, heads, block, row.shape[0]),
        out_shape=(
            jax.ShapeDtypeStruct((rows, hd), BF16),
            jax.ShapeDtypeStruct((heads, rows), F32),
        ),
        in_specs=[SM, VM],
        out_specs=(VM, VM),
        scratch_shapes=[pltpu.VMEM((hd, rows), BF16)],
        compiler_params=pltpu.CompilerParams(vmem_limit_bytes=LIMIT),
        cost_estimate=takes(22),
        name="attention_forward",
    )(row, qkv)


def attention_backward(row, qkv, o, lse, do, block, h, before=()):
    rows, wide = qkv.shape
    hd = wide // 3
    heads = hd // HEAD
    return pl.pallas_call(
        functools.partial(backward_kernel, heads, h, block, row.shape[0]),
        out_shape=jax.ShapeDtypeStruct((rows, (h + 1) * 3 * HEAD), BF16),
        in_specs=[SM] + [VM] * (4 + len(before)),
        out_specs=VM,
        scratch_shapes=[
            pltpu.VMEM((HEAD, rows), BF16),
            pltpu.VMEM((rows, HEAD), F32),
            pltpu.VMEM((rows, hd), F32),
            pltpu.VMEM((rows, hd), F32),
        ],
        compiler_params=pltpu.CompilerParams(vmem_limit_bytes=LIMIT),
        cost_estimate=takes(16),
        name="attention_backward",
    )(row, qkv, o, lse, do, *before)


def tier_bounds(n):
    bounds = [(0, 1)]
    while bounds[-1][1] < n:
        bounds.append((bounds[-1][1], 2 * bounds[-1][1]))
    return bounds


def norm_parts(value):
    mean = jnp.mean(value, axis=-1, keepdims=True)
    centred = value - mean
    spread = jnp.mean(centred * centred, axis=-1, keepdims=True)
    scale = lax.rsqrt(spread + 1e-05)
    return centred * scale, scale


def project_kernel(at_ref, x_ref, gain_ref, shift_ref, w_ref, b_ref, *rest):
    x_out, qkv_out = rest[-2:]
    x = x_ref[...]
    n, _ = norm_parts(x.astype(F32))
    low = (n * gain_ref[...] + shift_ref[...]).astype(BF16)
    mixed = jnp.dot(low, w_ref[...], preferred_element_type=F32) + b_ref[...]
    x_out[...] = x
    qkv_out[...] = mixed.astype(BF16)


def project(at, x, gain, shift, w, b, total, held):
    rows, width = x.shape
    wide = w.shape[1]

    def fixed(shape):
        return pl.BlockSpec(shape, lambda i, at: (0, 0))

    given = () if held is None else held
    return pl.pallas_call(
        project_kernel,
        grid_spec=pltpu.PrefetchScalarGridSpec(
            num_scalar_prefetch=1,
            grid=(1,),
            in_specs=[
                fixed((rows, width)),
                fixed((1, width)),
                fixed((1, width)),
                fixed((width, wide)),
                fixed((1, wide)),
            ]
            + [pl.BlockSpec(memory_space=pl.ANY)] * len(given),
            out_specs=[
                pl.BlockSpec((rows, width), lambda i, at: (at[0], 0)),
                pl.BlockSpec((rows, wide), lambda i, at: (at[0], 0)),
            ],
        ),
        out_shape=(
            jax.ShapeDtypeStruct((total, width), BF16),
            jax.ShapeDtypeStruct((total, wide), BF16),
        ),
        input_output_aliases={6: 0, 7: 1} if given else {},
        cost_estimate=takes(2),
        compiler_params=pltpu.CompilerParams(vmem_limit_bytes=24 << 20),
        name="project",
    )(at.reshape(1), x, gain, shift, w, b, *given)


def attend_out_kernel(
    count_ref,
    merged_ref,
    x_ref,
    wout_ref,
    bout_ref,
    gain_ref,
    shift_ref,
    low_ref,
    middle_ref,
    stat_ref,
):
    rows = x_ref.shape[0]
    merged = jnp.concatenate([merged_ref[k] for k in range(merged_ref.shape[0])], axis=1)
    attn = jnp.dot(merged, wout_ref[...], preferred_element_type=F32) + bout_ref[...]
    middle = x_ref[...].astype(F32) + attn
    middle_ref[...] = middle
    n, _ = norm_parts(middle)
    low_ref[...] = (n * gain_ref[...] + shift_ref[...]).astype(BF16)
    valid = lax.broadcasted_iota(jnp.int32, (rows, 1), 0) < count_ref[0]
    stat_ref[...] = jnp.sum(jnp.where(valid, attn * attn, 0.0), axis=0, keepdims=True)


def attend_out(count, merged, x, wout, bout, gain, shift):
    rows, width = x.shape
    return pl.pallas_call(
        attend_out_kernel,
        in_specs=[SM] + [VM] * 6,
        out_specs=(VM,) * 3,
        out_shape=(
            jax.ShapeDtypeStruct((rows, width), BF16),
            jax.ShapeDtypeStruct((rows, width), F32),
            jax.ShapeDtypeStruct((1, width), F32),
        ),
        cost_estimate=takes(5),
        compiler_params=pltpu.CompilerParams(vmem_limit_bytes=40 << 20),
        name="attend_out",
    )(count, merged, x, wout, bout, gain, shift)


GELU = 0.7978845608028654


def feed_kernel(n_fsdp, rel_ref, count_ref, bfc_ref, wproj_ref, wfc_ref, *rest):
    low_refs, rest = rest[:n_fsdp], rest[n_fsdp:]
    dy_refs, rest = rest[:n_fsdp], rest[n_fsdp:]
    tiers = tier_bounds(n_fsdp)
    dtwo_refs, rest = rest[: len(tiers)], rest[len(tiers) :]
    hidden_ref, di_ref, dmlp_ref, low_s = rest
    step = pl.program_id(0)
    rows = low_s.shape[0]
    valid = lax.broadcasted_iota(jnp.int32, (rows, 1), 0) < count_ref[step]

    for k in range(n_fsdp):

        @pl.when(step == k)
        def _():
            low_s[...] = low_refs[k][...]
            dy = dy_refs[k][...]
            dmlp_ref[...] = jnp.where(valid, dy, jnp.zeros_like(dy))

    u = jnp.dot(low_s[...], wfc_ref[...], preferred_element_type=F32) + bfc_ref[...]
    dh = lax.dot_general(dmlp_ref[...], wproj_ref[...], NT, preferred_element_type=F32)
    square = u * u
    t = jnp.tanh(GELU * u * (1.0 + 0.044715 * square))
    side = 0.5 * (1.0 + t)
    hidden_ref[...] = (u * side).astype(BF16)
    slope = side + 0.5 * u * (1.0 - t * t) * (GELU * (1.0 + 3 * 0.044715 * square))
    di = (dh * slope).astype(BF16)
    di_ref[...] = di
    dtwo = lax.dot_general(di, wfc_ref[...], NT, preferred_element_type=F32)
    for (lo, hi), out_ref in zip(tiers, dtwo_refs):

        @pl.when((step >= lo) & (step < hi))
        def _():
            out_ref[...] = dtwo.astype(out_ref.dtype)


def feed(rel, counts, low_pieces, dy_pieces, wfc, wproj, bfc):
    rows, width = low_pieces[0].shape
    n_fsdp = len(low_pieces)
    wide = wproj.shape[0]
    tiers = tier_bounds(n_fsdp)

    def whole(*shape):
        return pl.BlockSpec(shape, lambda g, *_: (0,) * len(shape), pipeline_mode=pl.Buffered(1))

    def tier(lo, hi):
        return pl.BlockSpec((rows, width), lambda g, *_: (jnp.clip(g - lo, 0, hi - lo - 1), 0))

    each = pl.BlockSpec((rows, wide), lambda g, *_: (g, 0))
    return pl.pallas_call(
        functools.partial(feed_kernel, n_fsdp),
        grid_spec=pltpu.PrefetchScalarGridSpec(
            num_scalar_prefetch=2,
            grid=(n_fsdp,),
            in_specs=[
                whole(1, wide),
                whole(wide, width),
                pl.BlockSpec(
                    (width, wide), lambda g, rel, _: (0, rel[0]), pipeline_mode=pl.Buffered(1)
                ),
            ]
            + [whole(rows, width)] * (2 * n_fsdp),
            out_specs=[tier(lo, hi) for lo, hi in tiers]
            + [each, each, pl.BlockSpec((rows, width), lambda g, *_: (g, 0))],
            scratch_shapes=[pltpu.VMEM((rows, width), BF16)],
        ),
        out_shape=tuple(
            [
                jax.ShapeDtypeStruct(((hi - lo) * rows, width), F32 if lo == 0 else BF16)
                for lo, hi in tiers
            ]
            + [jax.ShapeDtypeStruct((n_fsdp * rows, wide), BF16)] * 2
            + [jax.ShapeDtypeStruct((n_fsdp * rows, width), BF16)]
        ),
        cost_estimate=takes(20),
        compiler_params=pltpu.CompilerParams(vmem_limit_bytes=52 << 20),
        name="feed",
    )(rel, counts, bfc, wproj, wfc, *low_pieces, *dy_pieces)


def feed_grads_kernel(n_fsdp, hidden_ref, di_ref, dmlp_ref, wproj_ref, *rest):
    low_refs, rest = rest[:n_fsdp], rest[n_fsdp:]
    tiers = tier_bounds(n_fsdp)
    mlp_refs, rest = rest[: len(tiers)], rest[len(tiers) :]
    gproj_ref, gfc_ref, gbfc_ref = rest[:3]
    scratch = rest[3:]
    step = pl.program_id(0)
    rows, wide = hidden_ref.shape
    n_seq, _, thin, _ = gfc_ref.shape
    width = dmlp_ref.shape[1]
    share = width // n_fsdp

    hidden = hidden_ref[...]
    di = di_ref[...]
    mlp = jnp.dot(hidden, wproj_ref[...], preferred_element_type=F32)
    for (lo, hi), out_ref in zip(tiers, mlp_refs):

        @pl.when((step >= lo) & (step < hi))
        def _():
            out_ref[...] = mlp.astype(out_ref.dtype)

    sums = jnp.sum(di.astype(F32), axis=0, keepdims=True)

    @pl.when(step == 0)
    def _():
        gbfc_ref[...] = sums

    @pl.when(step > 0)
    def _():
        gbfc_ref[...] += sums

    def store_fc(i, g):
        for k in range(n_seq):
            gfc_ref[k, i] = g[k * thin : (k + 1) * thin]

    if len(scratch) == 3:
        low_s, proj_s, fc_s = scratch

        @pl.when(step == 0)
        def _():
            proj_s[...] = jnp.zeros_like(proj_s)
            fc_s[...] = jnp.zeros_like(fc_s)

        for k in range(n_fsdp):

            @pl.when(step == k)
            def _():
                low_s[...] = low_refs[k][...]

        proj_s[...] += jnp.dot(hidden.T, dmlp_ref[...], preferred_element_type=F32)
        fc_s[...] += jnp.dot(low_s[...].T, di, preferred_element_type=F32)

        @pl.when(step == n_fsdp - 1)
        def _():
            gproj_ref[...] = proj_s[...].astype(BF16)
            for i in range(n_fsdp):
                store_fc(i, fc_s[i * share : (i + 1) * share, :].astype(BF16))

        return

    hiddent_s, di_s, dmlp_s, lowt_s = scratch
    for k in range(n_fsdp):

        @pl.when(step == k)
        def _():
            at = slice(k * rows, (k + 1) * rows)
            hiddent_s[:, at] = hidden.T
            di_s[at, :] = di
            dmlp_s[at, :] = dmlp_ref[...]
            lowt_s[:, at] = low_refs[k][...].T

    @pl.when(step == n_fsdp - 1)
    def _():
        tile = min(256, wide)

        def proj_tile(i, _):
            at = pl.multiple_of(i * tile, tile)
            g = jnp.dot(hiddent_s[pl.ds(at, tile), :], dmlp_s[...], preferred_element_type=F32)
            gproj_ref[pl.ds(at, tile), :] = g.astype(BF16)
            return 0

        lax.fori_loop(0, wide // tile, proj_tile, 0)

        def fc_tile(i, _):
            at = pl.multiple_of(i * share, share)
            g = jnp.dot(lowt_s[pl.ds(at, share), :], di_s[...], preferred_element_type=F32)
            store_fc(i, g.astype(BF16))
            return 0

        lax.fori_loop(0, n_fsdp, fc_tile, 0)


def feed_grads(hidden, di, dmlp, wproj, low_pieces, n_seq):
    rows, width = low_pieces[0].shape
    n_fsdp = len(low_pieces)
    wide = wproj.shape[0]
    total = n_fsdp * rows
    thin = width // n_fsdp // n_seq
    tiers = tier_bounds(n_fsdp)
    if total > 2048:
        scratch = [pltpu.VMEM((rows, width), BF16)]
        scratch += [pltpu.VMEM((wide, width), F32), pltpu.VMEM((width, wide), F32)]
    else:
        scratch = [pltpu.VMEM((wide, total), BF16), pltpu.VMEM((total, wide), BF16)]
        scratch += [pltpu.VMEM((total, width), BF16), pltpu.VMEM((width, total), BF16)]

    def whole(*shape):
        return pl.BlockSpec(shape, lambda g: (0,) * len(shape), pipeline_mode=pl.Buffered(1))

    def last(*shape):
        return pl.BlockSpec(shape, lambda g: (0,) * len(shape))

    def tier(lo, hi):
        return pl.BlockSpec((rows, width), lambda g: (jnp.clip(g - lo, 0, hi - lo - 1), 0))

    each = pl.BlockSpec((rows, wide), lambda g: (g, 0))
    return pl.pallas_call(
        functools.partial(feed_grads_kernel, n_fsdp),
        grid=(n_fsdp,),
        in_specs=[each, each, pl.BlockSpec((rows, width), lambda g: (g, 0)), whole(wide, width)]
        + [whole(rows, width)] * n_fsdp,
        out_specs=[tier(lo, hi) for lo, hi in tiers]
        + [last(wide, width), last(n_seq, n_fsdp, thin, wide), last(1, wide)],
        out_shape=tuple(
            [
                jax.ShapeDtypeStruct(((hi - lo) * rows, width), F32 if lo == 0 else BF16)
                for lo, hi in tiers
            ]
            + [
                jax.ShapeDtypeStruct((wide, width), BF16),
                jax.ShapeDtypeStruct((n_seq, n_fsdp, thin, wide), BF16),
                jax.ShapeDtypeStruct((1, wide), F32),
            ]
        ),
        scratch_shapes=scratch,
        cost_estimate=takes(18),
        compiler_params=pltpu.CompilerParams(vmem_limit_bytes=52 << 20),
        name="feed_grads",
    )(hidden, di, dmlp, wproj, *low_pieces)


def middle_back_kernel(
    n_fsdp,
    terms,
    count_ref,
    merged_ref,
    middle_ref,
    dy_ref,
    gain_ref,
    wout_ref,
    later_ref,
    *rest,
):
    term_refs, rest = rest[:terms], rest[terms:]
    gout_ref, d_middle_ref, d_merged_ref, vec_ref, passed_ref = rest
    passed_ref[...] = later_ref[...]
    n_seq, rows, hd = merged_ref.shape
    thin = gout_ref.shape[2]
    valid = lax.broadcasted_iota(jnp.int32, (rows, 1), 0) < count_ref[0]
    n, scale = norm_parts(middle_ref[...])
    d_two = functools.reduce(jnp.add, [ref[...].astype(F32) for ref in term_refs])
    d_result = jnp.where(valid, dy_ref[...].astype(F32), 0.0)
    e = d_two * gain_ref[...]
    d_middle = d_result + scale * (
        e - jnp.mean(e, axis=-1, keepdims=True) - n * jnp.mean(e * n, axis=-1, keepdims=True)
    )
    d_middle_ref[...] = d_middle
    d_attn = d_middle.astype(BF16)
    d_merged = lax.dot_general(d_attn, wout_ref[...], NT, preferred_element_type=F32).astype(BF16)
    for k in range(n_seq):
        d_merged_ref[k] = d_merged[:, k * hd : (k + 1) * hd]
    vec_ref[0:1, :] = jnp.sum(d_attn.astype(F32), axis=0, keepdims=True)
    vec_ref[1:2, :] = jnp.sum(d_two * n, axis=0, keepdims=True)
    vec_ref[2:3, :] = jnp.sum(d_two, axis=0, keepdims=True)
    vec_ref[3:4, :] = jnp.sum(d_result, axis=0, keepdims=True)
    merged = jnp.concatenate([merged_ref[k] for k in range(n_seq)], axis=1)
    gout = jnp.dot(merged.T, d_attn, preferred_element_type=F32).astype(BF16)
    for f in range(n_fsdp):
        for k in range(n_seq):
            at = (f * n_seq + k) * thin
            gout_ref[k, f] = gout[at : at + thin]


def middle_back(n_fsdp, count, merged, middle, dy, gain, wout, later, terms):
    rows, width = middle.shape
    n_seq = merged.shape[0]
    thin = width // n_fsdp // n_seq
    return pl.pallas_call(
        functools.partial(middle_back_kernel, n_fsdp, len(terms)),
        in_specs=[SM] + [VM] * (6 + len(terms)),
        out_specs=(VM,) * 5,
        out_shape=(
            jax.ShapeDtypeStruct((n_seq, n_fsdp, thin, width), BF16),
            jax.ShapeDtypeStruct((rows, width), F32),
            jax.ShapeDtypeStruct(merged.shape, BF16),
            jax.ShapeDtypeStruct((4, width), F32),
            jax.ShapeDtypeStruct(later.shape, BF16),
        ),
        cost_estimate=takes(7),
        compiler_params=pltpu.CompilerParams(vmem_limit_bytes=48 << 20),
        name="middle_back",
    )(count, merged, middle, dy, gain, wout, later, *terms)


def finish_kernel(count_ref, middle_ref, bproj_ref, *rest):
    term_refs, output_ref, stat_ref = rest[:-2], rest[-2], rest[-1]
    rows = middle_ref.shape[0]
    valid = lax.broadcasted_iota(jnp.int32, (rows, 1), 0) < count_ref[0]
    branch = functools.reduce(jnp.add, [ref[...].astype(F32) for ref in term_refs])
    branch = branch + bproj_ref[...]
    result = middle_ref[...] + branch
    output_ref[...] = jnp.where(valid, result, 0.0).astype(BF16)
    stat_ref[0:1, :] = jnp.sum(jnp.where(valid, result * result, 0.0), axis=0, keepdims=True)
    stat_ref[1:2, :] = jnp.sum(jnp.where(valid, branch * branch, 0.0), axis=0, keepdims=True)


def finish(count, middle, bproj, terms):
    rows, width = middle.shape
    return pl.pallas_call(
        finish_kernel,
        in_specs=[SM] + [VM] * (2 + len(terms)),
        out_specs=(VM,) * 2,
        out_shape=(
            jax.ShapeDtypeStruct((rows, width), BF16),
            jax.ShapeDtypeStruct((2, width), F32),
        ),
        cost_estimate=takes(3),
        compiler_params=pltpu.CompilerParams(vmem_limit_bytes=32 << 20),
        name="finish",
    )(count, middle, bproj, *terms)


def qkv_grad_kernel(x_ref, d_ref, w_ref, gain_ref, shift_ref, g_ref, vec_ref, sum_ref, acc):
    step = pl.program_id(0)
    n, _ = norm_parts(x_ref[...].astype(F32))
    low = (n * gain_ref[...] + shift_ref[...]).astype(BF16)
    d = d_ref[...]
    part = lax.dot_general(d, w_ref[...], NT, preferred_element_type=F32)
    gain_part = jnp.sum(part * n, axis=0, keepdims=True)
    shift_part = jnp.sum(part, axis=0, keepdims=True)
    sum_part = jnp.sum(d.astype(F32), axis=0, keepdims=True)
    g = jnp.dot(low.T, d, preferred_element_type=F32)

    @pl.when(step == 0)
    def _():
        acc[...] = g
        vec_ref[0:1, :] = gain_part
        vec_ref[1:2, :] = shift_part
        sum_ref[...] = sum_part

    @pl.when(step > 0)
    def _():
        acc[...] += g
        vec_ref[0:1, :] += gain_part
        vec_ref[1:2, :] += shift_part
        sum_ref[...] += sum_part

    @pl.when(step == pl.num_programs(0) - 1)
    def _():
        g_ref[...] = acc[...].astype(BF16)


def qkv_grads(x_all, d_own, w_own, gain, shift, block):
    total, width = x_all.shape
    wide = w_own.shape[1]

    def whole(*shape):
        return pl.BlockSpec(shape, lambda g: (0,) * len(shape))

    return pl.pallas_call(
        qkv_grad_kernel,
        grid=(total // block,),
        in_specs=[
            pl.BlockSpec((block, width), lambda g: (g, 0)),
            pl.BlockSpec((block, wide), lambda g: (g, 0)),
            whole(width, wide),
            whole(1, width),
            whole(1, width),
        ],
        out_specs=[whole(width, wide), whole(2, width), whole(1, wide)],
        out_shape=(
            jax.ShapeDtypeStruct((width, wide), BF16),
            jax.ShapeDtypeStruct((2, width), F32),
            jax.ShapeDtypeStruct((1, wide), F32),
        ),
        scratch_shapes=[pltpu.VMEM((width, wide), F32)],
        cost_estimate=takes(13),
        compiler_params=pltpu.CompilerParams(vmem_limit_bytes=40 << 20),
        name="qkv_grads",
    )(x_all, d_own, w_own, gain, shift)


def input_grad_kernel(d_ref, x_ref, gain_ref, d_middle_ref, w_ref, out_ref, d_s, one_s):
    step = pl.program_id(0)
    steps, _, share = one_s.shape

    @pl.when(step == 0)
    def _():
        d_s[...] = jnp.concatenate([d_ref[k] for k in range(d_ref.shape[0])], axis=1)

    one_s[step] = lax.dot_general(d_s[...], w_ref[...], NT, preferred_element_type=F32)

    @pl.when(step == steps - 1)
    def _():
        n, scale = norm_parts(x_ref[...].astype(F32))
        d_one = jnp.concatenate([one_s[k] for k in range(steps)], axis=1)
        e = d_one * gain_ref[...]
        out_ref[...] = d_middle_ref[...] + scale * (
            e - jnp.mean(e, axis=-1, keepdims=True) - n * jnp.mean(e * n, axis=-1, keepdims=True)
        )


def input_gradient(d_packed, w_all, x, gain, d_middle):
    rows, width = x.shape
    n_seq, _, each = d_packed.shape
    wide = w_all.shape[1]
    steps = 4

    def whole(*shape):
        return pl.BlockSpec(shape, lambda g: (0,) * len(shape), pipeline_mode=pl.Buffered(1))

    return pl.pallas_call(
        input_grad_kernel,
        grid=(steps,),
        in_specs=[
            whole(n_seq, rows, each),
            whole(rows, width),
            whole(1, width),
            whole(rows, width),
            pl.BlockSpec((width // steps, wide), lambda g: (g, 0)),
        ],
        out_specs=whole(rows, width),
        out_shape=jax.ShapeDtypeStruct((rows, width), F32),
        scratch_shapes=[
            pltpu.VMEM((rows, wide), BF16),
            pltpu.VMEM((steps, rows, width // steps), F32),
        ],
        cost_estimate=takes(8),
        compiler_params=pltpu.CompilerParams(vmem_limit_bytes=40 << 20),
        name="input_gradient",
    )(d_packed, x, gain, d_middle, w_all)


def place_kernel(layout, count, order_ref, rel_ref, *refs):
    outs = refs[len(refs) - len(layout) :]
    step = pl.program_id(0)
    for k in range(count):

        @pl.when(step == k)
        def _():
            thin = refs[k].shape[0]
            at = 0
            for (kind, wide, blocks), out in zip(layout, outs):
                each = wide // blocks
                for a in range(blocks):
                    part = refs[k][:, at : at + each].astype(F32)
                    at += each
                    if kind == "rel":
                        lanes = pl.ds(pl.multiple_of(rel_ref[a] * each, each), each)
                        out[0, :, lanes] = part
                    elif len(out.shape) == 3:
                        out[0, a * thin : (a + 1) * thin, :] = part
                    else:
                        out[a * thin : (a + 1) * thin, :] = part


def place(order, rel, pieces, layout, n, held=None):
    thin = pieces[0].shape[0]
    shapes = []
    specs = []
    for kind, wide, blocks in layout:
        each = wide // blocks
        if kind == "cols" and each % 128 == 0:
            shapes.append((blocks * thin, n * each))
            specs.append(pl.BlockSpec((blocks * thin, each), lambda g, order, _: (0, order[g])))
            continue
        size = (thin, wide) if kind == "rel" else (blocks * thin, each)
        shapes.append((n,) + size)
        specs.append(pl.BlockSpec((1,) + size, lambda g, order, _: (order[g], 0, 0)))
    given = () if held is None else tuple(held)
    first = 2 + len(pieces)
    return pl.pallas_call(
        functools.partial(place_kernel, layout, len(pieces)),
        grid_spec=pltpu.PrefetchScalarGridSpec(
            num_scalar_prefetch=2,
            grid=(len(pieces),),
            in_specs=[
                pl.BlockSpec(p.shape, lambda g, *_: (0, 0), pipeline_mode=pl.Buffered(1))
                for p in pieces
            ]
            + [pl.BlockSpec(memory_space=pl.ANY)] * len(given),
            out_specs=specs,
        ),
        out_shape=tuple(jax.ShapeDtypeStruct(shape, F32) for shape in shapes),
        input_output_aliases={first + k: k for k in range(len(given))},
        cost_estimate=takes(len(pieces)),
        compiler_params=pltpu.CompilerParams(vmem_limit_bytes=48 << 20),
        name="place",
    )(order, rel, *pieces, *given)


def flat_matrices(placed, layout):
    results = []
    for (kind, _, _), out in zip(layout, placed):
        if len(out.shape) == 3 and kind == "cols":
            out = out.transpose(1, 0, 2).reshape(out.shape[1], -1)
        elif len(out.shape) == 3:
            out = out.reshape(-1, out.shape[2])
        results.append(out)
    return results


class Ring:
    def __init__(self, axis):
        self.axis = axis
        self.n = n = lax.axis_size(axis)
        me = lax.axis_index(axis)
        self.pos = jnp.where(me % 2 == 0, me // 2, n - 1 - me // 2)
        order = list(range(0, n, 2)) + list(range(1, n, 2))[::-1]
        self.up = [(order[i], order[(i + 1) % n]) for i in range(n)]
        self.down = [(b, a) for a, b in self.up]
        self.walk = [0]
        for step in range(1, n // 2):
            self.walk += [-step, step]
        self.walk.append(n // 2)
        p = (self.pos + jnp.asarray(self.walk, jnp.int32) + n) % n
        self.order = jnp.where(p < n // 2, 2 * p, 2 * (n - 1 - p) + 1)

    def shard(self, distance):
        n = self.n
        p = (self.pos + distance + n) % n
        return jnp.where(p < n // 2, 2 * p, 2 * (n - 1 - p) + 1)

    def send_up(self, value):
        return lax.ppermute(value, self.axis, self.up)

    def send_down(self, value):
        return lax.ppermute(value, self.axis, self.down)

    def gather(self, value):
        half = value.shape[0] // 2
        above = below = value
        out = [value]
        for _ in range(1, self.n // 2):
            below, above = yield self.send_up(below), self.send_down(above)
            out += [below, above]
        return out + list((yield self.send_up(below[:half]), self.send_down(above[half:])))

    def reduce(self, *values):
        rows = values[0].shape[0] // self.n
        half = rows // 2
        mid = self.n // 2

        def term(distance, first=0, count=rows):
            at = self.shard(distance) * rows + first
            parts = [lax.dynamic_slice_in_dim(v, at, count, 0).astype(F32) for v in values]
            return parts[0] if len(parts) == 1 else jnp.concatenate(parts, axis=1)

        up = self.send_up(term(mid, 0, half).astype(BF16))
        down = self.send_down(term(mid, half, rows - half).astype(BF16))
        for step in range(mid - 1, 0, -1):
            up, down = yield up, down
            mine = term(step)
            other = term(-step)
            if step == mid - 1:
                mine = jnp.concatenate([mine[:half] + up.astype(F32), mine[half:]], axis=0)
                other = jnp.concatenate([other[:half], other[half:] + down.astype(F32)], axis=0)
            else:
                mine = mine + up.astype(F32)
                other = other + down.astype(F32)
            up = self.send_up(mine.astype(BF16))
            down = self.send_down(other.astype(BF16))
        up, down = yield up, down
        return (term(0) + up.astype(F32) + down.astype(F32)).astype(BF16)


class Walk:
    def __init__(self, steps):
        self.steps = steps
        self.result = None
        self.moving = next(steps)

    def go(self, arrived):
        try:
            self.moving = self.steps.send(arrived)
        except StopIteration as end:
            self.moving = None
            self.result = end.value


def milestone(*values):
    return lax.optimization_barrier(values)


def bits(n):
    return [1 << b for b in range(n.bit_length() - 1)]


def swap(value, axis, bit):
    n = lax.axis_size(axis)
    return lax.ppermute(value, axis, [(i, i ^ bit) for i in range(n)])


def reach(n):
    masks = [0]
    for bit in reversed(bits(n)):
        masks = masks + [m | bit for m in masks]
    return masks


def cube_gather(value, axis):
    held = [value]
    for bit in reversed(bits(lax.axis_size(axis))):
        held = held + [swap(block, axis, bit) for block in held]
    return held


class Scatter:
    def __init__(self, tiers, axis):
        self.axis = axis
        self.left = self.top = len(tiers) - 1
        self.size = tiers[0].shape[0]
        self.terms = [[t] for t in tiers]
        self.moving = None

    def send(self):
        parts = self.terms[self.left]
        away = parts[0] if len(parts) == 1 else add_up(parts).astype(BF16)
        self.moving = swap(away, self.axis, 1 << (self.top - self.left))

    def take(self):
        for j, (lo, hi) in enumerate(tier_bounds(1 << (self.left - 1))):
            self.terms[j].append(self.moving[lo * self.size : hi * self.size])
        self.left -= 1


def add_up(terms):
    return functools.reduce(jnp.add, [t.astype(F32) for t in terms])


def cube_exchange(value, axis, dim):
    me = lax.axis_index(axis)
    n = lax.axis_size(axis)
    size = value.shape[dim] // n
    out = []
    for mask in reach(n):
        block = lax.dynamic_slice_in_dim(value, (me ^ mask) * size, size, dim)
        if mask:
            block = lax.ppermute(block, axis, [(i, i ^ mask) for i in range(n)])
        out.append(block)
    return out


def shards(
    tokens,
    cotangent,
    lengths,
    deal,
    ln1_gain,
    ln1_shift,
    w_qkv,
    bias_qv,
    w_out,
    bias_out,
    ln2_gain,
    ln2_shift,
    w_fc,
    bias_fc,
    w_proj,
    bias_proj,
):
    x = tokens[0]
    dy = cotangent[0]
    rows, width = x.shape
    ring = Ring("seq")
    n_seq = ring.n
    n_fsdp = lax.axis_size("fsdp")
    me_seq = lax.axis_index("seq")
    me_fsdp = lax.axis_index("fsdp")
    total_rows = rows * n_seq
    heads = H // n_seq
    hd = heads * HEAD
    wide = w_fc.shape[1]
    share = w_qkv.shape[0]
    groups = jnp.arange(n_fsdp, dtype=jnp.int32)
    picked = (deal[:, None] == groups[None, :]).astype(jnp.int32)
    home_rows = jnp.sum(picked[:, :, None] * lengths[None], axis=1)
    row = jnp.sum(jnp.where((groups == me_fsdp)[:, None], home_rows, 0), axis=0)
    last = lengths.shape[1] - 1
    masks = reach(n_fsdp)
    rel = me_fsdp ^ jnp.asarray(masks, jnp.int32)

    own_cols = lax.dynamic_slice_in_dim(w_qkv, me_seq * 3 * hd, 3 * hd, 1)
    small = (ln1_gain, ln1_shift, bias_qv, bias_out, ln2_gain, ln2_shift, bias_proj)
    small = jnp.concatenate(small)
    extra = -(-small.shape[0] // (3 * hd * 16)) * 16
    tail = jnp.pad(small, (0, extra * 3 * hd - small.shape[0])).reshape(extra, 3 * hd)

    walk = Walk(ring.gather(x))
    moved, mine, w_out = milestone(walk.moving, (own_cols, tail), w_out)
    walk.go(moved)
    wout = lax.all_gather(w_out, "fsdp", axis=0, tiled=True)
    packs = [jnp.concatenate(mine, axis=0)]
    held = None
    for bit in reversed(bits(n_fsdp)):
        packs = packs + [swap(p, "fsdp", bit) for p in packs]

    def projected(blocks):
        nonlocal held
        for k in blocks:
            if k < n_seq - 1:
                at = ring.shard(ring.walk[k])
            else:
                at = ring.shard(n_seq // 2) * 2 + (k - n_seq + 1)
            held = project(
                at, pieces[k], gain_one, shift_one, w_roles, b_own, total_rows, held
            )

    moved_first = moved
    moved, packs, w_fc = milestone(walk.moving, packs, w_fc)
    walk.go(moved)
    wfc = lax.all_gather(w_fc, "fsdp", axis=0, tiled=True)

    w_own = jnp.zeros((width, 3 * hd), BF16)
    vectors = jnp.zeros((n_fsdp, tail.size), BF16)
    for k, p in enumerate(packs):
        index = me_fsdp ^ masks[k]
        w_own = lax.dynamic_update_slice_in_dim(w_own, p[:share], index * share, 0)
        vectors = lax.dynamic_update_slice_in_dim(vectors, p[share:].reshape(1, -1), index, 0)
    w_roles = w_own.reshape(width, heads, 3, HEAD).transpose(0, 2, 1, 3).reshape(width, 3 * hd)
    cut = []
    at = 0
    for count in (share, share, 2 * share, share, share, share, share):
        cut.append(vectors[:, at : at + count].reshape(1, -1).astype(F32))
        at += count
    gain_one, shift_one, bqv, bout, gain_two, shift_two, bproj = cut
    b_own = lax.dynamic_index_in_dim(bqv.reshape(n_seq, heads, 2, HEAD), me_seq, 0, keepdims=False)
    b_own = jnp.concatenate(
        [b_own[:, 0].reshape(1, hd), jnp.zeros((1, hd), F32), b_own[:, 1].reshape(1, hd)], axis=1
    )

    pieces = [x] + list(moved_first) + list(moved)
    done = 0
    while walk.result is None:
        ready = len(pieces)
        projected(range(done, ready))
        done = ready
        moved, held = milestone(walk.moving, held)
        walk.go(moved)
        pieces += list(moved)
    projected(range(done, len(pieces)))
    x_all, qkv = held

    attended, lse = attention_forward(row, qkv, rows)
    dy_first, attended = milestone(dy, attended)
    dy_pieces = cube_gather(dy_first, "fsdp")
    merged = lax.all_to_all(
        attended.reshape(n_seq, rows, hd), "seq", split_axis=0, concat_axis=0, tiled=True
    )
    merged, dy_pieces = milestone(merged, dy_pieces)

    ends = jnp.sum(home_rows[:, :last], axis=1)
    ends = jnp.sum(jnp.where(rel[:, None] == groups[None, :], ends[None, :], 0), axis=1)
    counts = jnp.clip(ends - me_seq * rows, 0, rows)
    low, middle, square_attn = attend_out(
        counts, merged, x, wout, bout, gain_two, shift_two
    )
    low_pieces = cube_gather(low, "fsdp")
    tiers = len(tier_bounds(n_fsdp))
    results = feed(
        rel, counts, low_pieces, dy_pieces, wfc, w_proj, bias_fc.astype(F32)[None]
    )
    d_two, (hidden, d_inner, d_mlp) = results[:tiers], results[tiers:]

    d_two = Scatter(d_two, "fsdp")
    while d_two.left > 1:
        d_two.send()
        d_two.moving, hidden = milestone(d_two.moving, hidden)
        d_two.take()
    d_two.send()
    results = feed_grads(hidden, d_inner, d_mlp, w_proj, low_pieces, n_seq)
    d_two.moving, results = milestone(d_two.moving, results)
    d_two.take()
    mlp, (gproj, gfc, gbfc) = results[:tiers], results[tiers:]
    gout, d_middle, d_merged, sums_two, w_qkv = middle_back(
        n_fsdp, counts, merged, middle, dy, gain_two, wout, w_qkv, d_two.terms[0]
    )
    w_all = lax.all_gather(w_qkv, "fsdp", axis=0, tiled=True)

    thin = share // n_seq
    blocks = wide // width
    gfc = gfc.reshape(n_seq * n_fsdp * thin, wide // n_fsdp)
    gout = gout.reshape(n_seq * n_fsdp * thin, width)
    d_merged, gproj, gfc, gout, mlp = milestone(d_merged, gproj, gfc, gout, mlp)
    d_heads = lax.all_to_all(d_merged, "seq", split_axis=0, concat_axis=0, tiled=True)
    together = gfc.shape[0] == gproj.shape[0]
    walk = Walk(ring.reduce(gproj, gfc, gout) if together else ring.reduce(gfc, gout))
    mlp = Scatter(mlp, "fsdp")
    while mlp.left > 1:
        mlp.send()
        mlp.moving, d_heads = milestone(mlp.moving, d_heads)
        mlp.take()
    mlp.send()
    moved, d_heads = milestone(walk.moving, d_heads)

    d_own = ()
    for h in range(heads):
        walk.go(moved)
        d_own = (
            attention_backward(
                row, qkv, attended, lse, d_heads.reshape(total_rows, hd), rows, h, d_own
            ),
        )
        moved, d_own, mlp.moving = milestone(walk.moving, d_own, mlp.moving)
    mlp.take()
    d_own = d_own[0]
    d_packed = lax.all_to_all(
        d_own.reshape(n_seq, rows, 3 * hd), "seq", split_axis=0, concat_axis=0, tiled=True
    )
    walk.go(moved)
    grad_qkv, sums_one, d_sums = qkv_grads(x_all, d_own, w_own, gain_one, shift_one, rows)
    while walk.result is None:
        moved, grad_qkv = milestone(walk.moving, grad_qkv)
        walk.go(moved)
    mine = walk.result
    if together:
        mine_proj, mine = mine[:, :width], mine[:, width:]
    else:
        walk = Walk(ring.reduce(gproj))
        while walk.result is None:
            walk.go(walk.moving)
        mine_proj = walk.result
    mine_proj = mine_proj.reshape(blocks, thin, width).transpose(1, 0, 2).reshape(thin, wide)
    mine = cube_exchange(mine, "fsdp", 0)
    parts = [
        lax.dynamic_slice_in_dim(grad_qkv, (me_fsdp ^ mask) * share, share, 0) for mask in masks
    ]
    parts = [jnp.concatenate(parts[lo:hi], axis=0) for lo, hi in tier_bounds(n_fsdp)]
    parts = Scatter(parts, "fsdp")
    while parts.left:
        parts.send()
        if parts.left > 1:
            parts.moving, mine = milestone(parts.moving, mine)
        parts.take()
    mine_fc = [m[:, : wide // n_fsdp] for m in mine]
    mine_out = add_up([m[:, wide // n_fsdp :] for m in mine]).astype(BF16)
    share_qkv = add_up(parts.terms[0]).astype(BF16)
    beside = share_qkv.reshape(n_seq, thin, 3 * hd).transpose(1, 0, 2).reshape(thin, -1)
    mine = jnp.concatenate([mine_proj] + mine_fc + [mine_out, beside], axis=1)

    mine, d_packed = milestone(mine, d_packed)
    walk = Walk(ring.gather(mine))
    output, square_ends = finish(counts, middle, bproj, mlp.terms[0])
    grad_bfc = lax.dynamic_update_slice_in_dim(
        jnp.zeros((n_fsdp, wide // n_fsdp), F32), gbfc, me_fsdp, 0
    )
    d_sums = d_sums.reshape(heads, 3, HEAD)
    d_sums = jnp.stack([d_sums[:, 0], d_sums[:, 2]], axis=1).reshape(1, 2 * hd)
    grad_bqv = lax.dynamic_update_slice_in_dim(
        jnp.zeros((n_seq, 2 * hd), F32), d_sums, me_seq, 0
    )
    squares = jnp.concatenate([square_ends[:1], square_attn, square_ends[1:]], axis=0)
    sums = jnp.concatenate(
        [
            sums_two.reshape(-1),
            grad_bfc.reshape(-1),
            jnp.sum(squares, axis=1),
            counts[:1].astype(F32),
            sums_one.reshape(-1),
            grad_bqv.reshape(-1),
        ]
    )
    hops = [(axis, bit) for axis in ("fsdp", "seq") for bit in bits(lax.axis_size(axis))]
    input_grad = None
    arrived = [mine]
    layout = (
        ("rows", wide, blocks),
        ("rel", wide, n_fsdp),
        ("rows", width, 1),
        ("cols", 3 * width, n_seq),
    )
    placed = None
    for step in range(n_seq // 2):
        count = -(-len(hops) // (n_seq // 2 - step))
        for axis, bit in hops[:count]:
            sums = sums + swap(sums, axis, bit)
        hops = hops[count:]
        if step == min(1, n_seq // 2 - 1):
            input_grad = input_gradient(d_packed, w_all, x, gain_one, d_middle)
        if step == n_seq // 2 - 1:
            placed = place(ring.order[: n_seq - 1], rel, arrived, layout, n_seq)
        moved, sums, output, input_grad, placed = milestone(
            walk.moving, sums, output, input_grad, placed
        )
        arrived += moved
        walk.go(moved)
    last_piece = [jnp.concatenate(walk.result[-2:], axis=0)]
    placed = place(ring.order[n_seq - 1 :], rel, last_piece, layout, n_seq, placed)
    grad_proj, grad_fc, grad_out, grad_wqkv = flat_matrices(placed, layout)

    def own_share(vector):
        count = vector.shape[0] // n_fsdp
        return lax.dynamic_slice_in_dim(vector, me_fsdp * count, count, 0)

    early = sums[: 4 * width + wide + 4]
    late = sums[4 * width + wide + 4 :]
    sum_bout, sum_g2, sum_s2, sum_bproj = [early[k * width : (k + 1) * width] for k in range(4)]
    sum_bfc = early[4 * width : 4 * width + wide]
    squared = early[4 * width + wide :]
    stats = jnp.sqrt(squared[:3] / (squared[3] * width))
    return (
        output[None],
        input_grad[None],
        own_share(late[:width]),
        own_share(late[width : 2 * width]),
        grad_wqkv,
        own_share(late[2 * width :]),
        grad_out,
        own_share(sum_bout),
        own_share(sum_g2),
        own_share(sum_s2),
        grad_fc,
        own_share(sum_bfc),
        grad_proj,
        own_share(sum_bproj),
        stats,
    )


def solution(mesh):
    rows_split = P("fsdp", "seq", None)
    matrix = P("fsdp", None)
    vector = P("fsdp")
    params = (
        vector,
        vector,
        matrix,
        vector,
        matrix,
        vector,
        vector,
        vector,
        matrix,
        vector,
        matrix,
        vector,
    )
    return jax.shard_map(
        shards,
        mesh=mesh,
        in_specs=(rows_split, rows_split, P(), P()) + params,
        out_specs=(rows_split, rows_split) + params + (P(),),
        check_vma=False,
    )
```

time: 724 us -> 468 us (0.65)
  local copies, waits for them, and re-layouts: 179 us -> 63.3 us
  Pallas kernels: 50.1 us -> 147 us
  waiting for transfers between devices: 253 us -> 159 us
  matrix products: 85.6 us -> 0 us
  starting transfers between devices: 98.6 us -> 60.9 us
  other arithmetic: 42.1 us -> 14.3 us
  between operations: 6.09 us -> 16.4 us
    pallas_call x1 -> x20, Pallas kernels: 28.5 us -> 124 us  [the longest x2 33.7 us: attention_backward(): pl.pallas_call(functools.partial(backward_kernel, heads, h, block, row.sh...]
    dot_general x30 -> x0, matrix products: 85.6 us -> none  [the longest x8 32.7 us: half(): return lax.dot_general(part, right, TN, preferred_element_type=F32)]
    ppermute x28 -> x12, waiting for transfers between devices: 78.9 us -> 14.5 us  [send_down(): return lax.ppermute(value, self.axis, self.down)]
    ppermute x33 -> x20, waiting for transfers between devices: 122 us -> 80.2 us  [swap(): return lax.ppermute(value, axis, [(i, i ^ bit) for i in range(n)])]
    dynamic_update_slice x34 -> x10, local copies, waits for them, and re-layouts: 38.9 us -> 1.45 us  [the longest x4 0.94 us: shards(): lax.dynamic_update_slice_in_dim(vectors, p[share:].reshape(1, -1), index, 0)]
    all_to_all x1 -> x2, waiting for transfers between devices: 0.01 us -> 26.6 us  [the longest x1 18.2 us: shards(): lax.all_to_all(d_own.reshape(n_seq, rows, 3 * hd), 'seq', split_axis=0, c...]
    convert_element_type x14 -> x1, local copies, waits for them, and re-layouts: 24.5 us -> 0.09 us  [shards(): cut.append(vectors[:, at:at + count].reshape(1, -1).astype(F32))]
    ppermute x28 -> x12, starting transfers between devices: 34.3 us -> 17 us  [send_up(): return lax.ppermute(value, self.axis, self.up)]
  transfers between devices with their start and end apart: 91 -> 53, of which waited for: 37 -> 27; matrix products, arithmetic and copies ran while one was open for 35% -> 8% of each run, Pallas kernels for 7% -> 25%
where the time goes in v2:
time: 468 us; the launch traced here: 460 us
  waiting for transfers between devices  159 us (34%)
  Pallas kernels  147 us (31%)
  local copies, waits for them, and re-layouts  63.3 us (14%)
  starting transfers between devices  60.9 us (13%)
  between operations  16.4 us (4%)
  other arithmetic  14.3 us (3%)
    ppermute x20, waiting for transfers between devices, swap(): return lax.ppermute(value, axis, [(i, i ^ bit) for i in range(n)])  80.2 us
    unnamed x144, local copies, waits for them, and re-layouts  41.3 us
    pallas_call x2, Pallas kernels, attention_backward(): pl.pallas_call(functools.partial(backward_kernel, heads, h, block, row.sh...  33.7 us
    ppermute x12, waiting for transfers between devices, send_up(): return lax.ppermute(value, self.axis, self.up)  31.9 us
    pallas_call x1, Pallas kernels, attention_forward(): pl.pallas_call(functools.partial(forward_kernel, heads, block, row.shape[...  22.5 us
    pallas_call x1, Pallas kernels, feed_grads(): pl.pallas_call(functools.partial(feed_grads_kernel, n_fsdp), grid=(n_fsdp...  21.3 us
    pallas_call x1, Pallas kernels, feed(): pl.pallas_call(functools.partial(feed_kernel, n_fsdp), grid_spec=pltpu.Pr...  18.8 us
    all_to_all x1, waiting for transfers between devices, shards(): lax.all_to_all(d_own.reshape(n_seq, rows, 3 * hd), 'seq', split_axis=0, c...  18.2 us
  transfers between devices with their start and end apart: 53, of which 27 were waited for; matrix products, arithmetic and copies ran while one was open for 8% of the time, Pallas kernels for 25%

profile of v2, /device:TPU:0, one launch (start us, length us, event | category | flops | bytes accessed | tf_op | source)
XLA Modules:
  0.0 460.2 jit_solution(12837949830817036618)
XLA Ops:
  17.1 10.9 %collective-permute-done.x_ref = bf16[384,1024]{1,0:T(8,128)(2,1)S(1)} collective-permute-done((bf16[384,1024]{1,0:T(8,128)(2,1)}, bf16[384,1024]{1,0:T(8,128)(2,1)S(1)}, u32[]{:S(2)}, u32[]{:S(2)}) %collective-permute-start) | collective-permute-done | bytes 786464 | tf_op jit(solution)/shard_map/ppermute | solution.py:817
  33.3 4.3 collective-permute-done.4
  39.1 8.7 %collective-permute-done.2.x_ref = bf16[384,1024]{1,0:T(8,128)(2,1)} collective-permute-done((bf16[384,1024]{1,0:T(8,128)(2,1)S(1)}, bf16[384,1024]{1,0:T(8,128)(2,1)}, u32[]{:S(2)}, u32[]{:S(2)}) %collective-permute-start.2) | collective-permute-done | bytes 786464 | tf_op jit(solution)/shard_map/ppermute | solution.py:817
  63.6 6.3 %collective-permute-done.7.x_ref = bf16[384,1024]{1,0:T(8,128)(2,1)S(1)} collective-permute-done((bf16[384,1024]{1,0:T(8,128)(2,1)}, bf16[384,1024]{1,0:T(8,128)(2,1)S(1)}, u32[]{:S(2)}, u32[]{:S(2)}) %collective-permute-start.7) | collective-permute-done | bytes 786464 | tf_op jit(solution)/shard_map/ppermute | solution.py:817
  84.5 22.5 %attention_forward.1 = (bf16[3072,128]{1,0:T(8,128)(2,1)}, f32[2,3072]{1,0:T(2,128)S(1)}) custom-call(s32[4]{0:T(128)S(1)} %select_reduce_fusion.len_ref, bf16[3072,384]{1,0:T(8,128)(2,1)S(1)} %get-tuple-element.191.qkv_ref), custom_call_target="tpu_custom_call" | custom-call | flops 24199999488 | bytes 1048576 | tf_op jit(solution)/shard_map/attention_forward/pallas_call | solution.py:163
  107.0 4.0 all-to-all-start
  111.0 16.6 %collective-permute-done.11.rest_5_ = bf16[384,1024]{1,0:T(8,128)(2,1)} collective-permute-done((bf16[384,1024]{1,0:T(8,128)(2,1)}, bf16[384,1024]{1,0:T(8,128)(2,1)}, u32[]{:S(2)}, u32[]{:S(2)}) %collective-permute-start.11) | collective-permute-done | bytes 786464 | tf_op jit(solution)/shard_map/ppermute | solution.py:883
  137.4 18.4 %collective-permute-done.14.rest_1_ = bf16[384,1024]{1,0:T(8,128)(2,1)S(1)} collective-permute-done((bf16[384,1024]{1,0:T(8,128)(2,1)S(1)}, bf16[384,1024]{1,0:T(8,128)(2,1)S(1)}, u32[]{:S(2)}, u32[]{:S(2)}) %collective-permute-start.14) | collective-permute-done | bytes 786464 | tf_op jit(solution)/shard_map/ppermute | solution.py:883
  159.3 18.8 %feed.1 = (f32[384,1024]{1,0:T(8,128)}, bf16[384,1024]{1,0:T(8,128)(2,1)S(1)}, bf16[768,1024]{1,0:T(8,128)(2,1)}, bf16[1536,1024]{1,0:T(8,128)(2,1)}, bf16[1536,...) custom-call(s32[4]{0:T(128)S(1)} %broadcast_xor_fusion.rel_ref, s32[4]{0:T(128)S(1)} %subtract_clamp_fusion.count_ref, ...), custom_call_target="tpu_custom_call" | custom-call | flops 22000001024 | bytes 1048576 | tf_op jit(solution)/shard_map/feed/pallas_call | solution.py:352
  184.8 21.3 %feed_grads.1 = (f32[384,1024]{1,0:T(8,128)}, bf16[384,1024]{1,0:T(8,128)(2,1)S(1)}, bf16[768,1024]{1,0:T(8,128)(2,1)}, bf16[1024,1024]{1,0:T(8,128)(2,1)}, bf16...) custom-call(bf16[1536,1024]{1,0:T(8,128)(2,1)} %get-tuple-element.209.hidden_ref, ...), custom_call_target="tpu_custom_call" | custom-call | flops 19800000512 | bytes 1048576 | tf_op jit(solution)/shard_map/feed_grads/pallas_call | solution.py:499
  207.6 8.4 %middle_back.1 = (bf16[8,4,32,1024]{3,2,1,0:T(8,128)(2,1)}, f32[384,1024]{1,0:T(8,128)S(1)}, bf16[8,384,128]{2,1,0:T(8,128)(2,1)S(1)}, f32[4,1024]{1,0:T(4,128)S(1)}, bf16[256,3072]{1,0:T(8,128)(2,1)}) custom-call(s32[4]{0:T(128)S(1)} %subtract_clamp_fusion.count_ref, bf16[8,384,128]{2,1,0:T(8,128)(2,1)S(1)} %all-to-all-done.merged_ref, ...), custom_call_target="tpu_custom_call" | custom-call | flops 7699999744 | bytes 1048576 | tf_op jit(solution)/shard_map/middle_back/pallas_call | solution.py:570
  218.1 5.8 %all-to-all-start.1 = ((bf16[8,384,128]{2,1,0:T(8,128)(2,1)}), bf16[8,384,128]{2,1,0:T(8,128)(2,1)S(1)}, u32[]{:S(2)}, u32[]{:S(2)}) async-start(bf16[8,384,128]{2,1,0:T(8,128)(2,1)} %copy-done.11), calls=%async_computation.1 | async-start | bytes 1572864 | tf_op jit(solution)/shard_map/all_to_all | solution.py:1077
  237.0 8.4 %all-to-all-done.1 = bf16[8,384,128]{2,1,0:T(8,128)(2,1)S(1)} async-done(((bf16[8,384,128]{2,1,0:T(8,128)(2,1)}), bf16[8,384,128]{2,1,0:T(8,128)(2,1)S(1)}, u32[]{:S(2)}, u32[]{:S(2)}) %all-to-all-start.1) | async-done | bytes 786464 | tf_op jit(solution)/shard_map/all_to_all | solution.py:1077
  256.3 16.4 %attention_backward.2.rest_0_ = bf16[3072,192]{1,0:T(8,128)(2,1)S(1)} custom-call(s32[4]{0:T(128)S(1)} %select_reduce_fusion.len_ref, bf16[3072,384]{1,0:T(8,128)(2,1)S(1)} %get-tuple-element.191.qkv_ref, bf16[3072,128]{1,0:T(8,128)(2,1)} %get-tuple-element.193.o_ref, f32[2,3072]{1,0:T(2,128)S(1)} %get-tuple-element.234.lse_ref, bf16[3072,128]{1,0:T(8,128)(2,1)S(1)} %bitcast.102), custom_call_target="tpu_custom_call" | custom-call | flops 17600000000 | bytes 1048576 | tf_op jit(solution)/shard_map/attention_backward/pallas_call | solution.py:182
  274.9 9.0 %collective-permute-done.24.rest_2_ = bf16[384,1024]{1,0:T(8,128)(2,1)S(1)} collective-permute-done((bf16[384,1024]{1,0:T(8,128)(2,1)S(1)}, bf16[384,1024]{1,0:T(8,128)(2,1)S(1)}, u32[]{:S(2)}, u32[]{:S(2)}) %collective-permute-start.24) | collective-permute-done | bytes 786464 | tf_op jit(solution)/shard_map/ppermute | solution.py:883
  286.5 17.3 %attention_backward.3.d_ref = bf16[3072,384]{1,0:T(8,128)(2,1)S(1)} custom-call(s32[4]{0:T(128)S(1)} %select_reduce_fusion.len_ref, bf16[3072,384]{1,0:T(8,128)(2,1)S(1)} %get-tuple-element.191.qkv_ref, bf16[3072,128]{1,0:T(8,128)(2,1)} %get-tuple-element.193.o_ref, f32[2,3072]{1,0:T(2,128)S(1)} %get-tuple-element.234.lse_ref, ...), custom_call_target="tpu_custom_call" | custom-call | flops 17600000000 | bytes 1048576 | tf_op jit(solution)/shard_map/attention_backward/pallas_call | solution.py:182
  316.3 11.9 %qkv_grads.1 = (bf16[1024,384]{1,0:T(8,128)(2,1)S(1)}, f32[2,1024]{1,0:T(2,128)S(1)}, f32[1,384]{1,0:T(1,128)S(1)}) custom-call(bf16[3072,1024]{1,0:T(8,128)(2,1)S(1)} %copy-done.1, bf16[3072,384]{1,0:T(8,128)(2,1)S(1)} %copy-done.5, bf16[1024,384]{1,0:T(8,128)(2,1)S(1)} %copy-done.3, f32[1,1024]{1,0:T(1,128)S(1)} %bitcast.113, f32[1,1024]{1,0:T(1,128)S(1)} %bitcast.124), custom_call_target="tpu_custom_call" | custom-call | flops 14300000256 | bytes 1048576 | tf_op jit(solution)/shard_map/qkv_grads/pallas_call | solution.py:652
  329.3 5.9 %collective-permute-done.28 = bf16[128,3072]{1,0:T(8,128)(2,1)} collective-permute-done((bf16[128,3072]{1,0:T(8,128)(2,1)}, bf16[128,3072]{1,0:T(8,128)(2,1)}, u32[]{:S(2)}, u32[]{:S(2)}) %collective-permute-start.28) | collective-permute-done | bytes 786464 | tf_op jit(solution)/shard_map/ppermute | solution.py:820
  354.1 18.2 %all-to-all-done.2.d_ref = bf16[8,384,384]{2,1,0:T(8,128)(2,1)S(1)} async-done(((bf16[8,384,384]{2,1,0:T(8,128)(2,1)}), bf16[8,384,384]{2,1,0:T(8,128)(2,1)S(1)}, u32[]{:S(2)}, u32[]{:S(2)}) %all-to-all-start.2) | async-done | bytes 2359328 | tf_op jit(solution)/shard_map/all_to_all | solution.py:1099
  372.3 3.9 collective-permute-start.34
  401.4 5.6 %input_gradient.1 = f32[384,1024]{1,0:T(8,128)} custom-call(bf16[8,384,384]{2,1,0:T(8,128)(2,1)S(1)} %all-to-all-done.2.d_ref, bf16[384,1024]{1,0:T(8,128)(2,1)S(1)} %bitcast.137, f32[1,1024]{1,0:T(1,128)S(1)} %bitcast.114, f32[384,1024]{1,0:T(8,128)S(1)} %copy-done.30, bf16[1024,3072]{1,0:T(8,128)(2,1)S(1)} %copy-done.16), custom_call_target="tpu_custom_call" | custom-call | flops 8800000000 | bytes 1048576 | tf_op jit(solution)/shard_map/input_gradient/pallas_call | solution.py:704
  407.0 5.2 %collective-permute-done.38.refs_3_ = bf16[32,12288]{1,0:T(8,128)(2,1)} collective-permute-done((bf16[32,12288]{1,0:T(8,128)(2,1)}, bf16[32,12288]{1,0:T(8,128)(2,1)}, u32[]{:S(2)}, u32[]{:S(2)}) %collective-permute-start.38) | collective-permute-done | bytes 786464 | tf_op jit(solution)/shard_map/ppermute | solution.py:817
  414.9 16.3 %collective-permute-done.43 = f32[12292]{0:T(1024)S(1)} collective-permute-done((f32[12292]{0:T(1024)S(1)}, f32[12292]{0:T(1024)S(1)}, u32[]{:S(2)}, u32[]{:S(2)}) %collective-permute-start.43) | collective-permute-done | bytes 49200 | tf_op jit(solution)/shard_map/ppermute | solution.py:883
  436.2 7.7 %place.2 = (f32[8,128,1024]{2,1,0:T(8,128)}, f32[8,32,4096]{2,1,0:T(8,128)}, f32[8,32,1024]{2,1,0:T(8,128)}, f32[256,3072]{1,0:T(8,128)}) custom-call(s32[7]{0:T(128)S(1)} %bitcast.139, s32[4]{0:T(128)S(1)} %broadcast_xor_fusion.rel_ref, bf16[32,12288]{1,0:T(8,128)(2,1)} %constant_dynamic-update-slice_fusion.2.refs_0_, ...), custom_call_target="tpu_custom_call" | custom-call | flops 7699999744 | bytes 1048576 | tf_op jit(solution)/shard_map/place/pallas_call | solution.py:764
  (362 shorter events, 172.2 us)
Async XLA Ops:
  7.2 123.0 %all-gather.4.cloned.1.call-start = ((), (), s32[]{:S(2)}) async-start(), calls=%async_computation.3 | async-start | bytes 2621440 | tf_op jit(solution)/shard_map/all_gather | solution.py:984
  7.2 20.8 %collective-permute-start = (bf16[384,1024]{1,0:T(8,128)(2,1)}, bf16[384,1024]{1,0:T(8,128)(2,1)S(1)}, u32[]{:S(2)}, u32[]{:S(2)}) collective-permute-start(bf16[384,1024]{1,0:T(8,128)(2,1)} %bitcast.133), channel_id=1, source_target_pairs={{0,8},{8,16},{16,24},{24,28},{28,20},{20,12},{12,4},{4,0},{1,9},{9... | collective-permute-start | bytes 2359304 | tf_op jit(solution)/shard_map/ppermute | solution.py:817
  10.3 19.2 %collective-permute-start.1 = (bf16[384,1024]{1,0:T(8,128)(2,1)}, bf16[384,1024]{1,0:T(8,128)(2,1)S(1)}, u32[]{:S(2)}, u32[]{:S(2)}) collective-permute-start(bf16[384,1024]{1,0:T(8,128)(2,1)} %bitcast.134), channel_id=1, source_target_pairs={{8,0},{16,8},{24,16},{28,24},{20,28},{12,20},{4,12},{0,4},{9,1},{1... | collective-permute-start | bytes 2359304 | tf_op jit(solution)/shard_map/ppermute | solution.py:820
  29.6 128.7 %all-gather.6.cloned.1.call-start = ((), (), s32[]{:S(2)}) async-start(), calls=%async_computation.4 | async-start | bytes 10485760 | tf_op jit(solution)/shard_map/all_gather | solution.py:1004
  107.0 20.6 %collective-permute-start.11 = (bf16[384,1024]{1,0:T(8,128)(2,1)}, bf16[384,1024]{1,0:T(8,128)(2,1)}, u32[]{:S(2)}, u32[]{:S(2)}) collective-permute-start(bf16[384,1024]{1,0:T(8,128)(2,1)} %bitcast.rest_4_.dy_ref), channel_id=1, source_target_pairs={{0,2},{1,3},{2,0},{3,1},{4,6},{5,7},{6,4},{7,5},{8,10},{9,11},{10,... | collective-permute-start | bytes 2359304 | tf_op jit(solution)/shard_map/ppermute | solution.py:883
  107.0 20.9 %all-to-all-start = ((bf16[8,384,128]{2,1,0:T(8,128)(2,1)}), bf16[8,384,128]{2,1,0:T(8,128)(2,1)S(1)}, u32[]{:S(2)}, u32[]{:S(2)}) async-start(bf16[8,384,128]{2,1,0:T(8,128)(2,1)} %bitcast.15), calls=%async_computation | async-start | bytes 1572864 | tf_op jit(solution)/shard_map/all_to_all | solution.py:1039
  136.2 19.6 %collective-permute-start.14 = (bf16[384,1024]{1,0:T(8,128)(2,1)S(1)}, bf16[384,1024]{1,0:T(8,128)(2,1)S(1)}, u32[]{:S(2)}, u32[]{:S(2)}) collective-permute-start(bf16[384,1024]{1,0:T(8,128)(2,1)S(1)} %get-tuple-element.199.rest_0_), channel_id=1, source_target_pairs={{0,2},{1,3},{2,0},{3,1},{4,6},{5,7},{6,4},{7,5},{8,10},{9,11},{10,... | collective-permute-start | bytes 2359304 | tf_op jit(solution)/shard_map/ppermute | solution.py:883
  136.5 19.3 %collective-permute-start.15 = (bf16[384,1024]{1,0:T(8,128)(2,1)S(1)}, bf16[384,1024]{1,0:T(8,128)(2,1)S(1)}, u32[]{:S(2)}, u32[]{:S(2)}) collective-permute-start(bf16[384,1024]{1,0:T(8,128)(2,1)S(1)} %get-tuple-element.199.rest_0_), channel_id=1, source_target_pairs={{0,1},{1,0},{2,3},{3,2},{4,5},{5,4},{6,7},{7,6},{8,9},{9,8},{10,11... | collective-permute-start | bytes 2359304 | tf_op jit(solution)/shard_map/ppermute | solution.py:883
  184.6 23.1 %collective-permute-start.18 = (bf16[384,1024]{1,0:T(8,128)(2,1)S(1)}, bf16[384,1024]{1,0:T(8,128)(2,1)S(1)}, u32[]{:S(2)}, u32[]{:S(2)}) collective-permute-start(bf16[384,1024]{1,0:T(8,128)(2,1)S(1)} %add_convert_fusion.6), channel_id=1, source_target_pairs={{0,2},{1,3},{2,0},{3,1},{4,6},{5,7},{6,4},{7,5},{8,10},{9,11},{10,... | collective-permute-start | bytes 2359304 | tf_op jit(solution)/shard_map/ppermute | solution.py:883
  218.1 27.3 %collective-permute-start.21 = (bf16[768,1024]{1,0:T(8,128)(2,1)}, bf16[768,1024]{1,0:T(8,128)(2,1)}, u32[]{:S(2)}, u32[]{:S(2)}) collective-permute-start(bf16[768,1024]{1,0:T(8,128)(2,1)} %get-tuple-element.229), channel_id=1, source_target_pairs={{0,1},{1,0},{2,3},{3,2},{4,5},{5,4},{6,7},{7,6},{8,9},{9,8},{10,11... | collective-permute-start | bytes 4718600 | tf_op jit(solution)/shard_map/ppermute | solution.py:883
  218.1 27.3 %all-to-all-start.1 = ((bf16[8,384,128]{2,1,0:T(8,128)(2,1)}), bf16[8,384,128]{2,1,0:T(8,128)(2,1)S(1)}, u32[]{:S(2)}, u32[]{:S(2)}) async-start(bf16[8,384,128]{2,1,0:T(8,128)(2,1)} %copy-done.11), calls=%async_computation.1 | async-start | bytes 1572864 | tf_op jit(solution)/shard_map/all_to_all | solution.py:1077
  223.8 172.3 %all-gather.8.cloned.1.call-start = ((), (), s32[]{:S(2)}) async-start(), calls=%async_computation.5 | async-start | bytes 7864320 | tf_op jit(solution)/shard_map/all_gather | solution.py:1070
  227.8 21.2 %collective-permute-start.20 = (bf16[64,3072]{1,0:T(8,128)(2,1)}, bf16[64,3072]{1,0:T(8,128)(2,1)}, u32[]{:S(2)}, u32[]{:S(2)}) collective-permute-start(bf16[64,3072]{1,0:T(8,128)(2,1)} %pad_maximum_fusion.6), channel_id=1, source_target_pairs={{8,0},{16,8},{24,16},{28,24},{20,28},{12,20},{4,12},{0,4},{9,1},{1... | collective-permute-start | bytes 1179656 | tf_op jit(solution)/shard_map/ppermute | solution.py:820
  247.4 36.5 %collective-permute-start.24 = (bf16[384,1024]{1,0:T(8,128)(2,1)S(1)}, bf16[384,1024]{1,0:T(8,128)(2,1)S(1)}, u32[]{:S(2)}, u32[]{:S(2)}) collective-permute-start(bf16[384,1024]{1,0:T(8,128)(2,1)S(1)} %add_convert_fusion.5), channel_id=1, source_target_pairs={{0,2},{1,3},{2,0},{3,1},{4,6},{5,7},{6,4},{7,5},{8,10},{9,11},{10,... | collective-permute-start | bytes 2359304 | tf_op jit(solution)/shard_map/ppermute | solution.py:883
  250.2 33.7 %collective-permute-start.23 = (bf16[128,3072]{1,0:T(8,128)(2,1)S(1)}, bf16[128,3072]{1,0:T(8,128)(2,1)S(1)}, u32[]{:S(2)}, u32[]{:S(2)}) collective-permute-start(bf16[128,3072]{1,0:T(8,128)(2,1)S(1)} %pad_maximum_fusion.3), channel_id=1, source_target_pairs={{8,0},{16,8},{24,16},{28,24},{20,28},{12,20},{4,12},{0,4},{9,1},{1... | collective-permute-start | bytes 2359304 | tf_op jit(solution)/shard_map/ppermute | solution.py:820
  252.8 31.1 %collective-permute-start.22 = (bf16[128,3072]{1,0:T(8,128)(2,1)S(1)}, bf16[128,3072]{1,0:T(8,128)(2,1)S(1)}, u32[]{:S(2)}, u32[]{:S(2)}) collective-permute-start(bf16[128,3072]{1,0:T(8,128)(2,1)S(1)} %pad_maximum_fusion.1), channel_id=1, source_target_pairs={{0,8},{8,16},{16,24},{24,28},{28,20},{20,12},{12,4},{4,0},{1,9},{9... | collective-permute-start | bytes 2359304 | tf_op jit(solution)/shard_map/ppermute | solution.py:817
  284.1 19.7 %collective-permute-start.26 = (bf16[128,3072]{1,0:T(8,128)(2,1)S(1)}, bf16[128,3072]{1,0:T(8,128)(2,1)S(1)}, u32[]{:S(2)}, u32[]{:S(2)}) collective-permute-start(bf16[128,3072]{1,0:T(8,128)(2,1)S(1)} %add_convert_fusion.3), channel_id=1, source_target_pairs={{8,0},{16,8},{24,16},{28,24},{20,28},{12,20},{4,12},{0,4},{9,1},{1... | collective-permute-start | bytes 2359304 | tf_op jit(solution)/shard_map/ppermute | solution.py:820
  305.0 30.2 %collective-permute-start.28 = (bf16[128,3072]{1,0:T(8,128)(2,1)}, bf16[128,3072]{1,0:T(8,128)(2,1)}, u32[]{:S(2)}, u32[]{:S(2)}) collective-permute-start(bf16[128,3072]{1,0:T(8,128)(2,1)} %add_convert_fusion.1), channel_id=1, source_target_pairs={{8,0},{16,8},{24,16},{28,24},{20,28},{12,20},{4,12},{0,4},{9,1},{1... | collective-permute-start | bytes 2359304 | tf_op jit(solution)/shard_map/ppermute | solution.py:820
  307.5 27.7 %collective-permute-start.27 = (bf16[128,3072]{1,0:T(8,128)(2,1)}, bf16[128,3072]{1,0:T(8,128)(2,1)}, u32[]{:S(2)}, u32[]{:S(2)}) collective-permute-start(bf16[128,3072]{1,0:T(8,128)(2,1)} %add_convert_fusion.2), channel_id=1, source_target_pairs={{0,8},{8,16},{16,24},{24,28},{28,20},{20,12},{12,4},{4,0},{1,9},{9... | collective-permute-start | bytes 2359304 | tf_op jit(solution)/shard_map/ppermute | solution.py:817
  308.1 64.2 %all-to-all-start.2 = ((bf16[8,384,384]{2,1,0:T(8,128)(2,1)}), bf16[8,384,384]{2,1,0:T(8,128)(2,1)S(1)}, u32[]{:S(2)}, u32[]{:S(2)}) async-start(bf16[8,384,384]{2,1,0:T(8,128)(2,1)} %bitcast.101), calls=%async_computation.2 | async-start | bytes 4718592 | tf_op jit(solution)/shard_map/all_to_all | solution.py:1099
  393.4 18.8 %collective-permute-start.38 = (bf16[32,12288]{1,0:T(8,128)(2,1)}, bf16[32,12288]{1,0:T(8,128)(2,1)}, u32[]{:S(2)}, u32[]{:S(2)}) collective-permute-start(bf16[32,12288]{1,0:T(8,128)(2,1)} %collective-permute-done.34.refs_1_), channel_id=1, source_target_pairs={{0,8},{8,16},{16,24},{24,28},{28,20},{20,12},{12,4},{4,0},{1,9},{9... | collective-permute-start | bytes 2359304 | tf_op jit(solution)/shard_map/ppermute | solution.py:817
  393.5 18.8 %collective-permute-start.39 = (bf16[32,12288]{1,0:T(8,128)(2,1)}, bf16[32,12288]{1,0:T(8,128)(2,1)}, u32[]{:S(2)}, u32[]{:S(2)}) collective-permute-start(bf16[32,12288]{1,0:T(8,128)(2,1)} %collective-permute-done.35.refs_2_), channel_id=1, source_target_pairs={{8,0},{16,8},{24,16},{28,24},{20,28},{12,20},{4,12},{0,4},{9,1},{1... | collective-permute-start | bytes 2359304 | tf_op jit(solution)/shard_map/ppermute | solution.py:820
  412.2 19.0 %collective-permute-start.41 = (bf16[32,12288]{1,0:T(8,128)(2,1)}, bf16[32,12288]{1,0:T(8,128)(2,1)S(1)}, u32[]{:S(2)}, u32[]{:S(2)}) collective-permute-start(bf16[32,12288]{1,0:T(8,128)(2,1)} %collective-permute-done.38.refs_3_), channel_id=1, source_target_pairs={{0,8},{8,16},{16,24},{24,28},{28,20},{20,12},{12,4},{4,0},{1,9},{9... | collective-permute-start | bytes 2359304 | tf_op jit(solution)/shard_map/ppermute | solution.py:817
  412.2 19.0 %collective-permute-start.42 = (bf16[32,12288]{1,0:T(8,128)(2,1)}, bf16[32,12288]{1,0:T(8,128)(2,1)S(1)}, u32[]{:S(2)}, u32[]{:S(2)}) collective-permute-start(bf16[32,12288]{1,0:T(8,128)(2,1)} %collective-permute-done.39.refs_4_), channel_id=1, source_target_pairs={{8,0},{16,8},{24,16},{28,24},{20,28},{12,20},{4,12},{0,4},{9,1},{1... | collective-permute-start | bytes 2359304 | tf_op jit(solution)/shard_map/ppermute | solution.py:820
  (88 other events, 680.1 us)
Sparse Core Ops, SparseCore 0:
  29.7 22.8 all-gather.3
  54.1 62.3 all-gather.5
  237.0 63.8 all-gather.7

commit v3 on v2

--- a/solution.py
+++ b/solution.py
@@ -31,6 +31,43 @@
     return jnp.where((lane >= h * HEAD) & (lane < (h + 1) * HEAD), block, jnp.zeros_like(block))
 
 
+def beside(block, heads):
+    return jnp.concatenate([head_part(block, h, heads) for h in range(heads)], axis=0)
+
+
+def diagonal(wide, heads):
+    block = wide.shape[1] // heads
+    parts = [
+        wide[h * HEAD : (h + 1) * HEAD, h * block : (h + 1) * block] for h in range(heads)
+    ]
+    return jnp.concatenate(parts, axis=0)
+
+
+DIRECT = 4
+
+
+def visit(i, block, segs, len_ref, direct, loop):
+    r0 = pl.multiple_of(i * block, block)
+    place = r0 + lax.broadcasted_iota(jnp.int32, (1, block), 1)
+    start = seg_starts(len_ref, segs, place)
+    first = seg_starts(len_ref, segs, r0) // block
+    for n in range(1, DIRECT + 1):
+
+        @pl.when(i - first + 1 == n)
+        def _():
+            direct(n, r0, place, start, pl.multiple_of((i - n + 1) * block, block))
+
+    @pl.when(i - first + 1 > DIRECT)
+    def _():
+        loop(r0, place, start, first)
+
+
+def seen(c0, count, place, start, heads):
+    key_pos = c0 + lax.broadcasted_iota(jnp.int32, (count, place.shape[1]), 0)
+    ok = (key_pos >= start) & (key_pos <= place)
+    return jnp.concatenate([ok] * heads, axis=1)
+
+
 def forward_kernel(heads, block, segs, len_ref, qkv_ref, o_ref, lse_ref, vt_ref):
     hd = heads * HEAD
     steps = qkv_ref.shape[0] // block
@@ -41,119 +78,147 @@
         return 0
 
     lax.fori_loop(0, steps, flip, 0)
-    key_rows = lax.broadcasted_iota(jnp.int32, (block, block), 0)
+
+    def queries(r0):
+        return beside(qkv_ref[pl.ds(r0, block), 0:hd] * jnp.asarray(HEAD**-0.5, BF16), heads)
+
+    def store(r0, top, total, acc):
+        lse = top + jnp.log(total)
+        for h in range(heads):
+            lse_ref[h : h + 1, pl.ds(r0, block)] = lse[:, h * block : (h + 1) * block]
+        o_ref[pl.ds(r0, block), :] = diagonal(acc / total, heads).T.astype(BF16)
+
+    def direct(n, r0, place, start, c0):
+        keys = pl.ds(c0, n * block)
+        s = lax.dot_general(qkv_ref[keys, hd : 2 * hd], queries(r0), NT, preferred_element_type=F32)
+        s = jnp.where(seen(c0, n * block, place, start, heads), s, -1e30)
+        top = jnp.max(s, axis=0, keepdims=True)
+        p = jnp.exp(s - top)
+        total = jnp.sum(p, axis=0, keepdims=True)
+        acc = jnp.dot(vt_ref[:, keys], p.astype(BF16), preferred_element_type=F32)
+        store(r0, top, total, acc)
+
+    def loop(r0, place, start, first):
+        q = queries(r0)
+
+        def key_step(j, carry):
+            top, total, acc = carry
+            c0 = pl.multiple_of(j * block, block)
+            keys = pl.ds(c0, block)
+            s = lax.dot_general(qkv_ref[keys, hd : 2 * hd], q, NT, preferred_element_type=F32)
+            s = jnp.where(seen(c0, block, place, start, heads), s, -1e30)
+            new = jnp.maximum(top, jnp.max(s, axis=0, keepdims=True))
+            p = jnp.exp(s - new)
+            shrink = jnp.exp(top - new)
+            total = total * shrink + jnp.sum(p, axis=0, keepdims=True)
+            acc = acc * shrink + jnp.dot(
+                vt_ref[:, keys], p.astype(BF16), preferred_element_type=F32
+            )
+            return new, total, acc
+
+        wide = heads * block
+        init = (
+            jnp.full((1, wide), -1e30, F32),
+            jnp.zeros((1, wide), F32),
+            jnp.zeros((hd, wide), F32),
+        )
+        store(r0, *lax.fori_loop(first, r0 // block + 1, key_step, init))
 
     def query_step(i, _):
-        r0 = pl.multiple_of(i * block, block)
-        q = qkv_ref[pl.ds(r0, block), 0:hd] * jnp.asarray(HEAD**-0.5, BF16)
-        qs = [head_part(q, h, heads) for h in range(heads)]
-        place = r0 + lax.broadcasted_iota(jnp.int32, (1, block), 1)
-        start = seg_starts(len_ref, segs, place)
-        first = seg_starts(len_ref, segs, r0) // block
-
-        def key_step(j, carry):
-            c0 = pl.multiple_of(j * block, block)
-            kb = qkv_ref[pl.ds(c0, block), hd : 2 * hd]
-            key_pos = key_rows + c0
-            ok = (key_pos >= start) & (key_pos <= place)
-            out = []
-            for h in range(heads):
-                top, total, acc = carry[3 * h : 3 * h + 3]
-                s = lax.dot_general(kb, qs[h], NT, preferred_element_type=F32)
-                s = jnp.where(ok, s, -1e30)
-                new = jnp.maximum(top, jnp.max(s, axis=0, keepdims=True))
-                p = jnp.exp(s - new)
-                shrink = jnp.exp(top - new)
-                total = total * shrink + jnp.sum(p, axis=0, keepdims=True)
-                vt = vt_ref[h * HEAD : (h + 1) * HEAD, pl.ds(c0, block)]
-                acc = acc * shrink + jnp.dot(vt, p.astype(BF16), preferred_element_type=F32)
-                out += [new, total, acc]
-            return tuple(out)
-
-        init = (
-            jnp.full((1, block), -1e30, F32),
-            jnp.zeros((1, block), F32),
-            jnp.zeros((HEAD, block), F32),
-        ) * heads
-        res = lax.fori_loop(first, i + 1, key_step, init)
-        flat = jnp.concatenate([res[3 * h + 2] / res[3 * h + 1] for h in range(heads)], axis=0)
-        o_ref[pl.ds(r0, block), :] = flat.T.astype(BF16)
-        for h in range(heads):
-            lse_ref[h : h + 1, pl.ds(r0, block)] = res[3 * h] + jnp.log(res[3 * h + 1])
+        visit(i, block, segs, len_ref, direct, loop)
         return 0
 
     lax.fori_loop(0, steps, query_step, 0)
 
 
-def backward_kernel(heads, h, block, segs, len_ref, qkv_ref, o_ref, lse_ref, do_ref, *rest):
-    before_ref = rest[0] if h else None
-    d_ref, kt_ref, dq_ref, dk_ref, dv_ref = rest[-5:]
+def backward_kernel(
+    heads,
+    block,
+    segs,
+    len_ref,
+    qkv_ref,
+    o_ref,
+    lse_ref,
+    do_ref,
+    d_ref,
+    kt_ref,
+    dq_ref,
+    dk_ref,
+    dv_ref,
+):
     hd = heads * HEAD
     steps = qkv_ref.shape[0] // block
-    mine = slice(h * HEAD, (h + 1) * HEAD)
 
     def flip(i, _):
         at = pl.multiple_of(i * block, block)
-        kt_ref[:, pl.ds(at, block)] = qkv_ref[pl.ds(at, block), hd : 2 * hd].T[mine]
+        kt_ref[:, pl.ds(at, block)] = qkv_ref[pl.ds(at, block), hd : 2 * hd].T
         dk_ref[pl.ds(at, block), :] = jnp.zeros((block, hd), F32)
         dv_ref[pl.ds(at, block), :] = jnp.zeros((block, hd), F32)
         return 0
 
     lax.fori_loop(0, steps, flip, 0)
-    key_rows = lax.broadcasted_iota(jnp.int32, (block, block), 0)
+
+    def operands(r0):
+        rows = pl.ds(r0, block)
+        q = beside(qkv_ref[rows, 0:hd] * jnp.asarray(HEAD**-0.5, BF16), heads)
+        do = do_ref[rows, :]
+        both = (do.astype(F32) * o_ref[rows, :].astype(F32)).T
+        delta = [
+            jnp.sum(both[h * HEAD : (h + 1) * HEAD], axis=0, keepdims=True) for h in range(heads)
+        ]
+        lse = [lse_ref[h : h + 1, rows] for h in range(heads)]
+        return q, beside(do, heads), jnp.concatenate(delta, axis=1), jnp.concatenate(lse, axis=1)
+
+    def part(c0, count, place, start, q, do, delta, lse):
+        keys = pl.ds(c0, count)
+        s = lax.dot_general(qkv_ref[keys, hd : 2 * hd], q, NT, preferred_element_type=F32)
+        p = jnp.where(seen(c0, count, place, start, heads), jnp.exp(s - lse), 0.0)
+        dp = lax.dot_general(
+            qkv_ref[keys, 2 * hd : 3 * hd], do, NT, preferred_element_type=F32
+        )
+        ds = (p * (dp - delta)).astype(BF16)
+        dv_ref[keys, :] += jnp.dot(p.astype(BF16), do, preferred_element_type=F32)
+        dk_ref[keys, :] += jnp.dot(ds, q, preferred_element_type=F32)
+        return jnp.dot(kt_ref[:, keys], ds, preferred_element_type=F32)
+
+    def store(r0, dq):
+        dq_ref[pl.ds(r0, block), :] = (diagonal(dq, heads) * HEAD**-0.5).T
+
+    def direct(n, r0, place, start, c0):
+        store(r0, part(c0, n * block, place, start, *operands(r0)))
+
+    def loop(r0, place, start, first):
+        given = operands(r0)
+
+        def key_step(j, dq):
+            return dq + part(pl.multiple_of(j * block, block), block, place, start, *given)
+
+        init = jnp.zeros((hd, heads * block), F32)
+        store(r0, lax.fori_loop(first, r0 // block + 1, key_step, init))
 
     def query_step(i, _):
-        r0 = pl.multiple_of(i * block, block)
-        q = qkv_ref[pl.ds(r0, block), 0:hd] * jnp.asarray(HEAD**-0.5, BF16)
-        q = head_part(q, h, heads)
-        do = head_part(do_ref[pl.ds(r0, block), :], h, heads)
-        both = (do.astype(F32) * o_ref[pl.ds(r0, block), :].astype(F32)).T
-        delta = jnp.sum(both[mine], axis=0, keepdims=True)
-        lse = lse_ref[h : h + 1, pl.ds(r0, block)]
-        place = r0 + lax.broadcasted_iota(jnp.int32, (1, block), 1)
-        start = seg_starts(len_ref, segs, place)
-        first = seg_starts(len_ref, segs, r0) // block
-
-        def key_step(j, dq):
-            c0 = pl.multiple_of(j * block, block)
-            kb = qkv_ref[pl.ds(c0, block), hd : 2 * hd]
-            vb = qkv_ref[pl.ds(c0, block), 2 * hd : 3 * hd]
-            key_pos = key_rows + c0
-            ok = (key_pos >= start) & (key_pos <= place)
-            s = lax.dot_general(kb, q, NT, preferred_element_type=F32)
-            p = jnp.where(ok, jnp.exp(s - lse), 0.0)
-            dp = lax.dot_general(vb, do, NT, preferred_element_type=F32)
-            ds = (p * (dp - delta)).astype(BF16)
-            dv_ref[pl.ds(c0, block), :] += jnp.dot(p.astype(BF16), do, preferred_element_type=F32)
-            dk_ref[pl.ds(c0, block), :] += jnp.dot(ds, q, preferred_element_type=F32)
-            return dq + jnp.dot(kt_ref[:, pl.ds(c0, block)], ds, preferred_element_type=F32)
-
-        dq = lax.fori_loop(first, i + 1, key_step, jnp.zeros((HEAD, block), F32))
-        dq_ref[pl.ds(r0, block), :] = (dq * HEAD**-0.5).T
+        visit(i, block, segs, len_ref, direct, loop)
         return 0
 
     lax.fori_loop(0, steps, query_step, 0)
 
-    def finish(i, _):
-        at = pl.multiple_of(i * block, block)
-        rows = pl.ds(at, block)
-        d = [dq_ref[rows, :], dk_ref[rows, mine], dv_ref[rows, mine]]
-        d = jnp.concatenate(d, axis=1).astype(BF16)
-        if before_ref is not None:
-            d = jnp.concatenate([before_ref[rows, :], d], axis=1)
-        d_ref[rows, :] = d
+    def finish_rows(i, _):
+        rows = pl.ds(pl.multiple_of(i * block, block), block)
+        roles = [ref[rows, :] for ref in (dq_ref, dk_ref, dv_ref)]
+        parts = [v[:, h * HEAD : (h + 1) * HEAD] for h in range(heads) for v in roles]
+        d_ref[rows, :] = jnp.concatenate(parts, axis=1).astype(BF16)
         return 0
 
-    lax.fori_loop(0, steps, finish, 0)
+    lax.fori_loop(0, steps, finish_rows, 0)
 
 
 def takes(us):
-    return pl.CostEstimate(flops=int(us * 1.1e9), bytes_accessed=1 << 20, transcendentals=0)
+    return pl.CostEstimate(flops=int(us * 3.30e9), bytes_accessed=1 << 20, transcendentals=0)
 
 
 VM = pl.BlockSpec(memory_space=pltpu.VMEM)
 SM = pl.BlockSpec(memory_space=pltpu.SMEM)
-LIMIT = 40 << 20
+LIMIT = 32 << 20
 
 
 def attention_forward(row, qkv, block):
@@ -170,30 +235,25 @@
         out_specs=(VM, VM),
         scratch_shapes=[pltpu.VMEM((hd, rows), BF16)],
         compiler_params=pltpu.CompilerParams(vmem_limit_bytes=LIMIT),
-        cost_estimate=takes(22),
+        cost_estimate=takes(14),
         name="attention_forward",
     )(row, qkv)
 
 
-def attention_backward(row, qkv, o, lse, do, block, h, before=()):
+def attention_backward(row, qkv, o, lse, do, block):
     rows, wide = qkv.shape
     hd = wide // 3
     heads = hd // HEAD
     return pl.pallas_call(
-        functools.partial(backward_kernel, heads, h, block, row.shape[0]),
-        out_shape=jax.ShapeDtypeStruct((rows, (h + 1) * 3 * HEAD), BF16),
-        in_specs=[SM] + [VM] * (4 + len(before)),
+        functools.partial(backward_kernel, heads, block, row.shape[0]),
+        out_shape=jax.ShapeDtypeStruct((rows, wide), BF16),
+        in_specs=[SM] + [VM] * 4,
         out_specs=VM,
-        scratch_shapes=[
-            pltpu.VMEM((HEAD, rows), BF16),
-            pltpu.VMEM((rows, HEAD), F32),
-            pltpu.VMEM((rows, hd), F32),
-            pltpu.VMEM((rows, hd), F32),
-        ],
-        compiler_params=pltpu.CompilerParams(vmem_limit_bytes=LIMIT),
-        cost_estimate=takes(16),
+        scratch_shapes=[pltpu.VMEM((hd, rows), BF16)] + [pltpu.VMEM((rows, hd), F32)] * 3,
+        compiler_params=pltpu.CompilerParams(vmem_limit_bytes=44 << 20),
+        cost_estimate=takes(21),
         name="attention_backward",
-    )(row, qkv, o, lse, do, *before)
+    )(row, qkv, o, lse, do)
 
 
 def tier_bounds(n):
@@ -301,23 +361,25 @@
 GELU = 0.7978845608028654
 
 
-def feed_kernel(n_fsdp, rel_ref, count_ref, bfc_ref, wproj_ref, wfc_ref, *rest):
-    low_refs, rest = rest[:n_fsdp], rest[n_fsdp:]
-    dy_refs, rest = rest[:n_fsdp], rest[n_fsdp:]
-    tiers = tier_bounds(n_fsdp)
+def feed_kernel(
+    packs, rel_ref, which_ref, count_ref, bfc_ref, wproj_ref, wfc_ref, dy_ref, *rest
+):
+    low_refs, rest = rest[:packs], rest[packs:]
+    tiers = tier_bounds(packs)
     dtwo_refs, rest = rest[: len(tiers)], rest[len(tiers) :]
     hidden_ref, di_ref, dmlp_ref, low_s = rest
     step = pl.program_id(0)
     rows = low_s.shape[0]
     valid = lax.broadcasted_iota(jnp.int32, (rows, 1), 0) < count_ref[step]
 
-    for k in range(n_fsdp):
+    for k in range(packs):
 
         @pl.when(step == k)
         def _():
             low_s[...] = low_refs[k][...]
-            dy = dy_refs[k][...]
-            dmlp_ref[...] = jnp.where(valid, dy, jnp.zeros_like(dy))
+
+    dy = dy_ref[...]
+    dmlp_ref[...] = jnp.where(valid, dy, jnp.zeros_like(dy))
 
     u = jnp.dot(low_s[...], wfc_ref[...], preferred_element_type=F32) + bfc_ref[...]
     dh = lax.dot_general(dmlp_ref[...], wproj_ref[...], NT, preferred_element_type=F32)
@@ -336,11 +398,11 @@
             out_ref[...] = dtwo.astype(out_ref.dtype)
 
 
-def feed(rel, counts, low_pieces, dy_pieces, wfc, wproj, bfc):
+def feed(rel, which, counts, low_pieces, dy_all, wfc, wproj, bfc, own):
     rows, width = low_pieces[0].shape
-    n_fsdp = len(low_pieces)
+    packs = len(low_pieces)
     wide = wproj.shape[0]
-    tiers = tier_bounds(n_fsdp)
+    tiers = tier_bounds(packs)
 
     def whole(*shape):
         return pl.BlockSpec(shape, lambda g, *_: (0,) * len(shape), pipeline_mode=pl.Buffered(1))
@@ -350,109 +412,86 @@
 
     each = pl.BlockSpec((rows, wide), lambda g, *_: (g, 0))
     return pl.pallas_call(
-        functools.partial(feed_kernel, n_fsdp),
+        functools.partial(feed_kernel, packs),
         grid_spec=pltpu.PrefetchScalarGridSpec(
-            num_scalar_prefetch=2,
-            grid=(n_fsdp,),
+            num_scalar_prefetch=3,
+            grid=(packs,),
             in_specs=[
                 whole(1, wide),
                 whole(wide, width),
                 pl.BlockSpec(
-                    (width, wide), lambda g, rel, _: (0, rel[0]), pipeline_mode=pl.Buffered(1)
+                    (width, wide), lambda g, rel, *_: (0, rel[0]), pipeline_mode=pl.Buffered(1)
                 ),
+                pl.BlockSpec((rows, width), lambda g, rel, which, _: (which[g], 0)),
             ]
-            + [whole(rows, width)] * (2 * n_fsdp),
+            + [whole(rows, width)] * packs,
             out_specs=[tier(lo, hi) for lo, hi in tiers]
             + [each, each, pl.BlockSpec((rows, width), lambda g, *_: (g, 0))],
             scratch_shapes=[pltpu.VMEM((rows, width), BF16)],
         ),
         out_shape=tuple(
             [
-                jax.ShapeDtypeStruct(((hi - lo) * rows, width), F32 if lo == 0 else BF16)
+                jax.ShapeDtypeStruct(((hi - lo) * rows, width), F32 if lo == 0 and own else BF16)
                 for lo, hi in tiers
             ]
-            + [jax.ShapeDtypeStruct((n_fsdp * rows, wide), BF16)] * 2
-            + [jax.ShapeDtypeStruct((n_fsdp * rows, width), BF16)]
+            + [jax.ShapeDtypeStruct((packs * rows, wide), BF16)] * 2
+            + [jax.ShapeDtypeStruct((packs * rows, width), BF16)]
         ),
-        cost_estimate=takes(20),
+        cost_estimate=takes(10),
         compiler_params=pltpu.CompilerParams(vmem_limit_bytes=52 << 20),
         name="feed",
-    )(rel, counts, bfc, wproj, wfc, *low_pieces, *dy_pieces)
-
-
-def feed_grads_kernel(n_fsdp, hidden_ref, di_ref, dmlp_ref, wproj_ref, *rest):
+    )(rel, which, counts, bfc, wproj, wfc, dy_all, *low_pieces)
+
+
+def feed_grads_kernel(
+    near, n_fsdp, hid_a, hid_b, di_a, di_b, dmlp_a, dmlp_b, *rest
+):
     low_refs, rest = rest[:n_fsdp], rest[n_fsdp:]
-    tiers = tier_bounds(n_fsdp)
-    mlp_refs, rest = rest[: len(tiers)], rest[len(tiers) :]
     gproj_ref, gfc_ref, gbfc_ref = rest[:3]
     scratch = rest[3:]
     step = pl.program_id(0)
-    rows, wide = hidden_ref.shape
+    rows, wide = hid_a.shape
     n_seq, _, thin, _ = gfc_ref.shape
-    width = dmlp_ref.shape[1]
-    share = width // n_fsdp
-
-    hidden = hidden_ref[...]
-    di = di_ref[...]
-    mlp = jnp.dot(hidden, wproj_ref[...], preferred_element_type=F32)
-    for (lo, hi), out_ref in zip(tiers, mlp_refs):
-
-        @pl.when((step >= lo) & (step < hi))
-        def _():
-            out_ref[...] = mlp.astype(out_ref.dtype)
-
-    sums = jnp.sum(di.astype(F32), axis=0, keepdims=True)
+    share = n_seq * thin
 
     @pl.when(step == 0)
     def _():
-        gbfc_ref[...] = sums
-
-    @pl.when(step > 0)
-    def _():
-        gbfc_ref[...] += sums
+        gbfc_ref[...] = jnp.zeros_like(gbfc_ref)
 
     def store_fc(i, g):
         for k in range(n_seq):
             gfc_ref[k, i] = g[k * thin : (k + 1) * thin]
 
-    if len(scratch) == 3:
-        low_s, proj_s, fc_s = scratch
-
-        @pl.when(step == 0)
+    for k in range(n_fsdp):
+        hid_ref, di_ref, dmlp_ref = (hid_a, di_a, dmlp_a) if k < near else (hid_b, di_b, dmlp_b)
+
+        @pl.when(step == k)
         def _():
-            proj_s[...] = jnp.zeros_like(proj_s)
-            fc_s[...] = jnp.zeros_like(fc_s)
-
-        for k in range(n_fsdp):
-
-            @pl.when(step == k)
-            def _():
-                low_s[...] = low_refs[k][...]
-
-        proj_s[...] += jnp.dot(hidden.T, dmlp_ref[...], preferred_element_type=F32)
-        fc_s[...] += jnp.dot(low_s[...].T, di, preferred_element_type=F32)
-
-        @pl.when(step == n_fsdp - 1)
-        def _():
+            di = di_ref[...]
+            gbfc_ref[...] += jnp.sum(di.astype(F32), axis=0, keepdims=True)
+            if len(scratch) == 2:
+                proj_s, fc_s = scratch
+                proj = jnp.dot(hid_ref[...].T, dmlp_ref[...], preferred_element_type=F32)
+                fc = jnp.dot(low_refs[k][...].T, di, preferred_element_type=F32)
+                proj_s[...] = proj if k == 0 else proj_s[...] + proj
+                fc_s[...] = fc if k == 0 else fc_s[...] + fc
+            else:
+                hiddent_s, di_s, dmlp_s, lowt_s = scratch
+                at = slice(k * rows, (k + 1) * rows)
+                hiddent_s[:, at] = hid_ref[...].T
+                di_s[at, :] = di
+                dmlp_s[at, :] = dmlp_ref[...]
+                lowt_s[:, at] = low_refs[k][...].T
+
+    @pl.when(step == n_fsdp - 1)
+    def _():
+        if len(scratch) == 2:
+            proj_s, fc_s = scratch
             gproj_ref[...] = proj_s[...].astype(BF16)
             for i in range(n_fsdp):
                 store_fc(i, fc_s[i * share : (i + 1) * share, :].astype(BF16))
-
-        return
-
-    hiddent_s, di_s, dmlp_s, lowt_s = scratch
-    for k in range(n_fsdp):
-
-        @pl.when(step == k)
-        def _():
-            at = slice(k * rows, (k + 1) * rows)
-            hiddent_s[:, at] = hidden.T
-            di_s[at, :] = di
-            dmlp_s[at, :] = dmlp_ref[...]
-            lowt_s[:, at] = low_refs[k][...].T
-
-    @pl.when(step == n_fsdp - 1)
-    def _():
+            return
+        hiddent_s, di_s, dmlp_s, lowt_s = scratch
         tile = min(256, wide)
 
         def proj_tile(i, _):
@@ -472,16 +511,15 @@
         lax.fori_loop(0, n_fsdp, fc_tile, 0)
 
 
-def feed_grads(hidden, di, dmlp, wproj, low_pieces, n_seq):
+def feed_grads(near, far, low_pieces, n_seq):
     rows, width = low_pieces[0].shape
     n_fsdp = len(low_pieces)
-    wide = wproj.shape[0]
+    wide = near[0].shape[1]
     total = n_fsdp * rows
+    count = near[0].shape[0] // rows
     thin = width // n_fsdp // n_seq
-    tiers = tier_bounds(n_fsdp)
     if total > 2048:
-        scratch = [pltpu.VMEM((rows, width), BF16)]
-        scratch += [pltpu.VMEM((wide, width), F32), pltpu.VMEM((width, wide), F32)]
+        scratch = [pltpu.VMEM((wide, width), F32), pltpu.VMEM((width, wide), F32)]
     else:
         scratch = [pltpu.VMEM((wide, total), BF16), pltpu.VMEM((total, wide), BF16)]
         scratch += [pltpu.VMEM((total, width), BF16), pltpu.VMEM((width, total), BF16)]
@@ -492,52 +530,84 @@
     def last(*shape):
         return pl.BlockSpec(shape, lambda g: (0,) * len(shape))
 
+    def of_near(columns):
+        return pl.BlockSpec((rows, columns), lambda g: (jnp.minimum(g, count - 1), 0))
+
+    def of_far(columns):
+        return pl.BlockSpec((rows, columns), lambda g: (jnp.maximum(g - count, 0), 0))
+
+    pairs = [(of_near(wide), of_far(wide))] * 2 + [(of_near(width), of_far(width))]
+    return pl.pallas_call(
+        functools.partial(feed_grads_kernel, count, n_fsdp),
+        grid=(n_fsdp,),
+        in_specs=[spec for pair in pairs for spec in pair] + [whole(rows, width)] * n_fsdp,
+        out_specs=[last(wide, width), last(n_seq, n_fsdp, thin, wide), last(1, wide)],
+        out_shape=(
+            jax.ShapeDtypeStruct((wide, width), BF16),
+            jax.ShapeDtypeStruct((n_seq, n_fsdp, thin, wide), BF16),
+            jax.ShapeDtypeStruct((1, wide), F32),
+        ),
+        scratch_shapes=scratch,
+        cost_estimate=takes(15),
+        compiler_params=pltpu.CompilerParams(vmem_limit_bytes=48 << 20),
+        name="feed_grads",
+    )(near[0], far[0], near[1], far[1], near[2], far[2], *low_pieces)
+
+
+def feed_out_kernel(packs, hidden_ref, wproj_ref, *mlp_refs):
+    step = pl.program_id(0)
+    mlp = jnp.dot(hidden_ref[...], wproj_ref[...], preferred_element_type=F32)
+    for (lo, hi), out_ref in zip(tier_bounds(packs), mlp_refs):
+
+        @pl.when((step >= lo) & (step < hi))
+        def _():
+            out_ref[...] = mlp.astype(out_ref.dtype)
+
+
+def feed_out(hidden, wproj, rows, own):
+    wide, width = wproj.shape
+    packs = hidden.shape[0] // rows
+    tiers = tier_bounds(packs)
+
     def tier(lo, hi):
         return pl.BlockSpec((rows, width), lambda g: (jnp.clip(g - lo, 0, hi - lo - 1), 0))
 
-    each = pl.BlockSpec((rows, wide), lambda g: (g, 0))
     return pl.pallas_call(
-        functools.partial(feed_grads_kernel, n_fsdp),
-        grid=(n_fsdp,),
-        in_specs=[each, each, pl.BlockSpec((rows, width), lambda g: (g, 0)), whole(wide, width)]
-        + [whole(rows, width)] * n_fsdp,
-        out_specs=[tier(lo, hi) for lo, hi in tiers]
-        + [last(wide, width), last(n_seq, n_fsdp, thin, wide), last(1, wide)],
+        functools.partial(feed_out_kernel, packs),
+        grid=(packs,),
+        in_specs=[
+            pl.BlockSpec((rows, wide), lambda g: (g, 0)),
+            pl.BlockSpec((wide, width), lambda g: (0, 0), pipeline_mode=pl.Buffered(1)),
+        ],
+        out_specs=[tier(lo, hi) for lo, hi in tiers],
         out_shape=tuple(
-            [
-                jax.ShapeDtypeStruct(((hi - lo) * rows, width), F32 if lo == 0 else BF16)
-                for lo, hi in tiers
-            ]
-            + [
-                jax.ShapeDtypeStruct((wide, width), BF16),
-                jax.ShapeDtypeStruct((n_seq, n_fsdp, thin, wide), BF16),
-                jax.ShapeDtypeStruct((1, wide), F32),
-            ]
+            jax.ShapeDtypeStruct(((hi - lo) * rows, width), F32 if lo == 0 and own else BF16)
+            for lo, hi in tiers
         ),
-        scratch_shapes=scratch,
-        cost_estimate=takes(18),
-        compiler_params=pltpu.CompilerParams(vmem_limit_bytes=52 << 20),
-        name="feed_grads",
-    )(hidden, di, dmlp, wproj, *low_pieces)
+        cost_estimate=takes(0.3),
+        compiler_params=pltpu.CompilerParams(vmem_limit_bytes=20 << 20),
+        name="feed_out",
+    )(hidden, wproj)
 
 
 def middle_back_kernel(
     n_fsdp,
     terms,
+    rel_ref,
     count_ref,
     merged_ref,
     middle_ref,
     dy_ref,
     gain_ref,
     wout_ref,
-    later_ref,
     *rest,
 ):
+    tiers = tier_bounds(n_fsdp)
     term_refs, rest = rest[:terms], rest[terms:]
-    gout_ref, d_middle_ref, d_merged_ref, vec_ref, passed_ref = rest
-    passed_ref[...] = later_ref[...]
+    gout_refs, rest = rest[: len(tiers)], rest[len(tiers) :]
+    d_middle_ref, d_merged_ref, vec_ref, flip_s, order_s = rest
     n_seq, rows, hd = merged_ref.shape
-    thin = gout_ref.shape[2]
+    share = flip_s.shape[0] // n_fsdp
     valid = lax.broadcasted_iota(jnp.int32, (rows, 1), 0) < count_ref[0]
     n, scale = norm_parts(middle_ref[...])
     d_two = functools.reduce(jnp.add, [ref[...].astype(F32) for ref in term_refs])
@@ -556,32 +626,37 @@
     vec_ref[2:3, :] = jnp.sum(d_two, axis=0, keepdims=True)
     vec_ref[3:4, :] = jnp.sum(d_result, axis=0, keepdims=True)
     merged = jnp.concatenate([merged_ref[k] for k in range(n_seq)], axis=1)
-    gout = jnp.dot(merged.T, d_attn, preferred_element_type=F32).astype(BF16)
-    for f in range(n_fsdp):
-        for k in range(n_seq):
-            at = (f * n_seq + k) * thin
-            gout_ref[k, f] = gout[at : at + thin]
-
-
-def middle_back(n_fsdp, count, merged, middle, dy, gain, wout, later, terms):
+    flip_s[...] = merged.T
+    for k in range(n_fsdp):
+        at = pl.multiple_of(rel_ref[k] * share, share)
+        order_s[k * share : (k + 1) * share, :] = flip_s[pl.ds(at, share), :]
+    gout = jnp.dot(order_s[...], d_attn, preferred_element_type=F32).astype(BF16)
+    for (lo, hi), out_ref in zip(tiers, gout_refs):
+        out_ref[...] = gout[lo * share : hi * share]
+
+
+def middle_back(rel, count, merged, middle, dy, gain, wout, terms):
     rows, width = middle.shape
-    n_seq = merged.shape[0]
-    thin = width // n_fsdp // n_seq
+    n_fsdp = rel.shape[0]
+    share = width // n_fsdp
+    tiers = tier_bounds(n_fsdp)
     return pl.pallas_call(
         functools.partial(middle_back_kernel, n_fsdp, len(terms)),
-        in_specs=[SM] + [VM] * (6 + len(terms)),
-        out_specs=(VM,) * 5,
-        out_shape=(
-            jax.ShapeDtypeStruct((n_seq, n_fsdp, thin, width), BF16),
-            jax.ShapeDtypeStruct((rows, width), F32),
-            jax.ShapeDtypeStruct(merged.shape, BF16),
-            jax.ShapeDtypeStruct((4, width), F32),
-            jax.ShapeDtypeStruct(later.shape, BF16),
+        in_specs=[SM] * 2 + [VM] * (5 + len(terms)),
+        out_specs=(VM,) * (len(tiers) + 3),
+        out_shape=tuple(
+            [jax.ShapeDtypeStruct(((hi - lo) * share, width), BF16) for lo, hi in tiers]
+            + [
+                jax.ShapeDtypeStruct((rows, width), F32),
+                jax.ShapeDtypeStruct(merged.shape, BF16),
+                jax.ShapeDtypeStruct((4, width), F32),
+            ]
         ),
+        scratch_shapes=[pltpu.VMEM((width, rows), BF16)] * 2,
         cost_estimate=takes(7),
-        compiler_params=pltpu.CompilerParams(vmem_limit_bytes=48 << 20),
+        compiler_params=pltpu.CompilerParams(vmem_limit_bytes=36 << 20),
         name="middle_back",
-    )(count, merged, middle, dy, gain, wout, later, *terms)
+    )(rel, count, merged, middle, dy, gain, wout, *terms)
 
 
 def finish_kernel(count_ref, middle_ref, bproj_ref, *rest):
@@ -718,7 +793,7 @@
             pltpu.VMEM((steps, rows, width // steps), F32),
         ],
         cost_estimate=takes(8),
-        compiler_params=pltpu.CompilerParams(vmem_limit_bytes=40 << 20),
+        compiler_params=pltpu.CompilerParams(vmem_limit_bytes=32 << 20),
         name="input_gradient",
     )(d_packed, x, gain, d_middle, w_all)
 
@@ -890,9 +965,9 @@
     return masks
 
 
-def cube_gather(value, axis):
+def cube_gather(value, axis, n=None):
     held = [value]
-    for bit in reversed(bits(lax.axis_size(axis))):
+    for bit in reversed(bits(n or lax.axis_size(axis))):
         held = held + [swap(block, axis, bit) for block in held]
     return held
 
@@ -900,6 +975,7 @@
 class Scatter:
     def __init__(self, tiers, axis):
         self.axis = axis
+        tiers = list(tiers)
         self.left = self.top = len(tiers) - 1
         self.size = tiers[0].shape[0]
         self.terms = [[t] for t in tiers]
@@ -979,9 +1055,10 @@
     tail = jnp.pad(small, (0, extra * 3 * hd - small.shape[0])).reshape(extra, 3 * hd)
 
     walk = Walk(ring.gather(x))
-    moved, mine, w_out = milestone(walk.moving, (own_cols, tail), w_out)
+    wfc = lax.all_gather(w_fc, "fsdp", axis=0, tiled=True)
+    dy_all = lax.all_gather(dy, "fsdp", axis=0, tiled=True)
+    moved, mine = milestone(walk.moving, (own_cols, tail))
     walk.go(moved)
-    wout = lax.all_gather(w_out, "fsdp", axis=0, tiled=True)
     packs = [jnp.concatenate(mine, axis=0)]
     held = None
     for bit in reversed(bits(n_fsdp)):
@@ -999,9 +1076,10 @@
             )
 
     moved_first = moved
-    moved, packs, w_fc = milestone(walk.moving, packs, w_fc)
+    moved, packs, w_out = milestone(walk.moving, packs, w_out)
     walk.go(moved)
-    wfc = lax.all_gather(w_fc, "fsdp", axis=0, tiled=True)
+    top = n_fsdp // 2
+    wout_far = swap(w_out, "fsdp", top)
 
     w_own = jnp.zeros((width, 3 * hd), BF16)
     vectors = jnp.zeros((n_fsdp, tail.size), BF16)
@@ -1027,112 +1105,150 @@
         ready = len(pieces)
         projected(range(done, ready))
         done = ready
-        moved, held = milestone(walk.moving, held)
+        moved, held, wout_far = milestone(walk.moving, held, wout_far)
         walk.go(moved)
         pieces += list(moved)
     projected(range(done, len(pieces)))
     x_all, qkv = held
 
     attended, lse = attention_forward(row, qkv, rows)
-    dy_first, attended = milestone(dy, attended)
-    dy_pieces = cube_gather(dy_first, "fsdp")
+    wout = jnp.zeros((width, width), BF16)
+    wout_pieces = cube_gather(w_out, "fsdp", top) + cube_gather(wout_far, "fsdp", top)
+    for k, mask in enumerate(reach(top) + [m | top for m in reach(top)]):
+        wout = lax.dynamic_update_slice_in_dim(wout, wout_pieces[k], (me_fsdp ^ mask) * share, 0)
     merged = lax.all_to_all(
         attended.reshape(n_seq, rows, hd), "seq", split_axis=0, concat_axis=0, tiled=True
     )
-    merged, dy_pieces = milestone(merged, dy_pieces)
+
+    merged, wout = milestone(merged, wout)
 
     ends = jnp.sum(home_rows[:, :last], axis=1)
-    ends = jnp.sum(jnp.where(rel[:, None] == groups[None, :], ends[None, :], 0), axis=1)
-    counts = jnp.clip(ends - me_seq * rows, 0, rows)
+
+    def valid_counts(index):
+        of = jnp.sum(jnp.where(index[:, None] == groups[None, :], ends[None, :], 0), axis=1)
+        return jnp.clip(of - me_seq * rows, 0, rows)
+
+    near = me_fsdp ^ jnp.asarray(reach(top), jnp.int32)
+    far = near ^ top
+    near_far = jnp.concatenate([near, far])
+    counts = valid_counts(near)
     low, middle, square_attn = attend_out(
         counts, merged, x, wout, bout, gain_two, shift_two
     )
-    low_pieces = cube_gather(low, "fsdp")
-    tiers = len(tier_bounds(n_fsdp))
-    results = feed(
-        rel, counts, low_pieces, dy_pieces, wfc, w_proj, bias_fc.astype(F32)[None]
-    )
-    d_two, (hidden, d_inner, d_mlp) = results[:tiers], results[tiers:]
-
-    d_two = Scatter(d_two, "fsdp")
-    while d_two.left > 1:
-        d_two.send()
-        d_two.moving, hidden = milestone(d_two.moving, hidden)
-        d_two.take()
-    d_two.send()
-    results = feed_grads(hidden, d_inner, d_mlp, w_proj, low_pieces, n_seq)
-    d_two.moving, results = milestone(d_two.moving, results)
-    d_two.take()
-    mlp, (gproj, gfc, gbfc) = results[:tiers], results[tiers:]
-    gout, d_middle, d_merged, sums_two, w_qkv = middle_back(
-        n_fsdp, counts, merged, middle, dy, gain_two, wout, w_qkv, d_two.terms[0]
-    )
-    w_all = lax.all_gather(w_qkv, "fsdp", axis=0, tiled=True)
+
+    bfc = bias_fc.astype(F32)[None]
+    low_far = swap(low, "fsdp", top)
+    low_near = cube_gather(low, "fsdp", top)
+    halves = len(tier_bounds(top))
+    results = feed(rel, near, counts, low_near, dy_all, wfc, w_proj, bfc, True)
+    two_near, feed_near = Scatter(results[:halves], "fsdp"), results[halves:]
+    low_far, feed_near = milestone(low_far, feed_near)
+    while two_near.left:
+        two_near.send()
+        two_near.take()
+    low_far = cube_gather(low_far, "fsdp", top)
+    results = feed(rel, far, valid_counts(far), low_far, dy_all, wfc, w_proj, bfc, False)
+    two_far, feed_far = Scatter(results[:halves], "fsdp"), results[halves:]
+    while two_far.left:
+        two_far.send()
+        two_far.moving, feed_far, two_near.terms = milestone(
+            two_far.moving, feed_far, two_near.terms
+        )
+        two_far.take()
+
+    far_two = swap(add_up(two_far.terms[0]).astype(BF16), "fsdp", top)
+    gproj, gfc, gbfc = feed_grads(feed_near, feed_far, low_near + low_far, n_seq)
+    far_two, gproj, gfc = milestone(far_two, gproj, gfc)
 
     thin = share // n_seq
     blocks = wide // width
     gfc = gfc.reshape(n_seq * n_fsdp * thin, wide // n_fsdp)
-    gout = gout.reshape(n_seq * n_fsdp * thin, width)
-    d_merged, gproj, gfc, gout, mlp = milestone(d_merged, gproj, gfc, gout, mlp)
+    together = gfc.shape[0] == gproj.shape[0]
+    walk = Walk(ring.reduce(gproj, gfc) if together else ring.reduce(gfc))
+    results = middle_back(
+        rel, counts, merged, middle, dy, gain_two, wout, two_near.terms[0] + [far_two]
+    )
+    tiers = len(tier_bounds(n_fsdp))
+    gout, (d_middle, d_merged, sums_two) = results[:tiers], results[tiers:]
+    moved, d_merged, gout = milestone(walk.moving, d_merged, gout)
+
     d_heads = lax.all_to_all(d_merged, "seq", split_axis=0, concat_axis=0, tiled=True)
-    together = gfc.shape[0] == gproj.shape[0]
-    walk = Walk(ring.reduce(gproj, gfc, gout) if together else ring.reduce(gfc, gout))
-    mlp = Scatter(mlp, "fsdp")
-    while mlp.left > 1:
-        mlp.send()
-        mlp.moving, d_heads = milestone(mlp.moving, d_heads)
-        mlp.take()
-    mlp.send()
-    moved, d_heads = milestone(walk.moving, d_heads)
-
-    d_own = ()
-    for h in range(heads):
-        walk.go(moved)
-        d_own = (
-            attention_backward(
-                row, qkv, attended, lse, d_heads.reshape(total_rows, hd), rows, h, d_own
-            ),
-        )
-        moved, d_own, mlp.moving = milestone(walk.moving, d_own, mlp.moving)
-    mlp.take()
-    d_own = d_own[0]
+    walk.go(moved)
+    gout = Scatter(gout, "fsdp")
+    hidden = (feed_near[0], feed_far[0])
+    while gout.left > 1:
+        gout.send()
+        gout.moving, hidden = milestone(gout.moving, hidden)
+        gout.take()
+    gout.send()
+    mlp_near = Scatter(feed_out(hidden[0], w_proj, rows, True), "fsdp")
+    mlp_far = Scatter(feed_out(hidden[1], w_proj, rows, False), "fsdp")
+    while mlp_near.left:
+        mlp_near.send()
+        mlp_far.send()
+        mlp_near.take()
+        mlp_far.take()
+    mlp_far = add_up(mlp_far.terms[0]).astype(BF16)
+    gout.moving, mlp_far, mlp_near.terms = milestone(gout.moving, mlp_far, mlp_near.terms)
+    gout.take()
+    out_walk = Walk(ring.reduce(add_up(gout.terms[0])))
+    moved, d_heads, out_moved = milestone(walk.moving, d_heads, out_walk.moving)
+
+    walk.go(moved)
+    out_walk.go(out_moved)
+    mlp_far = swap(mlp_far, "fsdp", top)
+    d_own = attention_backward(row, qkv, attended, lse, d_heads.reshape(total_rows, hd), rows)
+    moved, out_moved, d_own, mlp_far = milestone(walk.moving, out_walk.moving, d_own, mlp_far)
     d_packed = lax.all_to_all(
         d_own.reshape(n_seq, rows, 3 * hd), "seq", split_axis=0, concat_axis=0, tiled=True
     )
     walk.go(moved)
+    out_walk.go(out_moved)
+    w_qkv = milestone(w_qkv, d_own)[0]
+    w_all = lax.all_gather(w_qkv, "fsdp", axis=0, tiled=True)
     grad_qkv, sums_one, d_sums = qkv_grads(x_all, d_own, w_own, gain_one, shift_one, rows)
     while walk.result is None:
-        moved, grad_qkv = milestone(walk.moving, grad_qkv)
+        moved, out_moved, grad_qkv, sums_one, d_sums, mlp_far = milestone(
+            walk.moving, out_walk.moving, grad_qkv, sums_one, d_sums, mlp_far
+        )
         walk.go(moved)
+        out_walk.go(out_moved)
     mine = walk.result
     if together:
-        mine_proj, mine = mine[:, :width], mine[:, width:]
+        mine_proj, mine_fc = mine[:, :width], mine[:, width:]
     else:
+        mine_fc = mine
         walk = Walk(ring.reduce(gproj))
         while walk.result is None:
             walk.go(walk.moving)
         mine_proj = walk.result
     mine_proj = mine_proj.reshape(blocks, thin, width).transpose(1, 0, 2).reshape(thin, wide)
-    mine = cube_exchange(mine, "fsdp", 0)
+    mine_fc = cube_exchange(mine_fc, "fsdp", 0)
     parts = [
         lax.dynamic_slice_in_dim(grad_qkv, (me_fsdp ^ mask) * share, share, 0) for mask in masks
     ]
     parts = [jnp.concatenate(parts[lo:hi], axis=0) for lo, hi in tier_bounds(n_fsdp)]
     parts = Scatter(parts, "fsdp")
-    while parts.left:
+    while parts.left > 1:
         parts.send()
-        if parts.left > 1:
-            parts.moving, mine = milestone(parts.moving, mine)
         parts.take()
-    mine_fc = [m[:, : wide // n_fsdp] for m in mine]
-    mine_out = add_up([m[:, wide // n_fsdp :] for m in mine]).astype(BF16)
+    while out_walk.result is None:
+        parts.terms, mine_fc, out_moved = milestone(parts.terms, mine_fc, out_walk.moving)
+        out_walk.go(out_moved)
+    parts.send()
+    parts.take()
     share_qkv = add_up(parts.terms[0]).astype(BF16)
-    beside = share_qkv.reshape(n_seq, thin, 3 * hd).transpose(1, 0, 2).reshape(thin, -1)
-    mine = jnp.concatenate([mine_proj] + mine_fc + [mine_out, beside], axis=1)
-
-    mine, d_packed = milestone(mine, d_packed)
+    beside_it = share_qkv.reshape(n_seq, thin, 3 * hd).transpose(1, 0, 2).reshape(thin, -1)
+    mine = jnp.concatenate([mine_proj] + mine_fc + [out_walk.result, beside_it], axis=1)
+
+    mine, d_packed, mlp_far, sums_one, d_sums = milestone(
+        mine, d_packed, mlp_far, sums_one, d_sums
+    )
     walk = Walk(ring.gather(mine))
-    output, square_ends = finish(counts, middle, bproj, mlp.terms[0])
+    output, square_ends = finish(counts, middle, bproj, mlp_near.terms[0] + [mlp_far])
+    squares = jnp.concatenate([square_ends[:1], square_attn, square_ends[1:]], axis=0)
+    squares = jnp.concatenate([jnp.sum(squares, axis=1), counts[:1].astype(F32)])[None]
+    squares = jnp.concatenate([squares, jnp.zeros((n_fsdp - 1, 4), F32)], axis=0)
     grad_bfc = lax.dynamic_update_slice_in_dim(
         jnp.zeros((n_fsdp, wide // n_fsdp), F32), gbfc, me_fsdp, 0
     )
@@ -1141,70 +1257,67 @@
     grad_bqv = lax.dynamic_update_slice_in_dim(
         jnp.zeros((n_seq, 2 * hd), F32), d_sums, me_seq, 0
     )
-    squares = jnp.concatenate([square_ends[:1], square_attn, square_ends[1:]], axis=0)
-    sums = jnp.concatenate(
-        [
-            sums_two.reshape(-1),
-            grad_bfc.reshape(-1),
-            jnp.sum(squares, axis=1),
-            counts[:1].astype(F32),
-            sums_one.reshape(-1),
-            grad_bqv.reshape(-1),
-        ]
-    )
-    hops = [(axis, bit) for axis in ("fsdp", "seq") for bit in bits(lax.axis_size(axis))]
-    input_grad = None
+    vectors = [sums_one[0], sums_one[1], grad_bqv, *[sums_two[k] for k in range(4)], grad_bfc]
+    vectors = [v.reshape(n_fsdp, -1) for v in vectors]
+    sums = jnp.concatenate(vectors + [squares], axis=1)
+    for bit in bits(n_fsdp):
+        sums = sums + swap(sums, "fsdp", bit)
+    hops = bits(n_seq)
     arrived = [mine]
+
     layout = (
         ("rows", wide, blocks),
         ("rel", wide, n_fsdp),
         ("rows", width, 1),
         ("cols", 3 * width, n_seq),
     )
-    placed = None
-    for step in range(n_seq // 2):
-        count = -(-len(hops) // (n_seq // 2 - step))
-        for axis, bit in hops[:count]:
-            sums = sums + swap(sums, axis, bit)
+    steps = n_seq // 2
+    input_grad = placed = own = squares = None
+    for step in range(steps):
+        ahead = steps - step
+        count = -(-len(hops) // max(1, ahead - 1))
+        for bit in hops[:count]:
+            sums = sums + swap(sums, "seq", bit)
         hops = hops[count:]
-        if step == min(1, n_seq // 2 - 1):
+        if ahead == min(3, steps):
             input_grad = input_gradient(d_packed, w_all, x, gain_one, d_middle)
-        if step == n_seq // 2 - 1:
-            placed = place(ring.order[: n_seq - 1], rel, arrived, layout, n_seq)
-        moved, sums, output, input_grad, placed = milestone(
-            walk.moving, sums, output, input_grad, placed
+        if ahead == 1:
+            own = lax.dynamic_slice_in_dim(sums, me_fsdp, 1, 0)[0]
+            squares = sums[0, -4:]
+            placed = place(ring.order, rel, arrived, layout, n_seq)
+        moved, sums, input_grad, placed, own, squares, output = milestone(
+            walk.moving, sums, input_grad, placed, own, squares, output
         )
-        arrived += moved
+        if ahead > 1:
+            arrived += list(moved)
         walk.go(moved)
+    stats = jnp.sqrt(squares[:3] / (squares[3] * width))
+    farthest = ring.shard(n_seq // 2).reshape(1)
     last_piece = [jnp.concatenate(walk.result[-2:], axis=0)]
-    placed = place(ring.order[n_seq - 1 :], rel, last_piece, layout, n_seq, placed)
+    placed = place(farthest, rel, last_piece, layout, n_seq, placed)
     grad_proj, grad_fc, grad_out, grad_wqkv = flat_matrices(placed, layout)
 
-    def own_share(vector):
-        count = vector.shape[0] // n_fsdp
-        return lax.dynamic_slice_in_dim(vector, me_fsdp * count, count, 0)
-
-    early = sums[: 4 * width + wide + 4]
-    late = sums[4 * width + wide + 4 :]
-    sum_bout, sum_g2, sum_s2, sum_bproj = [early[k * width : (k + 1) * width] for k in range(4)]
-    sum_bfc = early[4 * width : 4 * width + wide]
-    squared = early[4 * width + wide :]
-    stats = jnp.sqrt(squared[:3] / (squared[3] * width))
+    shares = []
+    at = 0
+    for vector in vectors:
+        shares.append(own[at : at + vector.shape[1]])
+        at += vector.shape[1]
+    g1, s1, bqv, bout, g2, s2, bproj, bfc = shares
     return (
         output[None],
         input_grad[None],
-        own_share(late[:width]),
-        own_share(late[width : 2 * width]),
+        g1,
+        s1,
         grad_wqkv,
-        own_share(late[2 * width :]),
+        bqv,
         grad_out,
-        own_share(sum_bout),
-        own_share(sum_g2),
-        own_share(sum_s2),
+        bout,
+        g2,
+        s2,
         grad_fc,
-        own_share(sum_bfc),
+        bfc,
         grad_proj,
-        own_share(sum_bproj),
+        bproj,
         stats,
     )
 

time: 468 us -> 434 us (0.927)
  local copies, waits for them, and re-layouts: 63.3 us -> 43.2 us
  Pallas kernels: 147 us -> 127 us
  waiting for transfers between devices: 159 us -> 139 us
  starting transfers between devices: 60.9 us -> 80.3 us
  other arithmetic: 14.3 us -> 19 us
    all_to_all x1, waiting for transfers between devices: 18.2 us -> 1.56 us  [shards(): lax.all_to_all(d_own.reshape(n_seq, rows, 3 * hd), 'seq', split_axis=0, c...]
    unnamed x144 -> x188, local copies, waits for them, and re-layouts: 41.3 us -> 28.8 us
    ppermute x12 -> x16, waiting for transfers between devices: 31.9 us -> 42.7 us  [send_up(): return lax.ppermute(value, self.axis, self.up)]
    all_to_all x1, waiting for transfers between devices: 0.01 us -> 9.84 us  [shards(): lax.all_to_all(attended.reshape(n_seq, rows, hd), 'seq', split_axis=0, co...]
    pallas_call x4 -> x6, Pallas kernels: 73.8 us -> 64.4 us  [the longest x2 22.6 us: feed(): pl.pallas_call(functools.partial(feed_kernel, packs), grid_spec=pltpu.Pre...]
    ppermute x20 -> x24, starting transfers between devices: 12.5 us -> 21.7 us  [swap(): return lax.ppermute(value, axis, [(i, i ^ bit) for i in range(n)])]
    all_to_all x1, waiting for transfers between devices: 8.38 us -> 0.01 us  [shards(): lax.all_to_all(d_merged, 'seq', split_axis=0, concat_axis=0, tiled=True)]
    ppermute x12 -> x16, starting transfers between devices: 17 us -> 25.1 us  [send_up(): return lax.ppermute(value, self.axis, self.up)]
  transfers between devices with their start and end apart: 53 -> 65, of which waited for: 27 -> 30; matrix products, arithmetic and copies ran while one was open for 8% -> 6% of each run, Pallas kernels for 25% -> 29%
where the time goes in v3:
time: 434 us; the launch traced here: 425 us
  waiting for transfers between devices  139 us (32%)
  Pallas kernels  127 us (29%)
  starting transfers between devices  80.3 us (19%)
  local copies, waits for them, and re-layouts  43.2 us (10%)
  other arithmetic  19 us (4%)
  between operations  16.5 us (4%)
    ppermute x24, waiting for transfers between devices, swap(): return lax.ppermute(value, axis, [(i, i ^ bit) for i in range(n)])  75.5 us
    ppermute x16, waiting for transfers between devices, send_up(): return lax.ppermute(value, self.axis, self.up)  42.7 us
    unnamed x188, local copies, waits for them, and re-layouts  28.8 us
    ppermute x16, starting transfers between devices, send_up(): return lax.ppermute(value, self.axis, self.up)  25.1 us
    pallas_call x2, Pallas kernels, feed(): pl.pallas_call(functools.partial(feed_kernel, packs), grid_spec=pltpu.Pre...  22.6 us
    ppermute x24, starting transfers between devices, swap(): return lax.ppermute(value, axis, [(i, i ^ bit) for i in range(n)])  21.7 us
    pallas_call x1, Pallas kernels, attention_backward(): pl.pallas_call(functools.partial(backward_kernel, heads, block, row.shape...  20.9 us
    ppermute x16, starting transfers between devices, send_down(): return lax.ppermute(value, self.axis, self.down)  18.8 us
  transfers between devices with their start and end apart: 65, of which 30 were waited for; matrix products, arithmetic and copies ran while one was open for 6% of the time, Pallas kernels for 29%

profile of v3, /device:TPU:0, one launch (start us, length us, event | category | flops | bytes accessed | tf_op | source)
XLA Modules:
  0.0 425.2 jit_solution(11611107606491233466)
XLA Ops:
  13.7 15.1 %collective-permute-done.x_ref = bf16[384,1024]{1,0:T(8,128)(2,1)S(1)} collective-permute-done((bf16[384,1024]{1,0:T(8,128)(2,1)}, bf16[384,1024]{1,0:T(8,128)(2,1)S(1)}, u32[]{:S(2)}, u32[]{:S(2)}) %collective-permute-start) | collective-permute-done | bytes 786464 | tf_op jit(solution)/shard_map/ppermute | solution.py:892
  34.2 9.6 %collective-permute-done.4 = bf16[272,384]{1,0:T(8,128)(2,1)S(1)} collective-permute-done((bf16[272,384]{1,0:T(8,128)(2,1)S(1)}, bf16[272,384]{1,0:T(8,128)(2,1)S(1)}, u32[]{:S(2)}, u32[]{:S(2)}) %collective-permute-start.4) | collective-permute-done | bytes 208928 | tf_op jit(solution)/shard_map/ppermute | solution.py:958
  66.0 12.0 %collective-permute-done.9 = bf16[256,1024]{1,0:T(8,128)(2,1)} collective-permute-done((bf16[256,1024]{1,0:T(8,128)(2,1)}, bf16[256,1024]{1,0:T(8,128)(2,1)}, u32[]{:S(2)}, u32[]{:S(2)}) %collective-permute-start.9) | collective-permute-done | bytes 524320 | tf_op jit(solution)/shard_map/ppermute | solution.py:958
  82.3 3.6 collective-permute-done.10.x_ref
  89.0 14.7 %attention_forward.1 = (bf16[3072,128]{1,0:T(8,128)(2,1)}, f32[2,3072]{1,0:T(2,128)S(1)}) custom-call(s32[4]{0:T(128)S(1)} %select_reduce_fusion.len_ref, bf16[3072,384]{1,0:T(8,128)(2,1)S(1)} %get-tuple-element.218.qkv_ref), custom_call_target="tpu_custom_call" | custom-call | flops 46200000512 | bytes 1048576 | tf_op jit(solution)/shard_map/attention_forward/pallas_call | solution.py:228
  103.7 4.0 all-to-all-start
  111.0 9.8 %all-to-all-done.merged_ref = bf16[8,384,128]{2,1,0:T(8,128)(2,1)S(1)} async-done(((bf16[8,384,128]{2,1,0:T(8,128)(2,1)}), bf16[8,384,128]{2,1,0:T(8,128)(2,1)S(1)}, u32[]{:S(2)}, u32[]{:S(2)}) %all-to-all-start) | async-done | bytes 786464 | tf_op jit(solution)/shard_map/all_to_all | solution.py:1119
  129.8 11.6 %feed.2 = (f32[384,1024]{1,0:T(8,128)}, bf16[384,1024]{1,0:T(8,128)(2,1)}, bf16[768,1024]{1,0:T(8,128)(2,1)}, bf16[768,1024]{1,0:T(8,128)(2,1)}, bf16[768,1024]{1,0:T(8,128)(2,1)}) custom-call(s32[4]{0:T(128)S(1)} %broadcast_xor_fusion.1.rel_ref, s32[2]{0:T(128)S(1)} %get-tuple-element.415.which_ref, s32[2]{0:T(128)S(1)} %subtract_clamp_fusion.count_ref, ...), custom_call_target="tpu_custom_call" | custom-call | flops 32999999488 | bytes 1048576 | tf_op jit(solution)/shard_map/feed/pallas_call | solution.py:414
  141.3 5.4 %collective-permute-done.14.rest_0_.rest_2_ = bf16[384,1024]{1,0:T(8,128)(2,1)} collective-permute-done((bf16[384,1024]{1,0:T(8,128)(2,1)}, bf16[384,1024]{1,0:T(8,128)(2,1)}, u32[]{:S(2)}, u32[]{:S(2)}) %collective-permute-start.14) | collective-permute-done | bytes 786464 | tf_op jit(solution)/shard_map/ppermute | solution.py:958
  150.4 11.0 %feed.3 = (bf16[384,1024]{1,0:T(8,128)(2,1)S(1)}, bf16[384,1024]{1,0:T(8,128)(2,1)}, bf16[768,1024]{1,0:T(8,128)(2,1)}, bf16[768,1024]{1,0:T(8,128)(2,1)}, bf16[768,1024]{1,0:T(8,128)(2,1)}) custom-call(s32[4]{0:T(128)S(1)} %broadcast_xor_fusion.1.rel_ref, s32[2]{0:T(128)S(1)} %get-tuple-element.416.which_ref, s32[2]{0:T(128)S(1)} %subtract_clamp_fusion.1.count_ref, ...), custom_call_target="tpu_custom_call" | custom-call | flops 32999999488 | bytes 1048576 | tf_op jit(solution)/shard_map/feed/pallas_call | solution.py:414
  169.3 16.6 %feed_grads.1 = (bf16[1024,1024]{1,0:T(8,128)(2,1)}, bf16[8,4,32,1024]{3,2,1,0:T(8,128)(2,1)}, f32[1,1024]{1,0:T(1,128)S(1)}) custom-call(bf16[768,1024]{1,0:T(8,128)(2,1)S(1)} %copy-done.5, bf16[768,1024]{1,0:T(8,128)(2,1)} %get-tuple-element.261.hid_b.hidden_ref, bf16[768,1024]{1,0:T(8,128)(2,1)} %get-tuple-element.238.di_a, ...), custom_call_target="tpu_custom_call" | custom-call | flops 49500000256 | bytes 1048576 | tf_op jit(solution)/shard_map/feed_grads/pallas_call | solution.py:540
  193.5 5.8 %middle_back.1 = (bf16[256,1024]{1,0:T(8,128)(2,1)S(1)}, bf16[256,1024]{1,0:T(8,128)(2,1)S(1)}, bf16[512,1024]{1,0:T(8,128)(2,1)}, f32[384,1024]{1,0:T(8,128)S(1...) custom-call(s32[4]{0:T(128)S(1)} %broadcast_xor_fusion.1.rel_ref, s32[2]{0:T(128)S(1)} %subtract_clamp_fusion.count_ref, ...), custom_call_target="tpu_custom_call" | custom-call | flops 23100000256 | bytes 1048576 | tf_op jit(solution)/shard_map/middle_back/pallas_call | solution.py:643
  222.9 8.8 %collective-permute-done.25 = bf16[256,1024]{1,0:T(8,128)(2,1)S(1)} collective-permute-done((bf16[256,1024]{1,0:T(8,128)(2,1)S(1)}, bf16[256,1024]{1,0:T(8,128)(2,1)S(1)}, u32[]{:S(2)}, u32[]{:S(2)}) %collective-permute-start.25) | collective-permute-done | bytes 524320 | tf_op jit(solution)/shard_map/ppermute | solution.py:958
  245.9 20.9 %attention_backward.1.d_ref = bf16[3072,384]{1,0:T(8,128)(2,1)S(1)} custom-call(s32[4]{0:T(128)S(1)} %copy-done.19, bf16[3072,384]{1,0:T(8,128)(2,1)S(1)} %copy-done.39, bf16[3072,128]{1,0:T(8,128)(2,1)} %get-tuple-element.219.o_ref, f32[2,3072]{1,0:T(2,128)S(1)} %get-tuple-element.272.lse_ref, bf16[3072,128]{1,0:T(8,128)(2,1)S(1)} %bitcast.93), custom_call_target="tpu_custom_call" | custom-call | flops 69300002816 | bytes 1048576 | tf_op jit(solution)/shard_map/attention_backward/pallas_call | solution.py:247
  273.6 4.7 %all-to-all-start.2 = ((bf16[8,384,384]{2,1,0:T(8,128)(2,1)}), bf16[8,384,384]{2,1,0:T(8,128)(2,1)S(1)}, u32[]{:S(2)}, u32[]{:S(2)}) async-start(bf16[8,384,384]{2,1,0:T(8,128)(2,1)} %bitcast.91), calls=%async_computation.2 | async-start | bytes 4718592 | tf_op jit(solution)/shard_map/all_to_all | solution.py:1202
  283.5 12.2 %qkv_grads.1 = (bf16[1024,384]{1,0:T(8,128)(2,1)S(1)}, f32[2,1024]{1,0:T(2,128)S(1)}, f32[1,384]{1,0:T(1,128)S(1)}) custom-call(bf16[3072,1024]{1,0:T(8,128)(2,1)S(1)} %copy-done.37, bf16[3072,384]{1,0:T(8,128)(2,1)S(1)} %copy-done.4, bf16[1024,384]{1,0:T(8,128)(2,1)S(1)} %copy-done.2, f32[1,1024]{1,0:T(1,128)S(1)} %bitcast.105, f32[1,1024]{1,0:T(1,128)S(1)} %bitcast.116), custom_call_target="tpu_custom_call" | custom-call | flops 42900000768 | bytes 1048576 | tf_op jit(solution)/shard_map/qkv_grads/pallas_call | solution.py:727
  305.8 16.0 %collective-permute-done.43 = bf16[32,1024]{1,0:T(8,128)(2,1)S(1)} collective-permute-done((bf16[32,1024]{1,0:T(8,128)(2,1)S(1)}, bf16[32,1024]{1,0:T(8,128)(2,1)S(1)}, u32[]{:S(2)}, u32[]{:S(2)}) %collective-permute-start.43) | collective-permute-done | bytes 65568 | tf_op jit(solution)/shard_map/ppermute | solution.py:892
  323.8 8.5 %collective-permute-done.45 = bf16[256,384]{1,0:T(8,128)(2,1)S(1)} collective-permute-done((bf16[256,384]{1,0:T(8,128)(2,1)S(1)}, bf16[256,384]{1,0:T(8,128)(2,1)S(1)}, u32[]{:S(2)}, u32[]{:S(2)}) %collective-permute-start.45) | collective-permute-done | bytes 196640 | tf_op jit(solution)/shard_map/ppermute | solution.py:958
  334.0 7.5 %collective-permute-start.46 = (bf16[32,12288]{1,0:T(8,128)(2,1)S(1)}, bf16[32,12288]{1,0:T(8,128)(2,1)}, u32[]{:S(2)}, u32[]{:S(2)}) collective-permute-start(bf16[32,12288]{1,0:T(8,128)(2,1)S(1)} %constant_dynamic-update-slice_fusion.2.refs_0_), channel_id=1, source_target_pairs={{0,8},{8,16},{16,24},{24,28},{28,20},{20,12},{12,4},{4,0},{1,9},{9... | collective-permute-start | bytes 2359304 | tf_op jit(solution)/shard_map/ppermute | solution.py:892
  354.8 3.6 collective-permute-start.50
  370.6 5.5 %input_gradient.1 = f32[384,1024]{1,0:T(8,128)} custom-call(bf16[8,384,384]{2,1,0:T(8,128)(2,1)S(1)} %all-to-all-done.2.d_ref, bf16[384,1024]{1,0:T(8,128)(2,1)S(1)} %bitcast.126, f32[1,1024]{1,0:T(1,128)S(1)} %bitcast.106, f32[384,1024]{1,0:T(8,128)S(1)} %copy-done.44, bf16[1024,3072]{1,0:T(8,128)(2,1)S(1)} %copy-done.20), custom_call_target="tpu_custom_call" | custom-call | flops 26400000000 | bytes 1048576 | tf_op jit(solution)/shard_map/input_gradient/pallas_call | solution.py:779
  376.1 4.5 %collective-permute-done.51.refs_3_ = bf16[32,12288]{1,0:T(8,128)(2,1)} collective-permute-done((bf16[32,12288]{1,0:T(8,128)(2,1)}, bf16[32,12288]{1,0:T(8,128)(2,1)}, u32[]{:S(2)}, u32[]{:S(2)}) %collective-permute-start.51) | collective-permute-done | bytes 786464 | tf_op jit(solution)/shard_map/ppermute | solution.py:892
  384.8 17.2 %collective-permute-done.56 = f32[4,3076]{1,0:T(4,128)S(1)} collective-permute-done((f32[4,3076]{1,0:T(4,128)S(1)}, f32[4,3076]{1,0:T(4,128)S(1)}, u32[]{:S(2)}, u32[]{:S(2)}) %collective-permute-start.56) | collective-permute-done | bytes 49248 | tf_op jit(solution)/shard_map/ppermute | solution.py:958
  405.5 7.4 %place.2 = (f32[8,128,1024]{2,1,0:T(8,128)}, f32[8,32,4096]{2,1,0:T(8,128)}, f32[8,32,1024]{2,1,0:T(8,128)}, f32[256,3072]{1,0:T(8,128)}) custom-call(s32[8]{0:T(128)S(1)} %compare_select_fusion.2.order_ref, s32[4]{0:T(128)S(1)} %broadcast_xor_fusion.1.rel_ref, bf16[32,12288]{1,0:T(8,128)(2,1)S(1)} %constant_dynamic-update-slice_fusion.2.refs_0_, ...), custom_call_target="tpu_custom_call" | custom-call | flops 23100000256 | bytes 1048576 | tf_op jit(solution)/shard_map/place/pallas_call | solution.py:839
  (441 shorter events, 172.7 us)
Async XLA Ops:
  7.3 120.9 %all-gather.9.cloned.1.call-start = ((), (), s32[]{:S(2)}) async-start(), calls=%async_computation.5 | async-start | bytes 3932160 | tf_op jit(solution)/shard_map/all_gather | solution.py:1059
  8.0 120.9 %all-gather.5.cloned.1.call-start = ((), (), s32[]{:S(2)}) async-start(), calls=%async_computation.3 | async-start | bytes 10485760 | tf_op jit(solution)/shard_map/all_gather | solution.py:1058
  8.1 20.8 %collective-permute-start = (bf16[384,1024]{1,0:T(8,128)(2,1)}, bf16[384,1024]{1,0:T(8,128)(2,1)S(1)}, u32[]{:S(2)}, u32[]{:S(2)}) collective-permute-start(bf16[384,1024]{1,0:T(8,128)(2,1)} %bitcast.122), channel_id=1, source_target_pairs={{0,8},{8,16},{16,24},{24,28},{28,20},{20,12},{12,4},{4,0},{1,9},{9... | collective-permute-start | bytes 2359304 | tf_op jit(solution)/shard_map/ppermute | solution.py:892
  55.1 22.9 %collective-permute-start.9 = (bf16[256,1024]{1,0:T(8,128)(2,1)}, bf16[256,1024]{1,0:T(8,128)(2,1)}, u32[]{:S(2)}, u32[]{:S(2)}) collective-permute-start(bf16[256,1024]{1,0:T(8,128)(2,1)} %param.27), channel_id=1, source_target_pairs={{0,2},{1,3},{2,0},{3,1},{4,6},{5,7},{6,4},{7,5},{8,10},{9,11},{10,... | collective-permute-start | bytes 1572872 | tf_op jit(solution)/shard_map/ppermute | solution.py:958
  56.7 21.3 %collective-permute-start.7 = (bf16[384,1024]{1,0:T(8,128)(2,1)}, bf16[384,1024]{1,0:T(8,128)(2,1)S(1)}, u32[]{:S(2)}, u32[]{:S(2)}) collective-permute-start(bf16[384,1024]{1,0:T(8,128)(2,1)} %collective-permute-done.2.x_ref), channel_id=1, source_target_pairs={{0,8},{8,16},{16,24},{24,28},{28,20},{20,12},{12,4},{4,0},{1,9},{9... | collective-permute-start | bytes 2359304 | tf_op jit(solution)/shard_map/ppermute | solution.py:892
  126.4 20.3 %collective-permute-start.14 = (bf16[384,1024]{1,0:T(8,128)(2,1)}, bf16[384,1024]{1,0:T(8,128)(2,1)}, u32[]{:S(2)}, u32[]{:S(2)}) collective-permute-start(bf16[384,1024]{1,0:T(8,128)(2,1)} %get-tuple-element.223.rest_0_), channel_id=1, source_target_pairs={{0,2},{1,3},{2,0},{3,1},{4,6},{5,7},{6,4},{7,5},{8,10},{9,11},{10,... | collective-permute-start | bytes 2359304 | tf_op jit(solution)/shard_map/ppermute | solution.py:958
  204.7 32.4 %collective-permute-start.23 = (bf16[128,2048]{1,0:T(8,128)(2,1)}, bf16[128,2048]{1,0:T(8,128)(2,1)}, u32[]{:S(2)}, u32[]{:S(2)}) collective-permute-start(bf16[128,2048]{1,0:T(8,128)(2,1)} %pad_maximum_fusion.1), channel_id=1, source_target_pairs={{8,0},{16,8},{24,16},{28,24},{20,28},{12,20},{4,12},{0,4},{9,1},{1... | collective-permute-start | bytes 1572872 | tf_op jit(solution)/shard_map/ppermute | solution.py:895
  206.0 31.1 %all-to-all-start.1 = ((bf16[8,384,128]{2,1,0:T(8,128)(2,1)}), bf16[8,384,128]{2,1,0:T(8,128)(2,1)S(1)}, u32[]{:S(2)}, u32[]{:S(2)}) async-start(bf16[8,384,128]{2,1,0:T(8,128)(2,1)} %copy-done.11), calls=%async_computation.1 | async-start | bytes 1572864 | tf_op jit(solution)/shard_map/all_to_all | solution.py:1175
  235.5 31.4 %collective-permute-start.34 = (bf16[384,1024]{1,0:T(8,128)(2,1)}, bf16[384,1024]{1,0:T(8,128)(2,1)S(1)}, u32[]{:S(2)}, u32[]{:S(2)}) collective-permute-start(bf16[384,1024]{1,0:T(8,128)(2,1)} %add_convert_fusion), channel_id=1, source_target_pairs={{0,2},{1,3},{2,0},{3,1},{4,6},{5,7},{6,4},{7,5},{8,10},{9,11},{10,... | collective-permute-start | bytes 2359304 | tf_op jit(solution)/shard_map/ppermute | solution.py:958
  239.2 27.7 %collective-permute-start.33 = (bf16[32,1024]{1,0:T(8,128)(2,1)S(1)}, bf16[32,1024]{1,0:T(8,128)(2,1)S(1)}, u32[]{:S(2)}, u32[]{:S(2)}) collective-permute-start(bf16[32,1024]{1,0:T(8,128)(2,1)S(1)} %pad_maximum_fusion.7), channel_id=1, source_target_pairs={{8,0},{16,8},{24,16},{28,24},{20,28},{12,20},{4,12},{0,4},{9,1},{1... | collective-permute-start | bytes 196616 | tf_op jit(solution)/shard_map/ppermute | solution.py:895
  239.8 27.1 %collective-permute-start.32 = (bf16[32,1024]{1,0:T(8,128)(2,1)S(1)}, bf16[32,1024]{1,0:T(8,128)(2,1)S(1)}, u32[]{:S(2)}, u32[]{:S(2)}) collective-permute-start(bf16[32,1024]{1,0:T(8,128)(2,1)S(1)} %pad_maximum_fusion.6), channel_id=1, source_target_pairs={{0,8},{8,16},{16,24},{24,28},{28,20},{20,12},{12,4},{4,0},{1,9},{9... | collective-permute-start | bytes 196616 | tf_op jit(solution)/shard_map/ppermute | solution.py:892
  242.6 24.3 %collective-permute-start.31 = (bf16[128,2048]{1,0:T(8,128)(2,1)S(1)}, bf16[128,2048]{1,0:T(8,128)(2,1)S(1)}, u32[]{:S(2)}, u32[]{:S(2)}) collective-permute-start(bf16[128,2048]{1,0:T(8,128)(2,1)S(1)} %add_convert_fusion.5), channel_id=1, source_target_pairs={{8,0},{16,8},{24,16},{28,24},{20,28},{12,20},{4,12},{0,4},{9,1},{1... | collective-permute-start | bytes 1572872 | tf_op jit(solution)/shard_map/ppermute | solution.py:895
  245.7 21.3 %collective-permute-start.30 = (bf16[128,2048]{1,0:T(8,128)(2,1)S(1)}, bf16[128,2048]{1,0:T(8,128)(2,1)S(1)}, u32[]{:S(2)}, u32[]{:S(2)}) collective-permute-start(bf16[128,2048]{1,0:T(8,128)(2,1)S(1)} %add_convert_fusion.6), channel_id=1, source_target_pairs={{0,8},{8,16},{16,24},{24,28},{28,20},{20,12},{12,4},{4,0},{1,9},{9... | collective-permute-start | bytes 1572872 | tf_op jit(solution)/shard_map/ppermute | solution.py:892
  267.6 28.1 %collective-permute-start.37 = (bf16[32,1024]{1,0:T(8,128)(2,1)}, bf16[32,1024]{1,0:T(8,128)(2,1)S(1)}, u32[]{:S(2)}, u32[]{:S(2)}) collective-permute-start(bf16[32,1024]{1,0:T(8,128)(2,1)} %get-tuple-element.378), channel_id=1, source_target_pairs={{0,8},{8,16},{16,24},{24,28},{28,20},{20,12},{12,4},{4,0},{1,9},{9... | collective-permute-start | bytes 196616 | tf_op jit(solution)/shard_map/ppermute | solution.py:892
  269.1 26.6 %collective-permute-start.38 = (bf16[32,1024]{1,0:T(8,128)(2,1)}, bf16[32,1024]{1,0:T(8,128)(2,1)}, u32[]{:S(2)}, u32[]{:S(2)}) collective-permute-start(bf16[32,1024]{1,0:T(8,128)(2,1)} %get-tuple-element.377), channel_id=1, source_target_pairs={{8,0},{16,8},{24,16},{28,24},{20,28},{12,20},{4,12},{0,4},{9,1},{1... | collective-permute-start | bytes 196616 | tf_op jit(solution)/shard_map/ppermute | solution.py:895
  270.6 26.2 %collective-permute-start.36 = (bf16[128,2048]{1,0:T(8,128)(2,1)}, bf16[128,2048]{1,0:T(8,128)(2,1)}, u32[]{:S(2)}, u32[]{:S(2)}) collective-permute-start(bf16[128,2048]{1,0:T(8,128)(2,1)} %add_convert_fusion.3), channel_id=1, source_target_pairs={{8,0},{16,8},{24,16},{28,24},{20,28},{12,20},{4,12},{0,4},{9,1},{1... | collective-permute-start | bytes 1572872 | tf_op jit(solution)/shard_map/ppermute | solution.py:895
  273.4 23.4 %collective-permute-start.35 = (bf16[128,2048]{1,0:T(8,128)(2,1)}, bf16[128,2048]{1,0:T(8,128)(2,1)}, u32[]{:S(2)}, u32[]{:S(2)}) collective-permute-start(bf16[128,2048]{1,0:T(8,128)(2,1)} %add_convert_fusion.4), channel_id=1, source_target_pairs={{0,8},{8,16},{16,24},{24,28},{28,20},{20,12},{12,4},{4,0},{1,9},{9... | collective-permute-start | bytes 1572872 | tf_op jit(solution)/shard_map/ppermute | solution.py:892
  273.6 60.4 %all-to-all-start.2 = ((bf16[8,384,384]{2,1,0:T(8,128)(2,1)}), bf16[8,384,384]{2,1,0:T(8,128)(2,1)S(1)}, u32[]{:S(2)}, u32[]{:S(2)}) async-start(bf16[8,384,384]{2,1,0:T(8,128)(2,1)} %bitcast.91), calls=%async_computation.2 | async-start | bytes 4718592 | tf_op jit(solution)/shard_map/all_to_all | solution.py:1202
  278.3 87.0 %all-gather.7.cloned.1.call-start = ((), (), s32[]{:S(2)}) async-start(), calls=%async_computation.4 | async-start | bytes 7864320 | tf_op jit(solution)/shard_map/all_gather | solution.py:1208
  297.8 23.9 %collective-permute-start.43 = (bf16[32,1024]{1,0:T(8,128)(2,1)S(1)}, bf16[32,1024]{1,0:T(8,128)(2,1)S(1)}, u32[]{:S(2)}, u32[]{:S(2)}) collective-permute-start(bf16[32,1024]{1,0:T(8,128)(2,1)S(1)} %get-tuple-element.376), channel_id=1, source_target_pairs={{0,8},{8,16},{16,24},{24,28},{28,20},{20,12},{12,4},{4,0},{1,9},{9... | collective-permute-start | bytes 196616 | tf_op jit(solution)/shard_map/ppermute | solution.py:892
  298.9 22.8 %collective-permute-start.44 = (bf16[32,1024]{1,0:T(8,128)(2,1)S(1)}, bf16[32,1024]{1,0:T(8,128)(2,1)S(1)}, u32[]{:S(2)}, u32[]{:S(2)}) collective-permute-start(bf16[32,1024]{1,0:T(8,128)(2,1)S(1)} %get-tuple-element.375), channel_id=1, source_target_pairs={{8,0},{16,8},{24,16},{28,24},{20,28},{12,20},{4,12},{0,4},{9,1},{1... | collective-permute-start | bytes 196616 | tf_op jit(solution)/shard_map/ppermute | solution.py:895
  334.0 26.5 %collective-permute-start.46 = (bf16[32,12288]{1,0:T(8,128)(2,1)S(1)}, bf16[32,12288]{1,0:T(8,128)(2,1)}, u32[]{:S(2)}, u32[]{:S(2)}) collective-permute-start(bf16[32,12288]{1,0:T(8,128)(2,1)S(1)} %constant_dynamic-update-slice_fusion.2.refs_0_), channel_id=1, source_target_pairs={{0,8},{8,16},{16,24},{24,28},{28,20},{20,12},{12,4},{4,0},{1,9},{9... | collective-permute-start | bytes 2359304 | tf_op jit(solution)/shard_map/ppermute | solution.py:892
  381.2 20.7 %collective-permute-start.54 = (bf16[32,12288]{1,0:T(8,128)(2,1)}, bf16[32,12288]{1,0:T(8,128)(2,1)S(1)}, u32[]{:S(2)}, u32[]{:S(2)}) collective-permute-start(bf16[32,12288]{1,0:T(8,128)(2,1)} %collective-permute-done.51.refs_3_), channel_id=1, source_target_pairs={{0,8},{8,16},{16,24},{24,28},{28,20},{20,12},{12,4},{4,0},{1,9},{9... | collective-permute-start | bytes 2359304 | tf_op jit(solution)/shard_map/ppermute | solution.py:892
  381.8 20.2 %collective-permute-start.55 = (bf16[32,12288]{1,0:T(8,128)(2,1)}, bf16[32,12288]{1,0:T(8,128)(2,1)S(1)}, u32[]{:S(2)}, u32[]{:S(2)}) collective-permute-start(bf16[32,12288]{1,0:T(8,128)(2,1)} %collective-permute-done.52.refs_4_), channel_id=1, source_target_pairs={{8,0},{16,8},{24,16},{28,24},{20,28},{12,20},{4,12},{0,4},{9,1},{1... | collective-permute-start | bytes 2359304 | tf_op jit(solution)/shard_map/ppermute | solution.py:895
  (118 other events, 1071.7 us)
Sparse Core Ops, SparseCore 0:
  9.7 35.7 all-gather.8
  47.0 66.3 all-gather.4
  280.7 54.1 all-gather.6
